TPU v7x, 32 devices: a whole 2x2x4 slice. The times are simulated.
32 devices in a mesh: dirs: 2 (over y), taps: 4 (over z), tm: 2 (over x), floors: 2 (over core).
Axes of the slice: x: 2, y: 2, z: 4, core: 2. Of those that a mesh axis runs over, the one named last changes fastest.
Arguments:
- pressures: bfloat16 [4096, 16384], P(('dirs', 'tm'), ('taps', 'floors')), parts along dimension 0, may hold values from -6 to 6
- tap_area: bfloat16 [16384], P(('taps', 'floors')), may hold values from 0.29882812 to 3
- tap_panel: int32 [16384], P(('taps', 'floors')), may hold values from 0 to 255
- tap_floor: int32 [16384], P(('taps', 'floors')), may hold values from 0 to 15
- panel_shape: bfloat16 [256, 512], replicated, may hold values from -0.046875 to 0.046875
- floor_shape: bfloat16 [16, 512], replicated, may hold values from -0.25 to 0.25
- mode_order: int32 [512], replicated, may hold values from 0 to 511, each once
- mode_decay: float32 [512], replicated, may hold values from 4.8828125e-05 to 0.08
- mode_freq: float32 [512], replicated, may hold values from 0.02 to 1.2
Outputs:
- modal_response: float32 [512, 4096], P(('taps', 'floors'), ('dirs', 'tm')), parts along dimension 1
- floor_motion: float32 [16, 4096], P(('taps', 'floors'), ('dirs', 'tm')), parts along dimension 1
- floor_load: float32 [16, 4096], P(('taps', 'floors'), ('dirs', 'tm')), parts along dimension 1
There are 2 independent parts, one for each index of `dirs`. A program takes and returns all parts, laid end to end along the dimension named above; an argument that names none is the same for every part. Nothing has to cross between parts.
All inputs are finite; a program needn't handle non-finite values.
Results may differ from a plain program's by a relative error of at most 0.0029.
Values sent between devices are 32-bit elements; how exact they have to be, the bound alone decides.
No kernel may reach another device: no remote copies, remote signals or barrier semaphores. Data moves between devices by JAX's collectives and lax.ppermute only.
A program may use at most 64 MiB of HBM per device.

v0:
```python
import jax
import jax.numpy as jnp
from jax import lax
from jax.sharding import PartitionSpec as P

BLK = 256


def on_device(
    pressures,
    tap_area,
    tap_panel,
    tap_floor,
    panel_shape,
    floor_shape,
    mode_order,
    mode_decay,
    mode_freq,
):
    highest = lax.Precision.HIGHEST
    modes = mode_order.shape[0]
    owners = lax.axis_size(("taps", "floors"))
    mode_dev = modes // owners
    time_dev = pressures.shape[0]
    tap_dev = pressures.shape[1]
    floor_count = floor_shape.shape[0]
    block_count = time_dev // BLK
    owner = lax.axis_index(("taps", "floors"))
    load_scale = (floor_count / (tap_dev * owners)) ** 0.5
    floor_ids = jnp.arange(floor_count, dtype=jnp.int32)
    weights = jnp.where(
        tap_floor[None, :] == floor_ids[:, None], tap_area[None, :], jnp.zeros((), jnp.bfloat16)
    )
    load_part = lax.dot_general(
        weights, pressures, (((1,), (1,)), ((), ())), preferred_element_type=jnp.float32
    )
    floor_load = lax.psum_scatter(load_part, ("taps", "floors"), scatter_dimension=0, tiled=True)
    ordered = jnp.take(panel_shape, mode_order, axis=1)
    tributary = (
        jnp.take(ordered, tap_panel, axis=0).astype(jnp.float32)
        * tap_area.astype(jnp.float32)[:, None]
    ).astype(jnp.bfloat16)
    forces = lax.psum_scatter(
        lax.dot_general(
            tributary, pressures, (((0,), (1,)), ((), ())), preferred_element_type=jnp.float32
        ),
        ("taps", "floors"),
        scatter_dimension=0,
        tiled=True,
    )
    local_order = lax.dynamic_slice_in_dim(mode_order, owner * mode_dev, mode_dev)
    decays = jnp.take(mode_decay, local_order)
    angles = jnp.take(mode_freq, local_order)
    input_gain = jnp.sqrt(-jnp.expm1(-2.0 * decays))
    steps_in = jnp.arange(BLK, dtype=jnp.float32)
    differ = steps_in[:, None] - steps_in[None, :]
    causal = differ >= 0.0
    distance = jnp.maximum(differ, 0.0)
    toeplitz = jnp.where(
        causal[None],
        input_gain[:, None, None]
        * jnp.exp(-decays[:, None, None] * distance)
        * jnp.cos(angles[:, None, None] * distance),
        0.0,
    )
    force_blocks = forces.reshape(mode_dev, block_count, BLK)
    zero_resp = jnp.einsum("mij,mbj->mbi", toeplitz, force_blocks, precision=highest)
    to_end = BLK - 1.0 - steps_in
    end_scale = input_gain[:, None] * jnp.exp(-decays[:, None] * to_end)
    end_re = end_scale * jnp.cos(angles[:, None] * to_end)
    end_im = end_scale * jnp.sin(angles[:, None] * to_end)
    ends_re = jnp.einsum("mj,mbj->mb", end_re, force_blocks, precision=highest)
    ends_im = jnp.einsum("mj,mbj->mb", end_im, force_blocks, precision=highest)
    count = float(BLK)
    scale = jnp.exp(-decays * count)
    blk_re = scale * jnp.cos(angles * count)
    blk_im = scale * jnp.sin(angles * count)

    def advance(carried, inputs):
        state_re, state_im = carried
        push_re, push_im = inputs
        next_re = blk_re * state_re - blk_im * state_im + push_re
        next_im = blk_im * state_re + blk_re * state_im + push_im
        return ((next_re, next_im), carried)

    zeros_state = jnp.zeros((mode_dev,), jnp.float32)
    (group_re, group_im), (enter_re, enter_im) = lax.scan(
        advance, (zeros_state, zeros_state), (ends_re.T, ends_im.T)
    )
    gathered_re, gathered_im = (
        lax.all_gather(group_re[None], "tm", axis=0, tiled=True),
        lax.all_gather(group_im[None], "tm", axis=0, tiled=True),
    )
    position = lax.axis_index("tm")
    sources = jnp.arange(gathered_re.shape[0], dtype=jnp.int32)
    distance_tm = position - 1 - sources
    earlier_mask = (distance_tm >= 0)[:, None]
    lengths = (jnp.maximum(distance_tm, 0).astype(jnp.float32) * time_dev)[:, None]
    decay_pw = jnp.exp(-decays[None, :] * lengths)
    pw_re = decay_pw * jnp.cos(angles[None, :] * lengths)
    pw_im = decay_pw * jnp.sin(angles[None, :] * lengths)
    in_re = jnp.sum(jnp.where(earlier_mask, pw_re * gathered_re - pw_im * gathered_im, 0.0), axis=0)
    in_im = jnp.sum(jnp.where(earlier_mask, pw_im * gathered_re + pw_re * gathered_im, 0.0), axis=0)
    block_start = (jnp.arange(block_count, dtype=jnp.float32) * BLK)[:, None]
    start_scale = jnp.exp(-decays[None, :] * block_start)
    pb_re = start_scale * jnp.cos(angles[None, :] * block_start)
    pb_im = start_scale * jnp.sin(angles[None, :] * block_start)
    yb_re = pb_re * in_re[None, :] - pb_im * in_im[None, :] + enter_re
    yb_im = pb_im * in_re[None, :] + pb_re * in_im[None, :] + enter_im
    ahead = steps_in + 1.0
    ahead_scale = jnp.exp(-decays[:, None] * ahead)
    fr_re = ahead_scale * jnp.cos(angles[:, None] * ahead)
    fr_im = ahead_scale * jnp.sin(angles[:, None] * ahead)
    free_part = fr_re[:, None, :] * yb_re.T[:, :, None] - fr_im[:, None, :] * yb_im.T[:, :, None]
    motion = (zero_resp + free_part).reshape(mode_dev, time_dev)
    local_shape = jnp.take(floor_shape, local_order, axis=1).astype(jnp.float32)
    motion_part = jnp.dot(
        local_shape, motion, precision=highest, preferred_element_type=jnp.float32
    )
    floor_motion = lax.psum_scatter(
        motion_part, ("taps", "floors"), scatter_dimension=0, tiled=True
    )
    return (motion, floor_motion, floor_load * load_scale)


def solution(mesh):
    in_specs = (
        P(("dirs", "tm"), ("taps", "floors")),
        P(("taps", "floors")),
        P(("taps", "floors")),
        P(("taps", "floors")),
        P(),
        P(),
        P(),
        P(),
        P(),
    )
    out_specs = (
        P(("taps", "floors"), ("dirs", "tm")),
        P(("taps", "floors"), ("dirs", "tm")),
        P(("taps", "floors"), ("dirs", "tm")),
    )
    return jax.shard_map(
        on_device, mesh=mesh, in_specs=in_specs, out_specs=out_specs, check_vma=False
    )
```

profile of v0, /device:TPU:0, one launch (start us, length us, event | category | flops | bytes accessed | tf_op | source)
XLA Modules:
  0.0 209.6 jit_solution(1603378108236540857)
XLA Ops:
  7.2 0.0 reduce-scatter.2.cloned.1.call-start
  7.2 0.7 compare_select_fusion.1
  7.9 0.7 compare_and_fusion.2
  8.6 0.7 fusion.46
  9.3 0.7 compare_and_fusion
  10.0 0.7 convert_element_type.18
  10.7 1.1 copy.22
  11.8 2.0 gather_fusion
  13.8 0.1 select_bitcast_fusion
  13.9 0.1 copy.23
  14.0 7.5 %gather_fusion.1 = bf16[2048,512]{1,0:T(8,128)(2,1)S(1)} fusion(bf16[256,512]{1,0:T(8,128)(2,1)S(1)} %copy.23, s32[2048]{0:T(1024)S(1)} %fusion.46), kind=kCustom, calls=%fused_computation.3 | custom fusion | bytes 4202496 | tf_op jit(solution)/shard_map/jit(_take)/gather | solution.py:40
  21.7 6.5 %fusion.16 = f32[512,1024]{1,0:T(8,128)} fusion(bf16[1024,2048]{1,0:T(8,128)(2,1)} %param.13, f32[2048]{0:T(1024)S(1)} %convert_element_type.18, bf16[2048,512]{1,0:T(8,128)(2,1)S(1)} %gather_fusion.1, pred[2048]{0:T(1024)(128)(4,1)S(1)} %compare_and_fusion), kind=kOutput, calls=%fused_computation.26 | convolution fusion | flops 2151677952 | bytes 8398848 | tf_op jit(solution)/shard_map/dot_general | solution.py:44
  28.2 0.0 reduce-scatter.2.cloned.1.call-update
  28.2 0.0 all-reduce.8.cloned.1.call-start
  28.3 0.8 compare_and_fusion.1
  29.1 0.8 gather_fusion.3
  29.9 0.8 gather_fusion.4
  30.7 0.1 copy.26
  30.8 0.6 gather_fusion.2
  31.5 0.6 dynamic-slice
  32.8 0.1 fusion.25
  32.9 0.1 fusion.24
  33.0 0.6 fusion.27
  33.6 4.0 %fusion.33 = f32[16,1024]{1,0:T(8,128)} fusion(bf16[1024,2048]{1,0:T(8,128)(2,1)} %param.13, s32[2048]{0:T(1024)S(1)} %copy-done.5, bf16[2048]{0:T(1024)(128)(2,1)S(1)} %copy-done.3), kind=kOutput, calls=%fused_computation.48 | convolution fusion | flops 67174400 | bytes 4272128 | tf_op jit(solution)/shard_map/dot_general | solution.py:34
  37.6 29.4 %reduce-scatter.2.cloned.1.call-done = f32[64,1024]{1,0:T(8,128)} async-done(((f32[512,1024]{1,0:T(8,128)}), f32[64,1024]{1,0:T(8,128)}) %reduce-scatter.2.cloned.1.call-update) | async-done | bytes 262160 | tf_op jit(solution)/shard_map/reduce_scatter | solution.py:43
  67.0 1.1 reshape.184
  68.1 0.6 fusion.38
  68.7 0.1 copy.28
  68.8 0.6 fusion.36
  69.4 0.1 copy.30
  69.5 0.4 while.17
  69.9 0.2 dynamic-update-slice.1
  70.1 0.2 dynamic-update-slice
  70.3 4.9 %all-reduce.5 = (f32[128]{0:T(128)S(1)}, f32[128]{0:T(128)S(1)}) all-reduce(f32[128]{0:T(128)S(1)} %dynamic-update-slice.1, f32[128]{0:T(128)S(1)} %dynamic-update-slice), channel_id=3, replica_groups=mesh['dirs'=2,'taps'=4,'tm'=2,'floors'=2] {'tm'}, use_global_device_ids=true, to_apply=%add.1 | all-reduce | flops 256 | bytes 2048
  75.2 0.1 reshape.227
  75.3 0.1 reshape.226
  75.4 0.1 select_reduce_fusion.1
  75.5 0.1 add_bitcast_fusion.1
  75.7 0.1 copy.25
  75.8 0.1 copy.24
  75.9 70.5 %fusion.20 = f32[64,4,256]{2,1,0:T(4,128)S(1)} fusion(f32[64,4,256]{2,1,0:T(4,128)S(1)} %reshape.184, f32[64]{0:T(128)S(1)} %get-tuple-element.116, f32[256,256]{1,0:T(8,128)S(1)} %fusion.24, f32[64]{0:T(128)S(1)} %get-tuple-element.115, f32[64]{0:T(128)S(1)} %get-tuple-element.129, pred[256,256]{1,0:T(8,128)(4,1)S(1)} %fusion.25, f32[64,4]{1,0:T(8,128)S(1)} %copy.25, ...), kind=kOutput, calls=%fused_computation.30 | convolution fusion | flops 222560256 | bytes 985856 | tf_op jit(solution)/shard_map/mij,mbj->mbi/dot_general | solution.py:67
  146.4 0.1 copy.31
  146.5 0.9 fusion.42
  147.4 0.0 all-reduce.8.cloned.1.call-update
  147.4 0.6 dynamic-slice.2
  148.7 51.3 %all-reduce.8.cloned.1.call-done = (f32[16,1024]{1,0:T(8,128)}, f32[16,1024]{1,0:T(8,128)}) async-done(((f32[16,1024]{1,0:T(8,128)}, f32[16,1024]{1,0:T(8,128)}), (f32[16,1024]{1,0:T(8,128)}, f32[16,1024]{1,0:T(8,128)})) %all-reduce.8.cloned.1.call-update) | async-done | bytes 131088
  200.0 1.4 constant_dynamic-slice_fusion
  201.4 1.4 dynamic-slice_multiply_fusion
  (42 shorter events, 0.6 us)
Async XLA Ops:
  7.2 21.9 %copy-start = (f32[512]{0:T(512)S(1)}, f32[512]{0:T(512)}, u32[]{:S(2)}) copy-start(f32[512]{0:T(512)} %param.20) | copy-start | bytes 6148
  7.2 59.8 %reduce-scatter.2.cloned.1.call-start = ((), (), s32[]{:S(2)}) async-start(), calls=%async_computation.1 | async-start | bytes 2359296 | tf_op jit(solution)/shard_map/reduce_scatter | solution.py:43
  21.6 8.3 %copy-start.1 = (f32[512]{0:T(512)S(1)}, f32[512]{0:T(512)}, u32[]{:S(2)}) copy-start(f32[512]{0:T(512)} %param.21) | copy-start | bytes 6148
  21.6 9.1 %copy-start.4 = (bf16[16,512]{1,0:T(8,128)(2,1)S(1)}, bf16[16,512]{1,0:T(8,128)(2,1)}, u32[]{:S(2)}) copy-start(bf16[16,512]{1,0:T(8,128)(2,1)} %param.18) | copy-start | bytes 49156
  21.6 9.9 %copy-start.7 = (u32[32]{0:T(128)S(1)}, u32[32]{0:T(128)}, u32[]{:S(2)}) copy-start(u32[32]{0:T(128)} %constant.106) | copy-start | bytes 388
  21.6 11.9 %copy-start.3 = (bf16[2048]{0:T(1024)(128)(2,1)S(1)}, bf16[2048]{0:T(1024)(128)(2,1)}, u32[]{:S(2)}) copy-start(bf16[2048]{0:T(1024)(128)(2,1)} %param.14) | copy-start | bytes 12292
  21.6 11.9 %copy-start.5 = (s32[2048]{0:T(1024)S(1)}, s32[2048]{0:T(1024)}, u32[]{:S(2)}) copy-start(s32[2048]{0:T(1024)} %param.16) | copy-start | bytes 24580
  28.2 171.8 %all-reduce.8.cloned.1.call-start = ((), (), s32[]{:S(2)}) async-start(), calls=%async_computation.2 | async-start | bytes 262144
  75.9 71.6 %copy-start.6 = (u32[32]{0:T(128)S(1)}, u32[32]{0:T(128)}, u32[]{:S(2)}) copy-start(u32[32]{0:T(128)} %constant.118) | copy-start | bytes 388
  146.5 56.3 %copy-start.2 = (f32[8,8,4,256]{3,1,2,0:T(8,128)}, f32[8,8,4,256]{3,1,2,0:T(8,128)S(1)}, u32[]{:S(2)}) copy-start(f32[8,8,4,256]{3,1,2,0:T(8,128)S(1)} %copy.31) | copy-start | bytes 786436
Sparse Core Ops, SparseCore 0:
  28.3 38.5 reduce-scatter.1
  147.6 52.4 all-reduce.7
where the time goes:
time: 210 us
  matrix products  83.3 us (40%)
  waiting for transfers between devices  80.7 us (38%)
  local copies, waits for them, and re-layouts  18 us (9%)
  between operations  15.6 us (7%)
  other arithmetic  6.88 us (3%)
  blocking collectives  4.92 us (2%)
    dot_general x1, matrix products, on_device(): jnp.einsum('mij,mbj->mbi', toeplitz, force_blocks, precision=highest)  70.5 us
    unnamed x3, waiting for transfers between devices  51.4 us
    reduce_scatter x1, waiting for transfers between devices, on_device(): lax.psum_scatter(lax.dot_general(tributary, pressures, (((0,), (1,)), (()...  29.4 us
    gather x1, local copies, waits for them, and re-layouts, on_device(): jnp.take(ordered, tap_panel, axis=0).astype(jnp.float32)  7.54 us
    dot_general x1, matrix products, on_device(): lax.dot_general(tributary, pressures, (((0,), (1,)), ((), ())), preferred...  6.54 us
    unnamed x1, blocking collectives  4.92 us
    unnamed x26, local copies, waits for them, and re-layouts  4.29 us
  transfers between devices with their start and end apart: 2, of which 2 were waited for; matrix products, arithmetic and copies ran while one was open for 4% of the time, Pallas kernels for 0%

commit v1 on v0

v1 whole, which is shorter than its diff:
```python
import jax
import jax.numpy as jnp
from jax import lax
from jax.experimental import pallas as pl
from jax.experimental.pallas import tpu as pltpu
from jax.sharding import PartitionSpec as P

BLK = 256
TILE = 128
BF = jnp.bfloat16
F32 = jnp.float32
NN = (((1,), (0,)), ((), ()))
NT = (((1,), (1,)), ((), ()))
VMEM_LIMIT = 48 * 1024 * 1024


def dot(a, b, dims=NN):
    return lax.dot_general(a, b, dims, preferred_element_type=F32)


def split(x):
    hi = x.astype(BF)
    return hi, (x - hi.astype(F32)).astype(BF)


def dot_exact_left(a, x, dims=NN):
    hi, lo = split(x)
    return dot(a, hi, dims) + dot(a, lo, dims)


def dot_exact_right(x, b, dims=NN):
    hi, lo = split(x)
    return dot(hi, b, dims) + dot(lo, b, dims)


def params():
    return pltpu.CompilerParams(vmem_limit_bytes=VMEM_LIMIT)


def whole(n):
    return [pl.BlockSpec(memory_space=pltpu.VMEM)] * n


def make_tap_sums(panels, floors, taps, time):
    rows = panels + floors

    def body(press_ref, panel_ref, floor_ref, area_ref, sums_ref, weights):
        @pl.when(pl.program_id(0) == 0)
        def _():
            area = area_ref[...].astype(F32)
            ids = lax.broadcasted_iota(jnp.int32, (panels, taps), 0)
            weights[:panels] = jnp.where(ids == panel_ref[...], area, 0.0).astype(BF)
            ids = lax.broadcasted_iota(jnp.int32, (floors, taps), 0)
            weights[panels:] = jnp.where(ids == floor_ref[...], area, 0.0).astype(BF)

        sums_ref[...] = dot(weights[...], press_ref[...], NT)

    row = pl.BlockSpec((1, taps), lambda i: (0, 0))
    return pl.pallas_call(
        body,
        grid=(time // BLK,),
        in_specs=[pl.BlockSpec((BLK, taps), lambda i: (i, 0)), row, row, row],
        out_specs=pl.BlockSpec((rows, BLK), lambda i: (0, i)),
        out_shape=jax.ShapeDtypeStruct((rows, time), F32),
        scratch_shapes=[pltpu.VMEM((rows, taps), BF)],
        compiler_params=params(),
        name="tap_sums",
    )


def mode_tables(order, decay, freq, panel_shape, floor_shape):
    modes = order.shape[1]
    panels = panel_shape.shape[0]
    floors = floor_shape.shape[0]

    def body(order_ref, decay_ref, freq_ref, panel_ref, floor_ref, pt_ref, fs_ref, rate_ref):
        spread = jnp.broadcast_to(order_ref[...].astype(F32), (TILE, modes))
        column = spread.T[:, :1]
        ids = lax.broadcasted_iota(jnp.int32, (modes, modes), 1).astype(F32)
        hit = column == ids
        rate_ref[:, 0:1] = jnp.sum(jnp.where(hit, decay_ref[...], 0.0), axis=1, keepdims=True)
        rate_ref[:, 1:2] = jnp.sum(jnp.where(hit, freq_ref[...], 0.0), axis=1, keepdims=True)
        pick = jnp.where(hit, 1.0, 0.0).astype(BF)
        pt_ref[...] = dot(pick, panel_ref[...], NT)
        fs_ref[...] = dot(floor_ref[...], pick, NT)

    return pl.pallas_call(
        body,
        in_specs=whole(5),
        out_specs=tuple(whole(3)),
        out_shape=(
            jax.ShapeDtypeStruct((modes, panels), F32),
            jax.ShapeDtypeStruct((floors, modes), F32),
            jax.ShapeDtypeStruct((modes, 2), F32),
        ),
        compiler_params=params(),
        name="mode_tables",
    )(order, decay, freq, panel_shape, floor_shape)


def slot_forces(place, sums, pt, nz, nc, mode_dev):
    panels = pt.shape[1]
    rows, time = sums[0].shape

    def body(place_ref, *refs):
        sum_refs, pt_ref, out_refs = refs[:nc], refs[nc], refs[nc + 1 :]
        z, c = place_ref[0], place_ref[1]
        total = sum_refs[0][:panels]
        for ref in sum_refs[1:]:
            total = total + ref[:panels]
        picked = []
        for d in range(nz):
            owner = lax.rem(z + d, nz) * nc + c
            picked.append(pt_ref[pl.ds(pl.multiple_of(owner * mode_dev, mode_dev), mode_dev), :])
        left = jnp.concatenate(picked, axis=0).astype(BF)
        forces = dot_exact_left(left, total)
        for d in range(nz):
            out_refs[d][...] = forces[d * mode_dev : (d + 1) * mode_dev]

    steps = time // BLK
    return pl.pallas_call(
        body,
        grid=(steps,),
        in_specs=[pl.BlockSpec(memory_space=pltpu.SMEM)]
        + [pl.BlockSpec((rows, BLK), lambda i: (0, i))] * nc
        + [pl.BlockSpec(pt.shape, lambda i: (0, 0))],
        out_specs=[pl.BlockSpec((mode_dev, BLK), lambda i: (0, i))] * nz,
        out_shape=[jax.ShapeDtypeStruct((mode_dev, time), F32)] * nz,
        compiler_params=params(),
        name="slot_forces",
    )(place, *sums, pt)


def turn_tables(decay, freq):
    slots = decay.shape[0]
    lane = lax.broadcasted_iota(jnp.int32, (slots, BLK), 1)
    step_re, step_im = jnp.cos(freq), jnp.sin(freq)
    re = jnp.ones((slots, BLK), F32)
    im = jnp.zeros((slots, BLK), F32)
    bit = 1
    while bit < BLK:
        on = (lane & bit) != 0
        new_re = re * step_re - im * step_im
        new_im = re * step_im + im * step_re
        re = jnp.where(on, new_re, re)
        im = jnp.where(on, new_im, im)
        step_re, step_im = step_re * step_re - step_im * step_im, 2.0 * step_re * step_im
        bit *= 2
    steps = decay * lane.astype(F32)
    shrink = jnp.exp(-steps)
    gain = jnp.sqrt(1.0 - jnp.exp(-2.0 * decay)) * jnp.exp(steps)
    fade = jnp.exp(-decay * float(BLK))
    return (gain * re, -gain * im, shrink * re, shrink * im, fade * step_re, fade * step_im)


def triangle():
    row = lax.broadcasted_iota(jnp.int32, (BLK, BLK), 0)
    col = lax.broadcasted_iota(jnp.int32, (BLK, BLK), 1)
    return jnp.where(row <= col, 1.0, 0.0).astype(BF)


def turned(a, b):
    return (a[0] * b[0] - a[1] * b[1], a[0] * b[1] + a[1] * b[0])


def partial_states(place, sums, pt, rates, floor_slots, mode_dev, floor_dev, nc):
    modes, panels = pt.shape
    rows, time = sums[0].shape
    floors = floor_slots.shape[0]
    blocks = time // BLK

    def body(place_ref, *refs):
        sum_refs = refs[:nc]
        pt_ref, rate_ref, fs_ref = refs[nc : nc + 3]
        motion_ref, ends_ref, qr_ref, qi_ref, own_ref, hi_ref, lo_ref, tab_ref = refs[nc + 3 :]
        total = sum_refs[0][:panels]
        for ref in sum_refs[1:]:
            total = total + ref[:panels]
        hi_ref[...], lo_ref[...] = split(total)
        motion_ref[...] = jnp.zeros_like(motion_ref)
        tri = triangle()

        @pl.loop(0, modes // TILE)
        def _(i):
            at = pl.ds(pl.multiple_of(i * TILE, TILE), TILE)
            rate = rate_ref[at, :]
            pr, pi, qr, qi, zr, zi = turn_tables(rate[:, 0:1], rate[:, 1:2])
            qr_ref[at, :] = qr
            qi_ref[at, :] = qi
            tab_ref[0, at, :] = pr
            tab_ref[1, at, :] = pi
            shape = pt_ref[at, :].astype(BF)
            here = fs_ref[:, at].astype(BF)
            ar = jnp.zeros((TILE, 1), F32)
            ai = jnp.zeros((TILE, 1), F32)
            for b in range(blocks):
                cols = slice(b * BLK, (b + 1) * BLK)
                force = dot(shape, hi_ref[:, cols]) + dot(shape, lo_ref[:, cols])
                cr = dot_exact_right(force * pr, tri) + ar
                ci = dot_exact_right(force * pi, tri) + ai
                resp = qr * cr - qi * ci
                motion_ref[:, cols] += dot_exact_left(here, resp)
                ar, ai = turned((zr, zi), (cr[:, BLK - 1 :], ci[:, BLK - 1 :]))
            pad = jnp.zeros((TILE, TILE - 4), F32)
            ends_ref[:, at] = jnp.concatenate([ar, ai, zr, zi, pad], axis=1).T[:8]

        own = pl.ds(pl.multiple_of(place_ref[2] * mode_dev, mode_dev), mode_dev)
        own_ref[0] = tab_ref[0, own, :]
        own_ref[1] = tab_ref[1, own, :]
        own_ref[2] = qr_ref[own, :]
        own_ref[3] = qi_ref[own, :]

    return pl.pallas_call(
        body,
        in_specs=[pl.BlockSpec(memory_space=pltpu.SMEM)] + whole(nc + 3),
        out_specs=tuple(whole(5)),
        out_shape=(
            jax.ShapeDtypeStruct((floors, time), F32),
            jax.ShapeDtypeStruct((8, modes), F32),
            jax.ShapeDtypeStruct((modes, BLK), F32),
            jax.ShapeDtypeStruct((modes, BLK), F32),
            jax.ShapeDtypeStruct((4, mode_dev, BLK), F32),
        ),
        scratch_shapes=[
            pltpu.VMEM((panels, time), BF),
            pltpu.VMEM((panels, time), BF),
            pltpu.VMEM((2, modes, BLK), F32),
        ],
        compiler_params=params(),
        name="partial_states",
    )(place, *sums, pt, rates, floor_slots)


def floor_shares(place, motion, ends, enter, qr, qi, floor_slots, sums, nz, nc, floor_dev, mode_dev):
    floors, time = motion.shape
    modes = floor_slots.shape[1]
    blocks = time // BLK
    rows = -(-(2 * floor_dev + 2) // 8) * 8
    load_at = sums[0].shape[0] - floors
    owners = nz * nc

    def body(place_ref, motion_ref, ends_ref, enter_ref, qr_ref, qi_ref, fs_ref, *refs):
        sum_refs, out_refs = refs[:nc], refs[nc : nc + nz]
        motions, loads, starts = refs[nc + nz :]
        z, c = place_ref[0], place_ref[1]
        shape = fs_ref[...]
        turn = (ends_ref[2:3, :], ends_ref[3:4, :])
        state = (enter_ref[0:1, :], enter_ref[1:2, :])
        left_re, left_im = [], []
        for b in range(blocks):
            left_re.append(shape * state[0])
            left_im.append(shape * state[1])
            state = turned(turn, state)
        qr_hi, qr_lo = split(qr_ref[...])
        qi_hi, qi_lo = split(qi_ref[...])
        re_hi, re_lo = split(jnp.concatenate(left_re, axis=0))
        im_hi, im_lo = split(jnp.concatenate(left_im, axis=0))
        free = dot(re_hi, qr_hi) + dot(re_hi, qr_lo) + dot(re_lo, qr_hi)
        free = free - (dot(im_hi, qi_hi) + dot(im_hi, qi_lo) + dot(im_lo, qi_hi))
        load = sum_refs[0][load_at:]
        for ref in sum_refs[1:]:
            load = load + ref[load_at:]
        full = jnp.concatenate([free[b * floors : (b + 1) * floors] for b in range(blocks)], axis=1)
        full = full + motion_ref[...]
        for o in range(owners):
            motions[o] = full[o * floor_dev : (o + 1) * floor_dev]
            loads[o] = load[o * floor_dev : (o + 1) * floor_dev]
            starts[o] = enter_ref[0:2, o * mode_dev : (o + 1) * mode_dev]
        for d in range(nz):
            owner = lax.rem(z + d, nz) * nc + c
            out = out_refs[d]
            out[...] = jnp.zeros_like(out)
            out[:floor_dev] = motions[owner]
            out[floor_dev : 2 * floor_dev] = loads[owner]
            out[2 * floor_dev : 2 * floor_dev + 2, :mode_dev] = starts[owner]

    return pl.pallas_call(
        body,
        in_specs=[pl.BlockSpec(memory_space=pltpu.SMEM)] + whole(6 + nc),
        out_specs=whole(nz),
        out_shape=[jax.ShapeDtypeStruct((rows, time), F32)] * nz,
        scratch_shapes=[
            pltpu.VMEM((owners, floor_dev, time), F32),
            pltpu.VMEM((owners, floor_dev, time), F32),
            pltpu.VMEM((owners, 2, mode_dev), F32),
        ],
        compiler_params=params(),
        name="floor_shares",
    )(place, motion, ends, enter, qr, qi, floor_slots, *sums)


def own_response(forces, shares, tables, floor_dev, load_scale):
    mode_dev, time = forces[0].shape
    n = len(forces)
    blocks = time // BLK

    def body(*refs):
        force_refs, share_refs, tab_ref = refs[:n], refs[n : 2 * n], refs[2 * n]
        resp_ref, motion_ref, load_ref = refs[2 * n + 1 :]
        share = share_refs[0][...]
        for ref in share_refs[1:]:
            share = share + ref[...]
        motion_ref[...] = share[:floor_dev]
        load_ref[...] = share[floor_dev : 2 * floor_dev] * load_scale
        pr, pi, qr, qi = tab_ref[0], tab_ref[1], tab_ref[2], tab_ref[3]
        zr = (qr[:, BLK - 1 :] * qr[:, 1:2]) - (qi[:, BLK - 1 :] * qi[:, 1:2])
        zi = (qr[:, BLK - 1 :] * qi[:, 1:2]) + (qi[:, BLK - 1 :] * qr[:, 1:2])
        column = share[:, :TILE].T
        at = 2 * floor_dev
        ar, ai = column[:mode_dev, at : at + 1], column[:mode_dev, at + 1 : at + 2]
        tri = triangle()
        for b in range(blocks):
            cols = slice(b * BLK, (b + 1) * BLK)
            force = force_refs[0][:, cols]
            for ref in force_refs[1:]:
                force = force + ref[:, cols]
            cr = dot_exact_right(force * pr, tri) + ar
            ci = dot_exact_right(force * pi, tri) + ai
            resp_ref[:, cols] = qr * cr - qi * ci
            ar, ai = turned((zr, zi), (cr[:, BLK - 1 :], ci[:, BLK - 1 :]))

    return pl.pallas_call(
        body,
        in_specs=whole(2 * n + 1),
        out_specs=tuple(whole(3)),
        out_shape=(
            jax.ShapeDtypeStruct((mode_dev, time), F32),
            jax.ShapeDtypeStruct((floor_dev, time), F32),
            jax.ShapeDtypeStruct((floor_dev, time), F32),
        ),
        compiler_params=params(),
        name="own_response",
    )(*forces, *shares, tables)


def shifts(x, axis, n):
    return [lax.ppermute(x, axis, [(i, (i + d) % n) for i in range(n)]) for d in range(1, n)]


def on_device(
    pressures,
    tap_area,
    tap_panel,
    tap_floor,
    panel_shape,
    floor_shape,
    mode_order,
    mode_decay,
    mode_freq,
):
    nz = lax.axis_size("taps")
    nc = lax.axis_size("floors")
    nt = lax.axis_size("tm")
    owners = nz * nc
    modes = mode_order.shape[0]
    mode_dev = modes // owners
    time, taps = pressures.shape
    panels = panel_shape.shape[0]
    floors = floor_shape.shape[0]
    floor_dev = floors // owners
    load_scale = (floors / (taps * owners)) ** 0.5
    z, c = lax.axis_index("taps"), lax.axis_index("floors")
    place = jnp.stack([z, c, z * nc + c]).astype(jnp.int32)

    mine = make_tap_sums(panels, floors, taps, time)(
        pressures, tap_panel[None], tap_floor[None], tap_area[None]
    )
    sums = [mine] + shifts(mine, "floors", nc)
    pt, floor_slots, rates = mode_tables(
        mode_order[None], mode_decay[None], mode_freq[None], panel_shape, floor_shape
    )
    forces = slot_forces(place, sums, pt, nz, nc, mode_dev)

    def along(parts):
        return [parts[0]] + [
            lax.ppermute(parts[d], "taps", [(i, (i + d) % nz) for i in range(nz)])
            for d in range(1, nz)
        ]

    got_forces = along(forces)
    motion, ends, qr, qi, tables = partial_states(
        place, sums, pt, rates, floor_slots, mode_dev, floor_dev, nc
    )
    steps = [(i, i + 1) for i in range(nt - 1)]
    enter = jnp.zeros_like(ends)
    for hop in range(nt - 1):
        if hop:
            over = (ends[2:3], ends[3:4])
            for _ in range(time // BLK - 1):
                over = turned(over, (ends[2:3], ends[3:4]))
            re, im = turned(over, (enter[0:1], enter[1:2]))
            passed = ends + jnp.concatenate([re, im, jnp.zeros_like(ends[2:])], axis=0)
        else:
            passed = ends
        enter = lax.ppermute(passed, "tm", steps)
    shares = floor_shares(
        place, motion, ends, enter, qr, qi, floor_slots, sums, nz, nc, floor_dev, mode_dev
    )
    got_shares = along(shares)
    return own_response(got_forces, got_shares, tables, floor_dev, load_scale)


def solution(mesh):
    in_specs = (
        P(("dirs", "tm"), ("taps", "floors")),
        P(("taps", "floors")),
        P(("taps", "floors")),
        P(("taps", "floors")),
        P(),
        P(),
        P(),
        P(),
        P(),
    )
    out_specs = (
        P(("taps", "floors"), ("dirs", "tm")),
        P(("taps", "floors"), ("dirs", "tm")),
        P(("taps", "floors"), ("dirs", "tm")),
    )
    return jax.shard_map(
        on_device, mesh=mesh, in_specs=in_specs, out_specs=out_specs, check_vma=False
    )
```

time: 210 us -> 46.1 us (0.22)
  matrix products: 83.3 us -> 0 us
  waiting for transfers between devices: 80.7 us -> 11.7 us
  Pallas kernels: 0 us -> 17 us
  between operations: 15.6 us -> 0.7 us
  local copies, waits for them, and re-layouts: 18 us -> 4.3 us
  starting transfers between devices: 0.08 us -> 11.9 us
  other arithmetic: 6.88 us -> 0.08 us
  blocking collectives: 4.92 us -> 0 us
    dot_general x6 -> x0, matrix products: 83.3 us -> none  [the longest x1 70.5 us: on_device(): jnp.einsum('mij,mbj->mbi', toeplitz, force_blocks, precision=highest)]
    unnamed x3 -> x0, waiting for transfers between devices: 51.4 us -> none
    reduce_scatter x1 -> x0, waiting for transfers between devices: 29.4 us -> none  [on_device(): lax.psum_scatter(lax.dot_general(tributary, pressures, (((0,), (1,)), (()...]
    pallas_call x0 -> x6, Pallas kernels: none -> 17 us  [the longest x1 10.1 us: partial_states(): pl.pallas_call(body, in_specs=[pl.BlockSpec(memory_space=pltpu.SMEM)] + w...]
    ppermute x0 -> x8, starting transfers between devices: none -> 11.9 us  [the longest x6 8.01 us: along(): lax.ppermute(parts[d], 'taps', [(i, (i + d) % nz) for i in range(nz)])]
    ppermute x0 -> x8, waiting for transfers between devices: none -> 11.7 us  [the longest x6 8.71 us: along(): lax.ppermute(parts[d], 'taps', [(i, (i + d) % nz) for i in range(nz)])]
    gather x5 -> x0, local copies, waits for them, and re-layouts: 11.7 us -> none  [the longest x1 7.54 us: on_device(): jnp.take(ordered, tap_panel, axis=0).astype(jnp.float32)]
    unnamed x1 -> x0, blocking collectives: 4.92 us -> none
  transfers between devices with their start and end apart: 2 -> 8, of which waited for: 2 -> 5; matrix products, arithmetic and copies ran while one was open for 4% -> 0% of each run, Pallas kernels for 0% -> 26%
where the time goes in v1:
time: 46.1 us; the launch traced here: 45.8 us
  Pallas kernels  17 us (37%)
  starting transfers between devices  11.9 us (26%)
  waiting for transfers between devices  11.7 us (25%)
  local copies, waits for them, and re-layouts  4.3 us (9%)
  between operations  0.7 us (2%)
    pallas_call x1, Pallas kernels, partial_states(): pl.pallas_call(body, in_specs=[pl.BlockSpec(memory_space=pltpu.SMEM)] + w...  10.1 us
    ppermute x6, waiting for transfers between devices, along(): lax.ppermute(parts[d], 'taps', [(i, (i + d) % nz) for i in range(nz)])  8.71 us
    ppermute x6, starting transfers between devices, along(): lax.ppermute(parts[d], 'taps', [(i, (i + d) % nz) for i in range(nz)])  8.01 us
    unnamed x16, local copies, waits for them, and re-layouts  3.6 us
    ppermute x1, starting transfers between devices, on_device(): enter = lax.ppermute(passed, 'tm', steps)  3.38 us
    pallas_call x1, Pallas kernels, on_device(): make_tap_sums(panels, floors, taps, time)  2.24 us
    pallas_call x1, Pallas kernels, slot_forces(): pl.pallas_call(body, grid=(steps,), in_specs=[pl.BlockSpec(memory_space=p...  1.75 us
    ppermute x1, waiting for transfers between devices, shifts(): lax.ppermute(x, axis, [(i, (i + d) % n) for i in range(n)])  1.58 us
  transfers between devices with their start and end apart: 8, of which 5 were waited for; matrix products, arithmetic and copies ran while one was open for 0% of the time, Pallas kernels for 26%

profile of v1, /device:TPU:0, one launch (start us, length us, event | category | flops | bytes accessed | tf_op | source)
XLA Modules:
  0.0 45.8 jit_solution(14865009205614850373)
XLA Ops:
  0.6 0.7 %broadcast_in_dim.20.area_ref = bf16[1,2048]{1,0:T(2,128)(2,1)S(1)} reshape(bf16[2048]{0:T(1024)(128)(2,1)} %param.10) | data formatting | bytes 8192 | tf_op jit(solution)/shard_map/broadcast_in_dim | solution.py:366
  1.3 0.0 copy-start
  1.3 2.2 %copy-done = bf16[1024,2048]{1,0:T(8,128)(2,1)S(1)} copy-done((bf16[1024,2048]{1,0:T(8,128)(2,1)S(1)}, bf16[1024,2048]{1,0:T(8,128)(2,1)}, u32[]{:S(2)}) %copy-start) | copy-done | bytes 4194328
  3.5 0.0 copy-start.3
  3.5 0.7 %copy-done.3 = s32[2048]{0:T(1024)S(1)} copy-done((s32[2048]{0:T(1024)S(1)}, s32[2048]{0:T(1024)}, u32[]{:S(2)}) %copy-start.3) | copy-done | bytes 8216
  4.2 0.0 copy-start.4
  4.2 0.7 %copy-done.4 = s32[2048]{0:T(1024)S(1)} copy-done((s32[2048]{0:T(1024)S(1)}, s32[2048]{0:T(1024)}, u32[]{:S(2)}) %copy-start.4) | copy-done | bytes 8216
  4.9 0.0 copy-start.1
  4.9 0.0 copy-start.2
  4.9 0.0 copy-start.5
  4.9 0.0 copy-start.6
  4.9 0.0 copy-start.7
  4.9 2.2 %tap_sums.1.refs_0_ = f32[272,1024]{1,0:T(8,128)S(1)} custom-call(bf16[1024,2048]{1,0:T(8,128)(2,1)S(1)} %copy-done, s32[1,2048]{1,0:T(1,128)S(1)} %bitcast.8, s32[1,2048]{1,0:T(1,128)S(1)} %bitcast.9, bf16[1,2048]{1,0:T(2,128)(2,1)S(1)} %broadcast_in_dim.20.area_ref), custom_call_target="tpu_custom_call" | custom-call | tf_op jit(solution)/shard_map/tap_sums/pallas_call | solution.py:365
  7.2 0.5 %collective-permute-start = (f32[272,1024]{1,0:T(8,128)S(1)}, f32[272,1024]{1,0:T(8,128)S(1)}, u32[]{:S(2)}, u32[]{:S(2)}) collective-permute-start(f32[272,1024]{1,0:T(8,128)S(1)} %tap_sums.1.refs_0_), channel_id=1, source_target_pairs={{0,1},{1,0},{2,3},{3,2},{4,5},{5,4},{6,7},{7,6},{8,9},{9,8},{10,11... | collective-permute-start | bytes 3342344 | tf_op jit(solution)/shard_map/ppermute | solution.py:337
  7.7 0.0 copy-done.1
  7.7 0.0 copy-done.2
  7.7 0.0 copy-done.5
  7.7 0.0 copy-done.6
  7.7 0.0 copy-done.7
  7.7 0.7 %mode_tables.1 = (f32[512,256]{1,0:T(8,128)S(1)}, f32[16,512]{1,0:T(8,128)S(1)}, f32[512,2]{1,0:T(8,128)S(1)}) custom-call(s32[1,512]{1,0:T(1,128)S(1)} %bitcast.10, f32[1,512]{1,0:T(1,128)S(1)} %bitcast.11, f32[1,512]{1,0:T(1,128)S(1)} %bitcast.12, bf16[256,512]{1,0:T(8,128)(2,1)S(1)} %copy-done.1, bf16[16,512]{1,0:T(8,128)(2,1)S(1)} %copy-done.2), custom_call_target="tpu_custom_call" | custom-call | tf_op jit(solution)/shard_map/mode_tables/pallas_call | solution.py:87
  8.4 0.1 pad_add_fusion.place_ref
  8.5 1.6 %collective-permute-done.refs_1_ = f32[272,1024]{1,0:T(8,128)S(1)} collective-permute-done((f32[272,1024]{1,0:T(8,128)S(1)}, f32[272,1024]{1,0:T(8,128)S(1)}, u32[]{:S(2)}, u32[]{:S(2)}) %collective-permute-start) | collective-permute-done | bytes 1114144 | tf_op jit(solution)/shard_map/ppermute | solution.py:337
  10.1 1.8 %slot_forces.1 = (f32[64,1024]{1,0:T(8,128)S(1)}, f32[64,1024]{1,0:T(8,128)S(1)}, f32[64,1024]{1,0:T(8,128)S(1)}, f32[64,1024]{1,0:T(8,128)S(1)}) custom-call(s32[3]{0:T(128)S(1)} %pad_add_fusion.place_ref, f32[272,1024]{1,0:T(8,128)S(1)} %tap_sums.1.refs_0_, f32[272,1024]{1,0:T(8,128)S(1)} %collective-permute-done.refs_1_, ...), custom_call_target="tpu_custom_call" | custom-call | tf_op jit(solution)/shard_map/slot_forces/pallas_call | solution.py:121
  11.8 3.0 %collective-permute-start.1 = (f32[64,1024]{1,0:T(8,128)S(1)}, f32[64,1024]{1,0:T(8,128)S(1)}, u32[]{:S(2)}, u32[]{:S(2)}) collective-permute-start(f32[64,1024]{1,0:T(8,128)S(1)} %get-tuple-element.21), channel_id=1, source_target_pairs={{0,4},{4,8},{8,12},{12,0},{1,5},{5,9},{9,13},{13,1},{2,6},{6,10},{... | collective-permute-start | bytes 786440 | tf_op jit(solution)/shard_map/ppermute | solution.py:376
  14.8 2.6 %collective-permute-start.2 = (f32[64,1024]{1,0:T(8,128)S(1)}, f32[64,1024]{1,0:T(8,128)S(1)}, u32[]{:S(2)}, u32[]{:S(2)}) collective-permute-start(f32[64,1024]{1,0:T(8,128)S(1)} %get-tuple-element.22), channel_id=1, source_target_pairs={{0,8},{4,12},{8,0},{12,4},{1,9},{5,13},{9,1},{13,5},{2,10},{6,14},... | collective-permute-start | bytes 786440 | tf_op jit(solution)/shard_map/ppermute | solution.py:376
  17.4 1.3 %collective-permute-start.3 = (f32[64,1024]{1,0:T(8,128)S(1)}, f32[64,1024]{1,0:T(8,128)S(1)}, u32[]{:S(2)}, u32[]{:S(2)}) collective-permute-start(f32[64,1024]{1,0:T(8,128)S(1)} %get-tuple-element.23), channel_id=1, source_target_pairs={{0,12},{4,0},{8,4},{12,8},{1,13},{5,1},{9,5},{13,9},{2,14},{6,2},{... | collective-permute-start | bytes 786440 | tf_op jit(solution)/shard_map/ppermute | solution.py:376
  18.8 10.1 %partial_states.1 = (f32[16,1024]{1,0:T(8,128)S(1)}, f32[8,512]{1,0:T(8,128)S(1)}, f32[512,256]{1,0:T(8,128)S(1)}, f32[512,256]{1,0:T(8,128)S(1)}, f32[4,64,256]{2,1,0:T(8,128)S(1)}) custom-call(s32[3]{0:T(128)S(1)} %pad_add_fusion.place_ref, f32[272,1024]{1,0:T(8,128)S(1)} %tap_sums.1.refs_0_, f32[272,1024]{1,0:T(8,128)S(1)} %collective-permute-done.refs_1_, ...), custom_call_target="tpu_custom_call" | custom-call | tf_op jit(solution)/shard_map/partial_states/pallas_call | solution.py:213
  28.9 3.4 %collective-permute-start.4 = (f32[8,512]{1,0:T(8,128)S(1)}, f32[8,512]{1,0:T(8,128)S(1)}, u32[]{:S(2)}, u32[]{:S(2)}) collective-permute-start(f32[8,512]{1,0:T(8,128)S(1)} %get-tuple-element.27.ends_ref), channel_id=1, source_target_pairs={{0,2},{1,3},{4,6},{5,7},{8,10},{9,11},{12,14},{13,15},{16,18},{17,... | collective-permute-start | bytes 49160 | tf_op jit(solution)/shard_map/ppermute | solution.py:395
  32.3 1.4 %collective-permute-done.4.enter_ref = f32[8,512]{1,0:T(8,128)S(1)} collective-permute-done((f32[8,512]{1,0:T(8,128)S(1)}, f32[8,512]{1,0:T(8,128)S(1)}, u32[]{:S(2)}, u32[]{:S(2)}) %collective-permute-start.4) | collective-permute-done | bytes 16416 | tf_op jit(solution)/shard_map/ppermute | solution.py:395
  33.7 1.0 %floor_shares.1 = (f32[8,1024]{1,0:T(8,128)S(1)}, f32[8,1024]{1,0:T(8,128)S(1)}, f32[8,1024]{1,0:T(8,128)S(1)}, f32[8,1024]{1,0:T(8,128)S(1)}) custom-call(s32[3]{0:T(128)S(1)} %pad_add_fusion.place_ref, f32[16,1024]{1,0:T(8,128)S(1)} %get-tuple-element.26.motion_ref, f32[8,512]{1,0:T(8,128)S(1)} %get-tuple-element.27.ends_ref, ...), custom_call_target="tpu_custom_call" | custom-call | tf_op jit(solution)/shard_map/floor_shares/pallas_call | solution.py:277
  34.7 0.7 %collective-permute-start.5 = (f32[8,1024]{1,0:T(8,128)S(1)}, f32[8,1024]{1,0:T(8,128)S(1)}, u32[]{:S(2)}, u32[]{:S(2)}) collective-permute-start(f32[8,1024]{1,0:T(8,128)S(1)} %get-tuple-element.31), channel_id=1, source_target_pairs={{0,4},{4,8},{8,12},{12,0},{1,5},{5,9},{9,13},{13,1},{2,6},{6,10},{... | collective-permute-start | bytes 98312 | tf_op jit(solution)/shard_map/ppermute | solution.py:376
  35.4 0.3 collective-permute-start.6
  35.8 4.8 %collective-permute-done.5.refs_5_ = f32[8,1024]{1,0:T(8,128)S(1)} collective-permute-done((f32[8,1024]{1,0:T(8,128)S(1)}, f32[8,1024]{1,0:T(8,128)S(1)}, u32[]{:S(2)}, u32[]{:S(2)}) %collective-permute-start.5) | collective-permute-done | bytes 32800 | tf_op jit(solution)/shard_map/ppermute | solution.py:376
  40.6 0.0 collective-permute-start.7
  40.6 2.0 %collective-permute-done.6.refs_6_ = f32[8,1024]{1,0:T(8,128)S(1)} collective-permute-done((f32[8,1024]{1,0:T(8,128)S(1)}, f32[8,1024]{1,0:T(8,128)S(1)}, u32[]{:S(2)}, u32[]{:S(2)}) %collective-permute-start.6) | collective-permute-done | bytes 32800 | tf_op jit(solution)/shard_map/ppermute | solution.py:376
  42.6 1.9 %collective-permute-done.7.refs_7_ = f32[8,1024]{1,0:T(8,128)S(1)} collective-permute-done((f32[8,1024]{1,0:T(8,128)S(1)}, f32[8,1024]{1,0:T(8,128)S(1)}, u32[]{:S(2)}, u32[]{:S(2)}) %collective-permute-start.7) | collective-permute-done | bytes 32800 | tf_op jit(solution)/shard_map/ppermute | solution.py:376
  44.5 0.0 collective-permute-done.1.refs_1_
  44.5 0.0 collective-permute-done.2.refs_2_
  44.5 0.0 collective-permute-done.3.refs_3_
  44.5 1.2 %own_response.1 = (f32[64,1024]{1,0:T(8,128)}, f32[2,1024]{1,0:T(2,128)}, f32[2,1024]{1,0:T(2,128)}) custom-call(f32[64,1024]{1,0:T(8,128)S(1)} %get-tuple-element.20.refs_0_, f32[64,1024]{1,0:T(8,128)S(1)} %collective-permute-done.1.refs_1_, f32[64,1024]{1,0:T(8,128)S(1)} %collective-permute-done.2.refs_2_, f32[64,1024]{1,0:T(8,128)S(1)} %collective-permute-done.3.refs_3_, ...), custom_call_target="tpu_custom_call" | custom-call | tf_op jit(solution)/shard_map/own_response/pallas_call | solution.py:322
Async XLA Ops:
  1.3 2.2 %copy-start = (bf16[1024,2048]{1,0:T(8,128)(2,1)S(1)}, bf16[1024,2048]{1,0:T(8,128)(2,1)}, u32[]{:S(2)}) copy-start(bf16[1024,2048]{1,0:T(8,128)(2,1)} %press_ref.1) | copy-start | bytes 12582916
  3.5 0.7 %copy-start.3 = (s32[2048]{0:T(1024)S(1)}, s32[2048]{0:T(1024)}, u32[]{:S(2)}) copy-start(s32[2048]{0:T(1024)} %param.11) | copy-start | bytes 24580
  4.2 0.7 %copy-start.4 = (s32[2048]{0:T(1024)S(1)}, s32[2048]{0:T(1024)}, u32[]{:S(2)}) copy-start(s32[2048]{0:T(1024)} %param.12) | copy-start | bytes 24580
  4.9 2.8 %copy-start.1 = (bf16[256,512]{1,0:T(8,128)(2,1)S(1)}, bf16[256,512]{1,0:T(8,128)(2,1)}, u32[]{:S(2)}) copy-start(bf16[256,512]{1,0:T(8,128)(2,1)} %panel_ref.1) | copy-start | bytes 786436
  4.9 2.8 %copy-start.2 = (bf16[16,512]{1,0:T(8,128)(2,1)S(1)}, bf16[16,512]{1,0:T(8,128)(2,1)}, u32[]{:S(2)}) copy-start(bf16[16,512]{1,0:T(8,128)(2,1)} %floor_ref.1) | copy-start | bytes 49156
  4.9 2.8 %copy-start.5 = (s32[512]{0:T(512)S(1)}, s32[512]{0:T(512)}, u32[]{:S(2)}) copy-start(s32[512]{0:T(512)} %param.15) | copy-start | bytes 6148
  4.9 2.8 %copy-start.6 = (f32[512]{0:T(512)S(1)}, f32[512]{0:T(512)}, u32[]{:S(2)}) copy-start(f32[512]{0:T(512)} %param.16) | copy-start | bytes 6148
  4.9 2.8 %copy-start.7 = (f32[512]{0:T(512)S(1)}, f32[512]{0:T(512)}, u32[]{:S(2)}) copy-start(f32[512]{0:T(512)} %param.17) | copy-start | bytes 6148
  7.2 2.9 %collective-permute-start = (f32[272,1024]{1,0:T(8,128)S(1)}, f32[272,1024]{1,0:T(8,128)S(1)}, u32[]{:S(2)}, u32[]{:S(2)}) collective-permute-start(f32[272,1024]{1,0:T(8,128)S(1)} %tap_sums.1.refs_0_), channel_id=1, source_target_pairs={{0,1},{1,0},{2,3},{3,2},{4,5},{5,4},{6,7},{7,6},{8,9},{9,8},{10,11... | collective-permute-start | bytes 3342344 | tf_op jit(solution)/shard_map/ppermute | solution.py:337
  11.8 32.7 %collective-permute-start.1 = (f32[64,1024]{1,0:T(8,128)S(1)}, f32[64,1024]{1,0:T(8,128)S(1)}, u32[]{:S(2)}, u32[]{:S(2)}) collective-permute-start(f32[64,1024]{1,0:T(8,128)S(1)} %get-tuple-element.21), channel_id=1, source_target_pairs={{0,4},{4,8},{8,12},{12,0},{1,5},{5,9},{9,13},{13,1},{2,6},{6,10},{... | collective-permute-start | bytes 786440 | tf_op jit(solution)/shard_map/ppermute | solution.py:376
  14.8 29.7 %collective-permute-start.2 = (f32[64,1024]{1,0:T(8,128)S(1)}, f32[64,1024]{1,0:T(8,128)S(1)}, u32[]{:S(2)}, u32[]{:S(2)}) collective-permute-start(f32[64,1024]{1,0:T(8,128)S(1)} %get-tuple-element.22), channel_id=1, source_target_pairs={{0,8},{4,12},{8,0},{12,4},{1,9},{5,13},{9,1},{13,5},{2,10},{6,14},... | collective-permute-start | bytes 786440 | tf_op jit(solution)/shard_map/ppermute | solution.py:376
  17.4 27.1 %collective-permute-start.3 = (f32[64,1024]{1,0:T(8,128)S(1)}, f32[64,1024]{1,0:T(8,128)S(1)}, u32[]{:S(2)}, u32[]{:S(2)}) collective-permute-start(f32[64,1024]{1,0:T(8,128)S(1)} %get-tuple-element.23), channel_id=1, source_target_pairs={{0,12},{4,0},{8,4},{12,8},{1,13},{5,1},{9,5},{13,9},{2,14},{6,2},{... | collective-permute-start | bytes 786440 | tf_op jit(solution)/shard_map/ppermute | solution.py:376
  28.9 4.8 %collective-permute-start.4 = (f32[8,512]{1,0:T(8,128)S(1)}, f32[8,512]{1,0:T(8,128)S(1)}, u32[]{:S(2)}, u32[]{:S(2)}) collective-permute-start(f32[8,512]{1,0:T(8,128)S(1)} %get-tuple-element.27.ends_ref), channel_id=1, source_target_pairs={{0,2},{1,3},{4,6},{5,7},{8,10},{9,11},{12,14},{13,15},{16,18},{17,... | collective-permute-start | bytes 49160 | tf_op jit(solution)/shard_map/ppermute | solution.py:395
  34.7 5.9 %collective-permute-start.5 = (f32[8,1024]{1,0:T(8,128)S(1)}, f32[8,1024]{1,0:T(8,128)S(1)}, u32[]{:S(2)}, u32[]{:S(2)}) collective-permute-start(f32[8,1024]{1,0:T(8,128)S(1)} %get-tuple-element.31), channel_id=1, source_target_pairs={{0,4},{4,8},{8,12},{12,0},{1,5},{5,9},{9,13},{13,1},{2,6},{6,10},{... | collective-permute-start | bytes 98312 | tf_op jit(solution)/shard_map/ppermute | solution.py:376
  35.4 7.1 %collective-permute-start.6 = (f32[8,1024]{1,0:T(8,128)S(1)}, f32[8,1024]{1,0:T(8,128)S(1)}, u32[]{:S(2)}, u32[]{:S(2)}) collective-permute-start(f32[8,1024]{1,0:T(8,128)S(1)} %get-tuple-element.32), channel_id=1, source_target_pairs={{0,8},{4,12},{8,0},{12,4},{1,9},{5,13},{9,1},{13,5},{2,10},{6,14},... | collective-permute-start | bytes 98312 | tf_op jit(solution)/shard_map/ppermute | solution.py:376
  40.6 3.9 %collective-permute-start.7 = (f32[8,1024]{1,0:T(8,128)S(1)}, f32[8,1024]{1,0:T(8,128)S(1)}, u32[]{:S(2)}, u32[]{:S(2)}) collective-permute-start(f32[8,1024]{1,0:T(8,128)S(1)} %get-tuple-element.33), channel_id=1, source_target_pairs={{0,12},{4,0},{8,4},{12,8},{1,13},{5,1},{9,5},{13,9},{2,14},{6,2},{... | collective-permute-start | bytes 98312 | tf_op jit(solution)/shard_map/ppermute | solution.py:376

commit v2 on v1

v2 whole, which is shorter than its diff:
```python
import jax
import jax.numpy as jnp
from jax import lax
from jax.experimental import pallas as pl
from jax.experimental.pallas import tpu as pltpu
from jax.sharding import PartitionSpec as P

BLK = 256
TILE = 128
BF = jnp.bfloat16
F32 = jnp.float32
NN = (((1,), (0,)), ((), ()))
NT = (((1,), (1,)), ((), ()))
VMEM_LIMIT = 48 * 1024 * 1024


def dot(a, b, dims=NN):
    return lax.dot_general(a, b, dims, preferred_element_type=F32)


def split(x):
    hi = x.astype(BF)
    return hi, (x - hi.astype(F32)).astype(BF)


def dot_exact_left(a, x, dims=NN):
    hi, lo = split(x)
    return dot(a, hi, dims) + dot(a, lo, dims)


def dot_exact_right(x, b, dims=NN):
    hi, lo = split(x)
    return dot(hi, b, dims) + dot(lo, b, dims)


def params():
    return pltpu.CompilerParams(vmem_limit_bytes=VMEM_LIMIT)


def whole(n):
    return [pl.BlockSpec(memory_space=pltpu.VMEM)] * n


def tap_sums(pressures, tap_panel, tap_floor, tap_area, panels, floors):
    time, taps = pressures.shape
    rows = panels + floors
    chunks = time // BLK

    def body(press_hbm, panel_hbm, floor_hbm, area_hbm, sums_ref, press, panel, floor, area, weights, sems):
        small = [
            pltpu.make_async_copy(panel_hbm, panel, sems.at[chunks]),
            pltpu.make_async_copy(floor_hbm, floor, sems.at[chunks + 1]),
            pltpu.make_async_copy(area_hbm, area, sems.at[chunks + 2]),
        ]
        for copy in small:
            copy.start()
        large = []
        for i in range(chunks):
            at = pl.ds(i * BLK, BLK)
            large.append(pltpu.make_async_copy(press_hbm.at[at], press.at[at], sems.at[i]))
            large[i].start()
        for copy in small:
            copy.wait()
        each = area[...].astype(F32).reshape(1, taps)
        ids = lax.broadcasted_iota(jnp.int32, (panels, taps), 0)
        weights[:panels] = jnp.where(ids == panel[...], each, 0.0).astype(BF)
        ids = lax.broadcasted_iota(jnp.int32, (floors, taps), 0)
        weights[panels:] = jnp.where(ids == floor[...], each, 0.0).astype(BF)
        for i in range(chunks):
            at = slice(i * BLK, (i + 1) * BLK)
            large[i].wait()
            sums_ref[:, at] = dot(weights[...], press[at], NT)

    return pl.pallas_call(
        body,
        in_specs=[pl.BlockSpec(memory_space=pltpu.HBM)] * 4,
        out_specs=pl.BlockSpec(memory_space=pltpu.VMEM),
        out_shape=jax.ShapeDtypeStruct((rows, time), F32),
        scratch_shapes=[
            pltpu.VMEM((time, taps), BF),
            pltpu.VMEM((1, taps), jnp.int32),
            pltpu.VMEM((1, taps), jnp.int32),
            pltpu.VMEM(tap_area.shape, BF),
            pltpu.VMEM((rows, taps), BF),
            pltpu.SemaphoreType.DMA((chunks + 3,)),
        ],
        compiler_params=params(),
        name="tap_sums",
    )(pressures, tap_panel[None], tap_floor[None], tap_area)


def mode_tables(place, order, decay, freq, panel_shape, floor_shape, nz, nc):
    modes = order.shape[1]
    panels = panel_shape.shape[0]
    floors = floor_shape.shape[0]
    mode_dev = modes // (nz * nc)
    slots = mode_dev * nz
    bits = BLK.bit_length() - 1
    half = BLK // 2

    def body(place_ref, order_ref, decay_ref, freq_ref, panel_ref, floor_ref, pt_ref, fs_ref, tab_ref, turn_ref, column_ref):
        column_ref[...] = jnp.broadcast_to(order_ref[...].astype(F32), (TILE, modes)).T
        z, c = place_ref[0], place_ref[1]
        picked = []
        for d in range(nz):
            owner = lax.rem(z + d, nz) * nc + c
            picked.append(column_ref[pl.ds(pl.multiple_of(owner * mode_dev, mode_dev), mode_dev), :])
        column = jnp.concatenate(picked, axis=0)[:, :1]
        ids = lax.broadcasted_iota(jnp.int32, (slots, modes), 1).astype(F32)
        pick = jnp.where(column == ids, 1.0, 0.0).astype(BF)
        pt_ref[...] = dot(pick, panel_ref[...], NT).astype(BF)
        fs_ref[...] = dot(floor_ref[...], pick, NT)
        decays, angles = decay_ref[...], freq_ref[...]
        re, im = jnp.cos(angles), jnp.sin(angles)
        rows = [decays]
        square = decays * decays
        loss = 2.0 * jnp.exp(-decays) * decays * (1.0 + square * (1.0 / 6.0 + square * (1.0 / 120.0)))
        rows.append(jnp.sqrt(loss))
        for _ in range(bits + 1):
            rows += [re, im]
            re, im = re * re - im * im, 2.0 * re * im
        rows += [jnp.zeros_like(re)] * (-len(rows) % 16)
        count = len(rows)
        stack = jnp.concatenate(rows, axis=0)
        hi, mid = split(stack)
        low = (stack - hi.astype(F32) - mid.astype(F32)).astype(BF)
        parts = dot(pick, jnp.concatenate([hi, mid, low], axis=0), NT)
        cols = parts[:, :count] + parts[:, count : 2 * count] + parts[:, 2 * count : 3 * count]
        rate, gain = cols[:, 0:1], cols[:, 1:2]
        lane = lax.broadcasted_iota(jnp.int32, (slots, half), 1)
        cos = jnp.where((lane & 1) != 0, cols[:, 2:3], 1.0)
        sin = jnp.where((lane & 1) != 0, cols[:, 3:4], 0.0)
        for b in range(1, bits - 1):
            on = (lane & (1 << b)) != 0
            step = cols[:, 2 + 2 * b : 3 + 2 * b], cols[:, 3 + 2 * b : 4 + 2 * b]
            new_cos, new_sin = turned((cos, sin), step)
            cos, sin = jnp.where(on, new_cos, cos), jnp.where(on, new_sin, sin)
        at = 2 * bits
        far_cos, far_sin = turned((cos, sin), (cols[:, at : at + 1], cols[:, at + 1 : at + 2]))
        steps = rate * lane.astype(F32)
        shrink, grow = jnp.exp(-steps), gain * jnp.exp(steps)
        far_shrink = shrink * jnp.exp(-rate * float(half))
        far_grow = grow * jnp.exp(rate * float(half))
        near, far = slice(0, half), slice(half, BLK)
        tab_ref[0, :, near], tab_ref[0, :, far] = grow * cos, far_grow * far_cos
        tab_ref[1, :, near], tab_ref[1, :, far] = -grow * sin, -far_grow * far_sin
        tab_ref[2, :, near], tab_ref[2, :, far] = shrink * cos, far_shrink * far_cos
        tab_ref[3, :, near], tab_ref[3, :, far] = shrink * sin, far_shrink * far_sin
        fade = jnp.exp(-rate * float(BLK))
        turn_ref[...] = fade * cols[:, at + 2 : at + 4]

    return pl.pallas_call(
        body,
        in_specs=[pl.BlockSpec(memory_space=pltpu.SMEM)] + whole(5),
        out_specs=tuple(whole(4)),
        out_shape=(
            jax.ShapeDtypeStruct((slots, panels), BF),
            jax.ShapeDtypeStruct((floors, slots), F32),
            jax.ShapeDtypeStruct((4, slots, BLK), F32),
            jax.ShapeDtypeStruct((slots, 2), F32),
        ),
        scratch_shapes=[pltpu.VMEM((modes, TILE), F32)],
        compiler_params=params(),
        name="mode_tables",
    )(place, order, decay, freq, panel_shape, floor_shape)


def slot_forces(sums, pt, nz):
    slots, panels = pt.shape
    time = sums[0].shape[1]
    nc = len(sums)
    mode_dev = slots // nz

    def body(*refs):
        sum_refs, pt_ref, out_refs = refs[:nc], refs[nc], refs[nc + 1 :]
        left = pt_ref[...]
        for b in range(time // BLK):
            cols = slice(b * BLK, (b + 1) * BLK)
            total = sum_refs[0][:panels, cols]
            for ref in sum_refs[1:]:
                total = total + ref[:panels, cols]
            forces = dot_exact_left(left, total)
            for d in range(nz):
                out_refs[d][:, cols] = forces[d * mode_dev : (d + 1) * mode_dev]

    return pl.pallas_call(
        body,
        in_specs=whole(nc + 1),
        out_specs=whole(nz),
        out_shape=[jax.ShapeDtypeStruct((mode_dev, time), F32)] * nz,
        compiler_params=params(),
        name="slot_forces",
    )(*sums, pt)


def triangle():
    row = lax.broadcasted_iota(jnp.int32, (BLK, BLK), 0)
    col = lax.broadcasted_iota(jnp.int32, (BLK, BLK), 1)
    return jnp.where(row <= col, 1.0, 0.0).astype(BF)


def turned(a, b):
    return (a[0] * b[0] - a[1] * b[1], a[0] * b[1] + a[1] * b[0])


def partial_states(forces, tables, turns, floor_slots):
    nz = len(forces)
    mode_dev, time = forces[0].shape
    slots = turns.shape[0]
    floors = floor_slots.shape[0]
    blocks = time // BLK

    def body(*refs):
        force_refs = refs[:nz]
        tab_ref, turn_ref, fs_ref, motion_ref, ends_ref, all_ref = refs[nz:]
        for d in range(nz):
            all_ref[d * mode_dev : (d + 1) * mode_dev] = force_refs[d][...]
        tri = triangle()
        pad = jnp.zeros((TILE, TILE - 4), F32)
        for i in range(slots // TILE):
            at = slice(i * TILE, (i + 1) * TILE)
            pr, pi, qr, qi = tab_ref[0, at], tab_ref[1, at], tab_ref[2, at], tab_ref[3, at]
            turn = turn_ref[at, 0:1], turn_ref[at, 1:2]
            here = fs_ref[:, at].astype(BF)
            ar = jnp.zeros((TILE, 1), F32)
            ai = jnp.zeros((TILE, 1), F32)
            for b in range(blocks):
                cols = slice(b * BLK, (b + 1) * BLK)
                force = all_ref[at, cols]
                cr = dot_exact_right(force * pr, tri) + ar
                ci = dot_exact_right(force * pi, tri) + ai
                part = dot_exact_left(here, qr * cr - qi * ci)
                motion_ref[:, cols] = part if i == 0 else motion_ref[:, cols] + part
                ar, ai = turned(turn, (cr[:, BLK - 1 :], ci[:, BLK - 1 :]))
            ends_ref[:, at] = jnp.concatenate([ar, ai, *turn, pad], axis=1).T[:8]

    return pl.pallas_call(
        body,
        in_specs=whole(nz + 3),
        out_specs=tuple(whole(2)),
        out_shape=(
            jax.ShapeDtypeStruct((floors, time), F32),
            jax.ShapeDtypeStruct((8, slots), F32),
        ),
        scratch_shapes=[pltpu.VMEM((slots, time), F32)],
        compiler_params=params(),
        name="partial_states",
    )(*forces, tables, turns, floor_slots)


def floor_motion_share(motion, ends, enter, tables, floor_slots):
    floors, time = motion.shape
    blocks = time // BLK

    def body(motion_ref, ends_ref, enter_ref, tab_ref, fs_ref, out_ref):
        shape = fs_ref[...]
        turn = (ends_ref[2:3, :], ends_ref[3:4, :])
        state = (enter_ref[0:1, :], enter_ref[1:2, :])
        left_re, left_im = [], []
        for b in range(blocks):
            left_re.append(shape * state[0])
            left_im.append(shape * state[1])
            state = turned(turn, state)
        qr_hi, qr_lo = split(tab_ref[2])
        qi_hi, qi_lo = split(tab_ref[3])
        re_hi, re_lo = split(jnp.concatenate(left_re, axis=0))
        im_hi, im_lo = split(jnp.concatenate(left_im, axis=0))
        free = dot(re_hi, qr_hi) + dot(re_hi, qr_lo) + dot(re_lo, qr_hi)
        free = free - (dot(im_hi, qi_hi) + dot(im_hi, qi_lo) + dot(im_lo, qi_hi))
        for b in range(blocks):
            cols = slice(b * BLK, (b + 1) * BLK)
            out_ref[:, cols] = motion_ref[:, cols] + free[b * floors : (b + 1) * floors]

    return pl.pallas_call(
        body,
        in_specs=whole(5),
        out_specs=whole(1)[0],
        out_shape=jax.ShapeDtypeStruct((floors, time), F32),
        compiler_params=params(),
        name="floor_motion_share",
    )(motion, ends, enter, tables, floor_slots)


def owner_shares(place, motions, sums, enter, nz, floor_dev, mode_dev):
    nc = len(sums)
    floors, time = motions[0].shape
    rows = -(-(2 * floor_dev + 2) // 8) * 8
    load_at = sums[0].shape[0] - floors
    owners = nz * nc

    def body(place_ref, *refs):
        motion_refs, sum_refs, enter_ref = refs[:nc], refs[nc : 2 * nc], refs[2 * nc]
        out_refs, motion_all, load_all = refs[2 * nc + 1 : 2 * nc + 1 + nz], refs[-2], refs[-1]
        z, c = place_ref[0], place_ref[1]
        motion = motion_refs[0][...]
        load = sum_refs[0][load_at:]
        for i in range(1, nc):
            motion = motion + motion_refs[i][...]
            load = load + sum_refs[i][load_at:]
        for o in range(owners):
            motion_all[o] = motion[o * floor_dev : (o + 1) * floor_dev]
            load_all[o] = load[o * floor_dev : (o + 1) * floor_dev]
        for d in range(nz):
            owner = lax.rem(z + d, nz) * nc + c
            out = out_refs[d]
            out[...] = jnp.zeros_like(out)
            out[:floor_dev] = motion_all[owner]
            out[floor_dev : 2 * floor_dev] = load_all[owner]
            at = slice(d * mode_dev, (d + 1) * mode_dev)
            out[2 * floor_dev : 2 * floor_dev + 2, :mode_dev] = enter_ref[0:2, at]

    return pl.pallas_call(
        body,
        in_specs=[pl.BlockSpec(memory_space=pltpu.SMEM)] + whole(2 * nc + 1),
        out_specs=whole(nz),
        out_shape=[jax.ShapeDtypeStruct((rows, time), F32)] * nz,
        scratch_shapes=[pltpu.VMEM((owners, floor_dev, time), F32)] * 2,
        compiler_params=params(),
        name="owner_shares",
    )(place, *motions, *sums, enter)


def own_response(forces, shares, tables, turns, floor_dev, load_scale):
    mode_dev, time = forces[0].shape
    n = len(forces)
    blocks = time // BLK

    def body(*refs):
        force_refs, share_refs = refs[:n], refs[n : 2 * n]
        tab_ref, turn_ref, resp_ref, motion_ref, load_ref = refs[2 * n :]
        share = share_refs[0][...]
        for ref in share_refs[1:]:
            share = share + ref[...]
        motion_ref[...] = share[:floor_dev]
        load_ref[...] = share[floor_dev : 2 * floor_dev] * load_scale
        pr, pi, qr, qi = (tab_ref[i, :mode_dev] for i in range(4))
        turn = turn_ref[:mode_dev, 0:1], turn_ref[:mode_dev, 1:2]
        column = share[:, :TILE].T
        at = 2 * floor_dev
        ar, ai = column[:mode_dev, at : at + 1], column[:mode_dev, at + 1 : at + 2]
        tri = triangle()
        for b in range(blocks):
            cols = slice(b * BLK, (b + 1) * BLK)
            force = force_refs[0][:, cols]
            for ref in force_refs[1:]:
                force = force + ref[:, cols]
            cr = dot_exact_right(force * pr, tri) + ar
            ci = dot_exact_right(force * pi, tri) + ai
            resp_ref[:, cols] = qr * cr - qi * ci
            ar, ai = turned(turn, (cr[:, BLK - 1 :], ci[:, BLK - 1 :]))

    return pl.pallas_call(
        body,
        in_specs=whole(2 * n + 2),
        out_specs=tuple(whole(3)),
        out_shape=(
            jax.ShapeDtypeStruct((mode_dev, time), F32),
            jax.ShapeDtypeStruct((floor_dev, time), F32),
            jax.ShapeDtypeStruct((floor_dev, time), F32),
        ),
        compiler_params=params(),
        name="own_response",
    )(*forces, *shares, tables, turns)


def shifts(x, axis, n):
    return [lax.ppermute(x, axis, [(i, (i + d) % n) for i in range(n)]) for d in range(1, n)]


def along(parts, n):
    return [parts[0]] + [
        lax.ppermute(parts[d], "taps", [(i, (i + d) % n) for i in range(n)]) for d in range(1, n)
    ]


def on_device(
    pressures,
    tap_area,
    tap_panel,
    tap_floor,
    panel_shape,
    floor_shape,
    mode_order,
    mode_decay,
    mode_freq,
):
    nz = lax.axis_size("taps")
    nc = lax.axis_size("floors")
    nt = lax.axis_size("tm")
    owners = nz * nc
    modes = mode_order.shape[0]
    mode_dev = modes // owners
    time, taps = pressures.shape
    panels = panel_shape.shape[0]
    floors = floor_shape.shape[0]
    floor_dev = floors // owners
    load_scale = (floors / (taps * owners)) ** 0.5
    z, c = lax.axis_index("taps"), lax.axis_index("floors")
    place = jnp.stack([z, c, z * nc + c]).astype(jnp.int32)

    mine = tap_sums(pressures, tap_panel, tap_floor, tap_area, panels, floors)
    sums = [mine] + shifts(mine, "floors", nc)
    pt, floor_slots, tables, turns = mode_tables(
        place, mode_order[None], mode_decay[None], mode_freq[None], panel_shape, floor_shape, nz, nc
    )
    forces = slot_forces(sums, pt, nz)
    got_forces = along(forces, nz)
    motion, ends = partial_states(forces, tables, turns, floor_slots)
    enter = jnp.zeros_like(ends)
    for hop in range(nt - 1):
        passed = ends
        if hop:
            turn = (ends[2:3], ends[3:4])
            over = turn
            for _ in range(time // BLK - 1):
                over = turned(over, turn)
            passed = ends + jnp.concatenate([*turned(over, (enter[0:1], enter[1:2])), jnp.zeros_like(ends[2:])])
        enter = lax.ppermute(passed, "tm", [(i, (i + 1) % nt) for i in range(nt)])
        enter = jnp.where(lax.axis_index("tm") > 0, enter, 0.0)
    motion = floor_motion_share(motion, ends, enter, tables, floor_slots)
    motions = [motion] + shifts(motion, "floors", nc)
    shares = owner_shares(place, motions, sums, enter, nz, floor_dev, mode_dev)
    return own_response(
        got_forces, along(shares, nz), tables, turns, floor_dev, load_scale
    )


def solution(mesh):
    in_specs = (
        P(("dirs", "tm"), ("taps", "floors")),
        P(("taps", "floors")),
        P(("taps", "floors")),
        P(("taps", "floors")),
        P(),
        P(),
        P(),
        P(),
        P(),
    )
    out_specs = (
        P(("taps", "floors"), ("dirs", "tm")),
        P(("taps", "floors"), ("dirs", "tm")),
        P(("taps", "floors"), ("dirs", "tm")),
    )
    return jax.shard_map(
        on_device, mesh=mesh, in_specs=in_specs, out_specs=out_specs, check_vma=False
    )
```

time: 46.1 us -> 53.3 us (1.16)
  waiting for transfers between devices: 11.7 us -> 21.3 us
  Pallas kernels: 17 us -> 12.3 us
  local copies, waits for them, and re-layouts: 4.3 us -> 8.6 us
  starting transfers between devices: 11.9 us -> 9.77 us
    ppermute x7, waiting for transfers between devices: 10.1 us -> 20.1 us  [the longest x6 20.1 us: along(): lax.ppermute(parts[d], 'taps', [(i, (i + d) % n) for i in range(n)])]
    unnamed x16 -> x36, local copies, waits for them, and re-layouts: 3.6 us -> 8.6 us
    pallas_call x6 -> x7, Pallas kernels: 17 us -> 12.3 us  [the longest x1 3.67 us: tap_sums(): pl.pallas_call(body, in_specs=[pl.BlockSpec(memory_space=pltpu.HBM)] * 4,...]
    ppermute x7, starting transfers between devices: 11.4 us -> 9.19 us  [the longest x6 6.68 us: along(): lax.ppermute(parts[d], 'taps', [(i, (i + d) % n) for i in range(n)])]
    broadcast_in_dim x1 -> x0, local copies, waits for them, and re-layouts: 0.69 us -> none  [on_device(): tap_area[None]]
    ppermute x1 -> x2, waiting for transfers between devices: 1.58 us -> 1.24 us  [shifts(): lax.ppermute(x, axis, [(i, (i + d) % n) for i in range(n)])]
  transfers between devices with their start and end apart: 8 -> 9, of which waited for: 5 -> 4; matrix products, arithmetic and copies ran while one was open for 0% -> 0% of each run, Pallas kernels for 26% -> 7%
where the time goes in v2:
time: 53.3 us; the launch traced here: 52.8 us
  waiting for transfers between devices  21.3 us (40%)
  Pallas kernels  12.3 us (23%)
  starting transfers between devices  9.77 us (18%)
  local copies, waits for them, and re-layouts  8.6 us (16%)
  between operations  0.77 us (1%)
    ppermute x6, waiting for transfers between devices, along(): lax.ppermute(parts[d], 'taps', [(i, (i + d) % n) for i in range(n)])  20.1 us
    unnamed x36, local copies, waits for them, and re-layouts  8.6 us
    ppermute x6, starting transfers between devices, along(): lax.ppermute(parts[d], 'taps', [(i, (i + d) % n) for i in range(n)])  6.68 us
    pallas_call x1, Pallas kernels, tap_sums(): pl.pallas_call(body, in_specs=[pl.BlockSpec(memory_space=pltpu.HBM)] * 4,...  3.67 us
    pallas_call x1, Pallas kernels, partial_states(): pl.pallas_call(body, in_specs=whole(nz + 3), out_specs=tuple(whole(2)), o...  2.87 us
    ppermute x1, starting transfers between devices, on_device(): enter = lax.ppermute(passed, 'tm', [(i, (i + 1) % nt) for i in range(nt)])  2.51 us
    pallas_call x1, Pallas kernels, mode_tables(): pl.pallas_call(body, in_specs=[pl.BlockSpec(memory_space=pltpu.SMEM)] + w...  2.1 us
    pallas_call x1, Pallas kernels, own_response(): pl.pallas_call(body, in_specs=whole(2 * n + 2), out_specs=tuple(whole(3))...  1.6 us
  transfers between devices with their start and end apart: 9, of which 4 were waited for; matrix products, arithmetic and copies ran while one was open for 0% of the time, Pallas kernels for 7%

profile of v2, /device:TPU:0, one launch (start us, length us, event | category | flops | bytes accessed | tf_op | source)
XLA Modules:
  0.0 52.8 jit_solution(16317111918116955752)
XLA Ops:
  0.6 0.0 copy-start
  0.6 2.2 %copy-done = bf16[1024,2048]{1,0:T(8,128)(2,1)S(1)} copy-done((bf16[1024,2048]{1,0:T(8,128)(2,1)S(1)}, bf16[1024,2048]{1,0:T(8,128)(2,1)}, u32[]{:S(2)}) %copy-start) | copy-done | bytes 4194328
  2.8 0.7 %copy-done.10 = s32[2048]{0:T(1024)S(1)} copy-done((s32[2048]{0:T(1024)S(1)}, s32[2048]{0:T(1024)}, u32[]{:S(2)}) %copy-start.10) | copy-done | bytes 8216
  3.5 0.7 %copy-done.11 = s32[2048]{0:T(1024)S(1)} copy-done((s32[2048]{0:T(1024)S(1)}, s32[2048]{0:T(1024)}, u32[]{:S(2)}) %copy-start.11) | copy-done | bytes 8216
  4.2 0.7 %copy-done.14 = bf16[2048]{0:T(1024)(128)(2,1)S(1)} copy-done((bf16[2048]{0:T(1024)(128)(2,1)S(1)}, bf16[2048]{0:T(1024)(128)(2,1)}, u32[]{:S(2)}) %copy-start.14) | copy-done | bytes 4120
  4.9 3.7 %tap_sums.1.refs_0_.refs_2_ = f32[272,1024]{1,0:T(8,128)S(1)} custom-call(bf16[1024,2048]{1,0:T(8,128)(2,1)S(1)} %copy-done, s32[1,2048]{1,0:T(1,128)S(1)} %bitcast.8, s32[1,2048]{1,0:T(1,128)S(1)} %bitcast.9, bf16[2048]{0:T(1024)(128)(2,1)S(1)} %copy-done.14), custom_call_target="tpu_custom_call" | custom-call | tf_op jit(solution)/shard_map/tap_sums/pallas_call | solution.py:74
  8.6 0.5 collective-permute-start
  9.1 0.1 pad_add_fusion.place_ref
  9.2 0.0 copy-done.6
  9.2 0.7 %copy-done.9 = bf16[16,512]{1,0:T(8,128)(2,1)S(1)} copy-done((bf16[16,512]{1,0:T(8,128)(2,1)S(1)}, bf16[16,512]{1,0:T(8,128)(2,1)}, u32[]{:S(2)}) %copy-start.9) | copy-done | bytes 16408
  9.9 0.7 %copy-done.15 = s32[512]{0:T(512)S(1)} copy-done((s32[512]{0:T(512)S(1)}, s32[512]{0:T(512)}, u32[]{:S(2)}) %copy-start.15) | copy-done | bytes 2072
  10.6 0.7 %copy-done.16 = f32[512]{0:T(512)S(1)} copy-done((f32[512]{0:T(512)S(1)}, f32[512]{0:T(512)}, u32[]{:S(2)}) %copy-start.16) | copy-done | bytes 2072
  11.3 0.7 %copy-done.17 = f32[512]{0:T(512)S(1)} copy-done((f32[512]{0:T(512)S(1)}, f32[512]{0:T(512)}, u32[]{:S(2)}) %copy-start.17) | copy-done | bytes 2072
  11.9 2.1 %mode_tables.1 = (bf16[256,256]{1,0:T(8,128)(2,1)S(1)}, f32[16,256]{1,0:T(8,128)S(1)}, f32[4,256,256]{2,1,0:T(8,128)S(1)}, f32[256,2]{1,0:T(8,128)S(1)}) custom-call(s32[3]{0:T(128)S(1)} %pad_add_fusion.place_ref, s32[1,512]{1,0:T(1,128)S(1)} %bitcast.10, f32[1,512]{1,0:T(1,128)S(1)} %bitcast.11, f32[1,512]{1,0:T(1,128)S(1)} %bitcast.12, ...), custom_call_target="tpu_custom_call" | custom-call | tf_op jit(solution)/shard_map/mode_tables/pallas_call | solution.py:152
  14.1 0.0 collective-permute-done.refs_1_.refs_3_
  14.1 0.0 copy-done.12
  14.1 0.5 slot_forces.1
  14.6 0.0 copy-start.3
  14.6 0.0 copy-start.4
  14.6 0.0 copy-start.5
  14.6 0.1 copy-done.1
  14.7 2.9 %partial_states.1 = (f32[16,1024]{1,0:T(8,128)S(1)}, f32[8,256]{1,0:T(8,128)}) custom-call(f32[64,1024]{1,0:T(8,128)S(1)} %get-tuple-element.18.refs_0_, f32[64,1024]{1,0:T(8,128)S(1)} %get-tuple-element.19.refs_1_, f32[64,1024]{1,0:T(8,128)S(1)} %get-tuple-element.20.refs_2_, f32[64,1024]{1,0:T(8,128)S(1)} %get-tuple-element.21.refs_3_, ...), custom_call_target="tpu_custom_call" | custom-call | tf_op jit(solution)/shard_map/partial_states/pallas_call | solution.py:237
  17.6 0.0 copy-done.3
  17.6 0.0 copy-done.4
  17.6 0.0 copy-done.5
  17.6 0.6 %copy-done.7 = f32[16,1024]{1,0:T(8,128)} copy-done((f32[16,1024]{1,0:T(8,128)}, f32[16,1024]{1,0:T(8,128)S(1)}, u32[]{:S(2)}) %copy-start.7) | copy-done | bytes 65560
  18.2 2.5 %collective-permute-start.4 = (f32[8,256]{1,0:T(8,128)}, f32[8,256]{1,0:T(8,128)}, u32[]{:S(2)}, u32[]{:S(2)}) collective-permute-start(f32[8,256]{1,0:T(8,128)} %get-tuple-element.26.ends_ref), channel_id=1, source_target_pairs={{0,2},{2,0},{1,3},{3,1},{4,6},{6,4},{5,7},{7,5},{8,10},{10,8},{9,1... | collective-permute-start | bytes 24584 | tf_op jit(solution)/shard_map/ppermute | solution.py:418
  20.7 1.6 %collective-permute-start.1 = (f32[64,1024]{1,0:T(8,128)}, f32[64,1024]{1,0:T(8,128)S(1)}, u32[]{:S(2)}, u32[]{:S(2)}) collective-permute-start(f32[64,1024]{1,0:T(8,128)} %copy-done.5), channel_id=1, source_target_pairs={{0,4},{4,8},{8,12},{12,0},{1,5},{5,9},{9,13},{13,1},{2,6},{6,10},{... | collective-permute-start | bytes 786440 | tf_op jit(solution)/shard_map/ppermute | solution.py:372
  22.3 2.6 %collective-permute-start.2 = (f32[64,1024]{1,0:T(8,128)}, f32[64,1024]{1,0:T(8,128)S(1)}, u32[]{:S(2)}, u32[]{:S(2)}) collective-permute-start(f32[64,1024]{1,0:T(8,128)} %copy-done.4), channel_id=1, source_target_pairs={{0,8},{4,12},{8,0},{12,4},{1,9},{5,13},{9,1},{13,5},{2,10},{6,14},... | collective-permute-start | bytes 786440 | tf_op jit(solution)/shard_map/ppermute | solution.py:372
  24.9 1.3 %collective-permute-start.3 = (f32[64,1024]{1,0:T(8,128)}, f32[64,1024]{1,0:T(8,128)S(1)}, u32[]{:S(2)}, u32[]{:S(2)}) collective-permute-start(f32[64,1024]{1,0:T(8,128)} %copy-done.3), channel_id=1, source_target_pairs={{0,12},{4,0},{8,4},{12,8},{1,13},{5,1},{9,5},{13,9},{2,14},{6,2},{... | collective-permute-start | bytes 786440 | tf_op jit(solution)/shard_map/ppermute | solution.py:372
  26.2 0.0 collective-permute-done.4
  26.2 0.0 copy-start.8
  26.2 0.8 %copy-done.8 = f32[16,1024]{1,0:T(8,128)S(1)} copy-done((f32[16,1024]{1,0:T(8,128)S(1)}, f32[16,1024]{1,0:T(8,128)}, u32[]{:S(2)}) %copy-start.8) | copy-done | bytes 65560
  27.1 1.0 %floor_motion_share.1.refs_0_ = f32[16,1024]{1,0:T(8,128)S(1)} custom-call(f32[16,1024]{1,0:T(8,128)S(1)} %copy-done.8, f32[8,256]{1,0:T(8,128)} %get-tuple-element.26.ends_ref, f32[8,256]{1,0:T(8,128)S(1)} %broadcast_select_fusion.enter_ref.refs_4_, f32[4,256,256]{2,1,0:T(8,128)S(1)} %get-tuple-element.22.refs_4_.tab_ref.refs_8_, ...), custom_call_target="tpu_custom_call" | custom-call | tf_op jit(solution)/shard_map/floor_motion_share/pallas_call | solution.py:274
  28.1 0.1 collective-permute-start.5
  28.1 1.2 %collective-permute-done.5.refs_1_ = f32[16,1024]{1,0:T(8,128)S(1)} collective-permute-done((f32[16,1024]{1,0:T(8,128)S(1)}, f32[16,1024]{1,0:T(8,128)S(1)}, u32[]{:S(2)}, u32[]{:S(2)}) %collective-permute-start.5) | collective-permute-done | bytes 65568 | tf_op jit(solution)/shard_map/ppermute | solution.py:367
  29.4 0.0 copy-done.13
  29.4 0.6 %owner_shares.1 = (f32[8,1024]{1,0:T(8,128)S(1)}, f32[8,1024]{1,0:T(8,128)S(1)}, f32[8,1024]{1,0:T(8,128)S(1)}, f32[8,1024]{1,0:T(8,128)S(1)}) custom-call(s32[3]{0:T(128)S(1)} %copy-done.13, f32[16,1024]{1,0:T(8,128)S(1)} %floor_motion_share.1.refs_0_, f32[16,1024]{1,0:T(8,128)S(1)} %collective-permute-done.5.refs_1_, ...), custom_call_target="tpu_custom_call" | custom-call | tf_op jit(solution)/shard_map/owner_shares/pallas_call | solution.py:312
  30.0 0.7 %collective-permute-start.6 = (f32[8,1024]{1,0:T(8,128)S(1)}, f32[8,1024]{1,0:T(8,128)S(1)}, u32[]{:S(2)}, u32[]{:S(2)}) collective-permute-start(f32[8,1024]{1,0:T(8,128)S(1)} %get-tuple-element.28), channel_id=1, source_target_pairs={{0,4},{4,8},{8,12},{12,0},{1,5},{5,9},{9,13},{13,1},{2,6},{6,10},{... | collective-permute-start | bytes 98312 | tf_op jit(solution)/shard_map/ppermute | solution.py:372
  30.7 0.4 collective-permute-start.7
  31.2 12.5 %collective-permute-done.6.refs_5_ = f32[8,1024]{1,0:T(8,128)S(1)} collective-permute-done((f32[8,1024]{1,0:T(8,128)S(1)}, f32[8,1024]{1,0:T(8,128)S(1)}, u32[]{:S(2)}, u32[]{:S(2)}) %collective-permute-start.6) | collective-permute-done | bytes 32800 | tf_op jit(solution)/shard_map/ppermute | solution.py:372
  43.7 0.0 collective-permute-start.8
  43.7 6.6 %collective-permute-done.7.refs_6_ = f32[8,1024]{1,0:T(8,128)S(1)} collective-permute-done((f32[8,1024]{1,0:T(8,128)S(1)}, f32[8,1024]{1,0:T(8,128)S(1)}, u32[]{:S(2)}, u32[]{:S(2)}) %collective-permute-start.7) | collective-permute-done | bytes 32800 | tf_op jit(solution)/shard_map/ppermute | solution.py:372
  50.3 0.9 %collective-permute-done.8.refs_7_ = f32[8,1024]{1,0:T(8,128)S(1)} collective-permute-done((f32[8,1024]{1,0:T(8,128)S(1)}, f32[8,1024]{1,0:T(8,128)S(1)}, u32[]{:S(2)}, u32[]{:S(2)}) %collective-permute-start.8) | collective-permute-done | bytes 32800 | tf_op jit(solution)/shard_map/ppermute | solution.py:372
  51.2 0.0 collective-permute-done.1.refs_1_
  51.2 0.0 collective-permute-done.2.refs_2_
  51.2 0.0 collective-permute-done.3.refs_3_
  51.2 1.6 %own_response.1 = (f32[64,1024]{1,0:T(8,128)}, f32[2,1024]{1,0:T(2,128)}, f32[2,1024]{1,0:T(2,128)}) custom-call(f32[64,1024]{1,0:T(8,128)S(1)} %get-tuple-element.18.refs_0_, f32[64,1024]{1,0:T(8,128)S(1)} %collective-permute-done.1.refs_1_, f32[64,1024]{1,0:T(8,128)S(1)} %collective-permute-done.2.refs_2_, f32[64,1024]{1,0:T(8,128)S(1)} %collective-permute-done.3.refs_3_, ...), custom_call_target="tpu_custom_call" | custom-call | tf_op jit(solution)/shard_map/own_response/pallas_call | solution.py:352
  (15 shorter events, 0.0 us)
Async XLA Ops:
  0.6 2.2 %copy-start = (bf16[1024,2048]{1,0:T(8,128)(2,1)S(1)}, bf16[1024,2048]{1,0:T(8,128)(2,1)}, u32[]{:S(2)}) copy-start(bf16[1024,2048]{1,0:T(8,128)(2,1)} %press_hbm.1) | copy-start | bytes 12582916
  2.8 0.7 %copy-start.10 = (s32[2048]{0:T(1024)S(1)}, s32[2048]{0:T(1024)}, u32[]{:S(2)}) copy-start(s32[2048]{0:T(1024)} %param.11) | copy-start | bytes 24580
  3.5 0.7 %copy-start.11 = (s32[2048]{0:T(1024)S(1)}, s32[2048]{0:T(1024)}, u32[]{:S(2)}) copy-start(s32[2048]{0:T(1024)} %param.12) | copy-start | bytes 24580
  4.2 0.7 %copy-start.14 = (bf16[2048]{0:T(1024)(128)(2,1)S(1)}, bf16[2048]{0:T(1024)(128)(2,1)}, u32[]{:S(2)}) copy-start(bf16[2048]{0:T(1024)(128)(2,1)} %area_hbm.1) | copy-start | bytes 12292
  4.9 4.3 %copy-start.6 = (bf16[256,512]{1,0:T(8,128)(2,1)S(1)}, bf16[256,512]{1,0:T(8,128)(2,1)}, u32[]{:S(2)}) copy-start(bf16[256,512]{1,0:T(8,128)(2,1)} %panel_ref.1) | copy-start | bytes 786436
  8.6 5.5 %collective-permute-start = (f32[272,1024]{1,0:T(8,128)S(1)}, f32[272,1024]{1,0:T(8,128)S(1)}, u32[]{:S(2)}, u32[]{:S(2)}) collective-permute-start(f32[272,1024]{1,0:T(8,128)S(1)} %tap_sums.1.refs_0_.refs_2_), channel_id=1, source_target_pairs={{0,1},{1,0},{2,3},{3,2},{4,5},{5,4},{6,7},{7,6},{8,9},{9,8},{10,11... | collective-permute-start | bytes 3342344 | tf_op jit(solution)/shard_map/ppermute | solution.py:367
  9.2 4.9 %copy-start.12 = (s32[3]{0:T(128)}, s32[3]{0:T(128)S(1)}, u32[]{:S(2)}) copy-start(s32[3]{0:T(128)S(1)} %pad_add_fusion.place_ref) | copy-start | bytes 40
  9.2 0.7 %copy-start.9 = (bf16[16,512]{1,0:T(8,128)(2,1)S(1)}, bf16[16,512]{1,0:T(8,128)(2,1)}, u32[]{:S(2)}) copy-start(bf16[16,512]{1,0:T(8,128)(2,1)} %floor_ref.1) | copy-start | bytes 49156
  9.9 0.7 %copy-start.15 = (s32[512]{0:T(512)S(1)}, s32[512]{0:T(512)}, u32[]{:S(2)}) copy-start(s32[512]{0:T(512)} %param.15) | copy-start | bytes 6148
  10.6 0.7 %copy-start.16 = (f32[512]{0:T(512)S(1)}, f32[512]{0:T(512)}, u32[]{:S(2)}) copy-start(f32[512]{0:T(512)} %param.16) | copy-start | bytes 6148
  11.3 0.7 %copy-start.17 = (f32[512]{0:T(512)S(1)}, f32[512]{0:T(512)}, u32[]{:S(2)}) copy-start(f32[512]{0:T(512)} %param.17) | copy-start | bytes 6148
  14.0 0.7 %copy-start.1 = (f32[256,2]{1,0:T(8,128)}, f32[256,2]{1,0:T(8,128)S(1)}, u32[]{:S(2)}) copy-start(f32[256,2]{1,0:T(8,128)S(1)} %get-tuple-element.23.refs_5_.refs_9_) | copy-start | bytes 6148
  14.6 3.0 %copy-start.3 = (f32[64,1024]{1,0:T(8,128)}, f32[64,1024]{1,0:T(8,128)S(1)}, u32[]{:S(2)}) copy-start(f32[64,1024]{1,0:T(8,128)S(1)} %get-tuple-element.21.refs_3_) | copy-start | bytes 786436
  14.6 3.0 %copy-start.4 = (f32[64,1024]{1,0:T(8,128)}, f32[64,1024]{1,0:T(8,128)S(1)}, u32[]{:S(2)}) copy-start(f32[64,1024]{1,0:T(8,128)S(1)} %get-tuple-element.20.refs_2_) | copy-start | bytes 786436
  14.6 3.0 %copy-start.5 = (f32[64,1024]{1,0:T(8,128)}, f32[64,1024]{1,0:T(8,128)S(1)}, u32[]{:S(2)}) copy-start(f32[64,1024]{1,0:T(8,128)S(1)} %get-tuple-element.19.refs_1_) | copy-start | bytes 786436
  17.6 0.6 %copy-start.7 = (f32[16,1024]{1,0:T(8,128)}, f32[16,1024]{1,0:T(8,128)S(1)}, u32[]{:S(2)}) copy-start(f32[16,1024]{1,0:T(8,128)S(1)} %get-tuple-element.25.motion_ref) | copy-start | bytes 196612
  18.2 8.0 %collective-permute-start.4 = (f32[8,256]{1,0:T(8,128)}, f32[8,256]{1,0:T(8,128)}, u32[]{:S(2)}, u32[]{:S(2)}) collective-permute-start(f32[8,256]{1,0:T(8,128)} %get-tuple-element.26.ends_ref), channel_id=1, source_target_pairs={{0,2},{2,0},{1,3},{3,1},{4,6},{6,4},{5,7},{7,5},{8,10},{10,8},{9,1... | collective-permute-start | bytes 24584 | tf_op jit(solution)/shard_map/ppermute | solution.py:418
  20.7 8.7 %copy-start.13 = (s32[3]{0:T(128)S(1)}, s32[3]{0:T(128)}, u32[]{:S(2)}) copy-start(s32[3]{0:T(128)} %copy-done.12) | copy-start | bytes 40
  20.7 30.5 %collective-permute-start.1 = (f32[64,1024]{1,0:T(8,128)}, f32[64,1024]{1,0:T(8,128)S(1)}, u32[]{:S(2)}, u32[]{:S(2)}) collective-permute-start(f32[64,1024]{1,0:T(8,128)} %copy-done.5), channel_id=1, source_target_pairs={{0,4},{4,8},{8,12},{12,0},{1,5},{5,9},{9,13},{13,1},{2,6},{6,10},{... | collective-permute-start | bytes 786440 | tf_op jit(solution)/shard_map/ppermute | solution.py:372
  22.3 28.9 %collective-permute-start.2 = (f32[64,1024]{1,0:T(8,128)}, f32[64,1024]{1,0:T(8,128)S(1)}, u32[]{:S(2)}, u32[]{:S(2)}) collective-permute-start(f32[64,1024]{1,0:T(8,128)} %copy-done.4), channel_id=1, source_target_pairs={{0,8},{4,12},{8,0},{12,4},{1,9},{5,13},{9,1},{13,5},{2,10},{6,14},... | collective-permute-start | bytes 786440 | tf_op jit(solution)/shard_map/ppermute | solution.py:372
  24.9 26.3 %collective-permute-start.3 = (f32[64,1024]{1,0:T(8,128)}, f32[64,1024]{1,0:T(8,128)S(1)}, u32[]{:S(2)}, u32[]{:S(2)}) collective-permute-start(f32[64,1024]{1,0:T(8,128)} %copy-done.3), channel_id=1, source_target_pairs={{0,12},{4,0},{8,4},{12,8},{1,13},{5,1},{9,5},{13,9},{2,14},{6,2},{... | collective-permute-start | bytes 786440 | tf_op jit(solution)/shard_map/ppermute | solution.py:372
  26.2 0.8 %copy-start.8 = (f32[16,1024]{1,0:T(8,128)S(1)}, f32[16,1024]{1,0:T(8,128)}, u32[]{:S(2)}) copy-start(f32[16,1024]{1,0:T(8,128)} %copy-done.7) | copy-start | bytes 196612
  28.1 23.2 %copy-start.2 = (f32[256,2]{1,0:T(8,128)S(1)}, f32[256,2]{1,0:T(8,128)}, u32[]{:S(2)}) copy-start(f32[256,2]{1,0:T(8,128)} %copy-done.1) | copy-start | bytes 6148
  28.1 1.3 %collective-permute-start.5 = (f32[16,1024]{1,0:T(8,128)S(1)}, f32[16,1024]{1,0:T(8,128)S(1)}, u32[]{:S(2)}, u32[]{:S(2)}) collective-permute-start(f32[16,1024]{1,0:T(8,128)S(1)} %floor_motion_share.1.refs_0_), channel_id=1, source_target_pairs={{0,1},{1,0},{2,3},{3,2},{4,5},{5,4},{6,7},{7,6},{8,9},{9,8},{10,11... | collective-permute-start | bytes 196616 | tf_op jit(solution)/shard_map/ppermute | solution.py:367
  30.0 13.7 %collective-permute-start.6 = (f32[8,1024]{1,0:T(8,128)S(1)}, f32[8,1024]{1,0:T(8,128)S(1)}, u32[]{:S(2)}, u32[]{:S(2)}) collective-permute-start(f32[8,1024]{1,0:T(8,128)S(1)} %get-tuple-element.28), channel_id=1, source_target_pairs={{0,4},{4,8},{8,12},{12,0},{1,5},{5,9},{9,13},{13,1},{2,6},{6,10},{... | collective-permute-start | bytes 98312 | tf_op jit(solution)/shard_map/ppermute | solution.py:372
  30.7 19.6 %collective-permute-start.7 = (f32[8,1024]{1,0:T(8,128)S(1)}, f32[8,1024]{1,0:T(8,128)S(1)}, u32[]{:S(2)}, u32[]{:S(2)}) collective-permute-start(f32[8,1024]{1,0:T(8,128)S(1)} %get-tuple-element.29), channel_id=1, source_target_pairs={{0,8},{4,12},{8,0},{12,4},{1,9},{5,13},{9,1},{13,5},{2,10},{6,14},... | collective-permute-start | bytes 98312 | tf_op jit(solution)/shard_map/ppermute | solution.py:372
  43.7 7.5 %collective-permute-start.8 = (f32[8,1024]{1,0:T(8,128)S(1)}, f32[8,1024]{1,0:T(8,128)S(1)}, u32[]{:S(2)}, u32[]{:S(2)}) collective-permute-start(f32[8,1024]{1,0:T(8,128)S(1)} %get-tuple-element.30), channel_id=1, source_target_pairs={{0,12},{4,0},{8,4},{12,8},{1,13},{5,1},{9,5},{13,9},{2,14},{6,2},{... | collective-permute-start | bytes 98312 | tf_op jit(solution)/shard_map/ppermute | solution.py:372

commit v3 on v2

--- a/solution.py
+++ b/solution.py
@@ -11,7 +11,7 @@
 F32 = jnp.float32
 NN = (((1,), (0,)), ((), ()))
 NT = (((1,), (1,)), ((), ()))
-VMEM_LIMIT = 48 * 1024 * 1024
+VMEM_LIMIT = 16 * 1024 * 1024
 
 
 def dot(a, b, dims=NN):
@@ -37,59 +37,73 @@
     return pltpu.CompilerParams(vmem_limit_bytes=VMEM_LIMIT)
 
 
+def in_hbm(x):
+    return pltpu.with_memory_space_constraint(x, pltpu.HBM)
+
+
+def cost(us):
+    return pl.CostEstimate(flops=int(us * 5e8), bytes_accessed=int(us * 2e6), transcendentals=0)
+
+
 def whole(n):
     return [pl.BlockSpec(memory_space=pltpu.VMEM)] * n
 
 
-def tap_sums(pressures, tap_panel, tap_floor, tap_area, panels, floors):
+def tap_sums(pressures, tap_panel, tap_floor, tap_area, others, panels, floors):
     time, taps = pressures.shape
     rows = panels + floors
-    chunks = time // BLK
-
-    def body(press_hbm, panel_hbm, floor_hbm, area_hbm, sums_ref, press, panel, floor, area, weights, sems):
+    chunks = 2 if time % (2 * BLK) == 0 else 1
+    span = time // chunks
+    n = len(others)
+    given = (tap_panel, tap_floor, tap_area)
+
+    def body(press_hbm, *refs):
+        from_refs, sums_ref, kept = refs[: n + 3], refs[n + 3], refs[n + 4 : 2 * n + 4]
+        press, panel, floor, area, weights, sems = refs[2 * n + 4 :]
         small = [
-            pltpu.make_async_copy(panel_hbm, panel, sems.at[chunks]),
-            pltpu.make_async_copy(floor_hbm, floor, sems.at[chunks + 1]),
-            pltpu.make_async_copy(area_hbm, area, sems.at[chunks + 2]),
+            pltpu.make_async_copy(a, b, sems.at[chunks + i])
+            for i, (a, b) in enumerate(zip(from_refs, (panel, floor, area, *kept)))
         ]
-        for copy in small:
-            copy.start()
         large = []
         for i in range(chunks):
-            at = pl.ds(i * BLK, BLK)
+            at = pl.ds(i * span, span)
             large.append(pltpu.make_async_copy(press_hbm.at[at], press.at[at], sems.at[i]))
-            large[i].start()
-        for copy in small:
+        for copy in [*small[:3], *large, *small[3:]]:
+            copy.start()
+        for copy in small[:3]:
             copy.wait()
-        each = area[...].astype(F32).reshape(1, taps)
-        ids = lax.broadcasted_iota(jnp.int32, (panels, taps), 0)
-        weights[:panels] = jnp.where(ids == panel[...], each, 0.0).astype(BF)
-        ids = lax.broadcasted_iota(jnp.int32, (floors, taps), 0)
-        weights[panels:] = jnp.where(ids == floor[...], each, 0.0).astype(BF)
+        each = jnp.broadcast_to(area[...].astype(F32).reshape(1, taps), (16, taps))
+        row = lax.broadcasted_iota(jnp.int32, (16, taps), 0)
+        for ids, first, count in ((panel, 0, panels), (floor, panels, floors)):
+            at = jnp.broadcast_to(ids[...], (16, taps)) - row
+            for r in range(0, count, 16):
+                weights[first + r : first + r + 16] = jnp.where(at == r, each, 0.0).astype(BF)
         for i in range(chunks):
-            at = slice(i * BLK, (i + 1) * BLK)
+            at = slice(i * span, (i + 1) * span)
             large[i].wait()
             sums_ref[:, at] = dot(weights[...], press[at], NT)
-
-    return pl.pallas_call(
-        body,
-        in_specs=[pl.BlockSpec(memory_space=pltpu.HBM)] * 4,
-        out_specs=pl.BlockSpec(memory_space=pltpu.VMEM),
-        out_shape=jax.ShapeDtypeStruct((rows, time), F32),
+        for copy in small[3:]:
+            copy.wait()
+
+    out = pl.pallas_call(
+        body,
+        in_specs=[pl.BlockSpec(memory_space=pltpu.HBM)] * (n + 4),
+        out_specs=tuple(whole(n + 1)),
+        out_shape=(jax.ShapeDtypeStruct((rows, time), F32), *(jax.ShapeDtypeStruct(x.shape, x.dtype) for x in others)),
         scratch_shapes=[
             pltpu.VMEM((time, taps), BF),
-            pltpu.VMEM((1, taps), jnp.int32),
-            pltpu.VMEM((1, taps), jnp.int32),
-            pltpu.VMEM(tap_area.shape, BF),
+            *(pltpu.VMEM(x.shape, x.dtype) for x in given),
             pltpu.VMEM((rows, taps), BF),
-            pltpu.SemaphoreType.DMA((chunks + 3,)),
+            pltpu.SemaphoreType.DMA((chunks + n + 3,)),
         ],
         compiler_params=params(),
+        cost_estimate=cost(3),
         name="tap_sums",
-    )(pressures, tap_panel[None], tap_floor[None], tap_area)
-
-
-def mode_tables(place, order, decay, freq, panel_shape, floor_shape, nz, nc):
+    )(in_hbm(pressures), *(in_hbm(x) for x in given), *(in_hbm(x) for x in others))
+    return out[0], out[1:]
+
+
+def mode_tables(order, decay, freq, panel_shape, floor_shape, nz, nc):
     modes = order.shape[1]
     panels = panel_shape.shape[0]
     floors = floor_shape.shape[0]
@@ -98,9 +112,11 @@
     bits = BLK.bit_length() - 1
     half = BLK // 2
 
-    def body(place_ref, order_ref, decay_ref, freq_ref, panel_ref, floor_ref, pt_ref, fs_ref, tab_ref, turn_ref, column_ref):
+    def body(*refs):
+        order_ref, decay_ref, freq_ref, panel_ref, floor_ref = refs[:5]
+        pt_ref, fs_ref, tab_ref, turn_ref, own_ref, column_ref = refs[5:]
         column_ref[...] = jnp.broadcast_to(order_ref[...].astype(F32), (TILE, modes)).T
-        z, c = place_ref[0], place_ref[1]
+        z, c = lax.axis_index("taps"), lax.axis_index("floors")
         picked = []
         for d in range(nz):
             owner = lax.rem(z + d, nz) * nc + c
@@ -148,21 +164,24 @@
         tab_ref[3, :, near], tab_ref[3, :, far] = shrink * sin, far_shrink * far_sin
         fade = jnp.exp(-rate * float(BLK))
         turn_ref[...] = fade * cols[:, at + 2 : at + 4]
+        own_ref[...] = tab_ref[:, :mode_dev]
 
     return pl.pallas_call(
         body,
-        in_specs=[pl.BlockSpec(memory_space=pltpu.SMEM)] + whole(5),
-        out_specs=tuple(whole(4)),
+        in_specs=whole(5),
+        out_specs=tuple(whole(5)),
         out_shape=(
             jax.ShapeDtypeStruct((slots, panels), BF),
             jax.ShapeDtypeStruct((floors, slots), F32),
             jax.ShapeDtypeStruct((4, slots, BLK), F32),
             jax.ShapeDtypeStruct((slots, 2), F32),
+            jax.ShapeDtypeStruct((4, mode_dev, BLK), F32),
         ),
         scratch_shapes=[pltpu.VMEM((modes, TILE), F32)],
         compiler_params=params(),
+        cost_estimate=cost(2),
         name="mode_tables",
-    )(place, order, decay, freq, panel_shape, floor_shape)
+    )(order, decay, freq, panel_shape, floor_shape)
 
 
 def slot_forces(sums, pt, nz):
@@ -172,8 +191,12 @@
     mode_dev = slots // nz
 
     def body(*refs):
-        sum_refs, pt_ref, out_refs = refs[:nc], refs[nc], refs[nc + 1 :]
+        sum_refs, pt_ref, out_refs, load_ref = refs[:nc], refs[nc], refs[nc + 1 : -1], refs[-1]
         left = pt_ref[...]
+        load = sum_refs[0][panels:]
+        for ref in sum_refs[1:]:
+            load = load + ref[panels:]
+        load_ref[...] = load
         for b in range(time // BLK):
             cols = slice(b * BLK, (b + 1) * BLK)
             total = sum_refs[0][:panels, cols]
@@ -183,14 +206,17 @@
             for d in range(nz):
                 out_refs[d][:, cols] = forces[d * mode_dev : (d + 1) * mode_dev]
 
-    return pl.pallas_call(
+    out = pl.pallas_call(
         body,
         in_specs=whole(nc + 1),
-        out_specs=whole(nz),
-        out_shape=[jax.ShapeDtypeStruct((mode_dev, time), F32)] * nz,
-        compiler_params=params(),
+        out_specs=whole(nz + 1),
+        out_shape=[jax.ShapeDtypeStruct((mode_dev, time), F32)] * nz
+        + [jax.ShapeDtypeStruct((sums[0].shape[0] - panels, time), F32)],
+        compiler_params=params(),
+        cost_estimate=cost(1),
         name="slot_forces",
     )(*sums, pt)
+    return out[:nz], out[nz]
 
 
 def triangle():
@@ -244,18 +270,25 @@
         ),
         scratch_shapes=[pltpu.VMEM((slots, time), F32)],
         compiler_params=params(),
+        cost_estimate=cost(3),
         name="partial_states",
     )(*forces, tables, turns, floor_slots)
 
 
-def floor_motion_share(motion, ends, enter, tables, floor_slots):
+def floor_shares(motion, ends, enter, tables, floor_slots, forces):
     floors, time = motion.shape
     blocks = time // BLK
 
-    def body(motion_ref, ends_ref, enter_ref, tab_ref, fs_ref, out_ref):
+    def body(motion_ref, ends_ref, enter_ref, tab_ref, fs_ref, *refs):
+        force_refs, out_ref, force_ref = refs[:-2], refs[-2], refs[-1]
+        force = force_refs[0][...]
+        for ref in force_refs[1:]:
+            force = force + ref[...]
+        force_ref[...] = force
         shape = fs_ref[...]
         turn = (ends_ref[2:3, :], ends_ref[3:4, :])
-        state = (enter_ref[0:1, :], enter_ref[1:2, :])
+        later = lax.axis_index("tm") > 0
+        state = tuple(jnp.where(later, enter_ref[i : i + 1, :], 0.0) for i in (0, 1))
         left_re, left_im = [], []
         for b in range(blocks):
             left_re.append(shape * state[0])
@@ -273,33 +306,33 @@
 
     return pl.pallas_call(
         body,
-        in_specs=whole(5),
-        out_specs=whole(1)[0],
-        out_shape=jax.ShapeDtypeStruct((floors, time), F32),
-        compiler_params=params(),
-        name="floor_motion_share",
-    )(motion, ends, enter, tables, floor_slots)
-
-
-def owner_shares(place, motions, sums, enter, nz, floor_dev, mode_dev):
-    nc = len(sums)
+        in_specs=whole(5 + len(forces)),
+        out_specs=tuple(whole(2)),
+        out_shape=(jax.ShapeDtypeStruct((floors, time), F32), jax.ShapeDtypeStruct(forces[0].shape, F32)),
+        compiler_params=params(),
+        cost_estimate=cost(1),
+        name="floor_shares",
+    )(motion, ends, enter, tables, floor_slots, *forces)
+
+
+def owner_shares(motions, load, enter, nz, floor_dev, mode_dev):
+    nc = len(motions)
     floors, time = motions[0].shape
     rows = -(-(2 * floor_dev + 2) // 8) * 8
-    load_at = sums[0].shape[0] - floors
     owners = nz * nc
 
-    def body(place_ref, *refs):
-        motion_refs, sum_refs, enter_ref = refs[:nc], refs[nc : 2 * nc], refs[2 * nc]
-        out_refs, motion_all, load_all = refs[2 * nc + 1 : 2 * nc + 1 + nz], refs[-2], refs[-1]
-        z, c = place_ref[0], place_ref[1]
+    def body(*refs):
+        motion_refs, load_ref, enter_ref = refs[:nc], refs[nc], refs[nc + 1]
+        out_refs, motion_all, load_all = refs[nc + 2 : nc + 2 + nz], refs[-2], refs[-1]
+        z, c = lax.axis_index("taps"), lax.axis_index("floors")
+        later = lax.axis_index("tm") > 0
         motion = motion_refs[0][...]
-        load = sum_refs[0][load_at:]
-        for i in range(1, nc):
-            motion = motion + motion_refs[i][...]
-            load = load + sum_refs[i][load_at:]
+        for ref in motion_refs[1:]:
+            motion = motion + ref[...]
         for o in range(owners):
-            motion_all[o] = motion[o * floor_dev : (o + 1) * floor_dev]
-            load_all[o] = load[o * floor_dev : (o + 1) * floor_dev]
+            at = slice(o * floor_dev, (o + 1) * floor_dev)
+            motion_all[o] = motion[at]
+            load_all[o] = load_ref[at]
         for d in range(nz):
             owner = lax.rem(z + d, nz) * nc + c
             out = out_refs[d]
@@ -307,33 +340,34 @@
             out[:floor_dev] = motion_all[owner]
             out[floor_dev : 2 * floor_dev] = load_all[owner]
             at = slice(d * mode_dev, (d + 1) * mode_dev)
-            out[2 * floor_dev : 2 * floor_dev + 2, :mode_dev] = enter_ref[0:2, at]
+            out[2 * floor_dev : 2 * floor_dev + 2, :mode_dev] = jnp.where(later, enter_ref[0:2, at], 0.0)
 
     return pl.pallas_call(
         body,
-        in_specs=[pl.BlockSpec(memory_space=pltpu.SMEM)] + whole(2 * nc + 1),
+        in_specs=whole(nc + 2),
         out_specs=whole(nz),
         out_shape=[jax.ShapeDtypeStruct((rows, time), F32)] * nz,
         scratch_shapes=[pltpu.VMEM((owners, floor_dev, time), F32)] * 2,
         compiler_params=params(),
+        cost_estimate=cost(1),
         name="owner_shares",
-    )(place, *motions, *sums, enter)
+    )(*motions, load, enter)
 
 
 def own_response(forces, shares, tables, turns, floor_dev, load_scale):
     mode_dev, time = forces[0].shape
-    n = len(forces)
+    n, m = len(forces), len(shares)
     blocks = time // BLK
 
     def body(*refs):
-        force_refs, share_refs = refs[:n], refs[n : 2 * n]
-        tab_ref, turn_ref, resp_ref, motion_ref, load_ref = refs[2 * n :]
+        force_refs, share_refs = refs[:n], refs[n : n + m]
+        tab_ref, turn_ref, resp_ref, motion_ref, load_ref = refs[n + m :]
         share = share_refs[0][...]
         for ref in share_refs[1:]:
             share = share + ref[...]
         motion_ref[...] = share[:floor_dev]
         load_ref[...] = share[floor_dev : 2 * floor_dev] * load_scale
-        pr, pi, qr, qi = (tab_ref[i, :mode_dev] for i in range(4))
+        pr, pi, qr, qi = (tab_ref[i] for i in range(4))
         turn = turn_ref[:mode_dev, 0:1], turn_ref[:mode_dev, 1:2]
         column = share[:, :TILE].T
         at = 2 * floor_dev
@@ -351,7 +385,7 @@
 
     return pl.pallas_call(
         body,
-        in_specs=whole(2 * n + 2),
+        in_specs=whole(n + m + 2),
         out_specs=tuple(whole(3)),
         out_shape=(
             jax.ShapeDtypeStruct((mode_dev, time), F32),
@@ -359,6 +393,7 @@
             jax.ShapeDtypeStruct((floor_dev, time), F32),
         ),
         compiler_params=params(),
+        cost_estimate=cost(2),
         name="own_response",
     )(*forces, *shares, tables, turns)
 
@@ -395,15 +430,19 @@
     floors = floor_shape.shape[0]
     floor_dev = floors // owners
     load_scale = (floors / (taps * owners)) ** 0.5
-    z, c = lax.axis_index("taps"), lax.axis_index("floors")
-    place = jnp.stack([z, c, z * nc + c]).astype(jnp.int32)
-
-    mine = tap_sums(pressures, tap_panel, tap_floor, tap_area, panels, floors)
+
+    mine, kept = tap_sums(
+        pressures,
+        tap_panel[None],
+        tap_floor[None],
+        tap_area,
+        (mode_order[None], mode_decay[None], mode_freq[None], panel_shape, floor_shape),
+        panels,
+        floors,
+    )
     sums = [mine] + shifts(mine, "floors", nc)
-    pt, floor_slots, tables, turns = mode_tables(
-        place, mode_order[None], mode_decay[None], mode_freq[None], panel_shape, floor_shape, nz, nc
-    )
-    forces = slot_forces(sums, pt, nz)
+    pt, floor_slots, tables, turns, own = mode_tables(*kept, nz, nc)
+    forces, load = slot_forces(sums, pt, nz)
     got_forces = along(forces, nz)
     motion, ends = partial_states(forces, tables, turns, floor_slots)
     enter = jnp.zeros_like(ends)
@@ -414,14 +453,19 @@
             over = turn
             for _ in range(time // BLK - 1):
                 over = turned(over, turn)
-            passed = ends + jnp.concatenate([*turned(over, (enter[0:1], enter[1:2])), jnp.zeros_like(ends[2:])])
+            enter = jnp.where(lax.axis_index("tm") > 0, enter, 0.0)
+            passed = ends + jnp.concatenate(
+                [*turned(over, (enter[0:1], enter[1:2])), jnp.zeros_like(ends[2:])]
+            )
         enter = lax.ppermute(passed, "tm", [(i, (i + 1) % nt) for i in range(nt)])
         enter = jnp.where(lax.axis_index("tm") > 0, enter, 0.0)
-    motion = floor_motion_share(motion, ends, enter, tables, floor_slots)
+    early = [x for d, x in enumerate(got_forces) if d != nz // 2]
+    motion, force = floor_shares(motion, ends, enter, tables, floor_slots, early)
+    got_forces = [force, got_forces[nz // 2]]
     motions = [motion] + shifts(motion, "floors", nc)
-    shares = owner_shares(place, motions, sums, enter, nz, floor_dev, mode_dev)
+    shares = owner_shares(motions, load, enter, nz, floor_dev, mode_dev)
     return own_response(
-        got_forces, along(shares, nz), tables, turns, floor_dev, load_scale
+        got_forces, along(shares, nz), own, turns, floor_dev, load_scale
     )
 
 

time: 53.3 us -> 39.9 us (0.75)
  waiting for transfers between devices: 21.3 us -> 11.1 us
  local copies, waits for them, and re-layouts: 8.6 us -> 0 us
  starting transfers between devices: 9.77 us -> 18.2 us
  Pallas kernels: 12.3 us -> 9.67 us
    ppermute x6, waiting for transfers between devices: 20.1 us -> 7.83 us  [along(): lax.ppermute(parts[d], 'taps', [(i, (i + d) % n) for i in range(n)])]
    ppermute x6, starting transfers between devices: 6.68 us -> 15.9 us  [along(): lax.ppermute(parts[d], 'taps', [(i, (i + d) % n) for i in range(n)])]
    unnamed x36 -> x0, local copies, waits for them, and re-layouts: 8.6 us -> none
    pallas_call x6, Pallas kernels: 9.45 us -> 7.39 us  [the longest x1 3.29 us: tap_sums(): pl.pallas_call(body, in_specs=[pl.BlockSpec(memory_space=pltpu.HBM)] * (n...]
    ppermute x1, waiting for transfers between devices: 0.01 us -> 1.22 us  [on_device(): enter = lax.ppermute(passed, 'tm', [(i, (i + 1) % nt) for i in range(nt)])]
    ppermute x1, starting transfers between devices: 2.51 us -> 1.68 us  [on_device(): enter = lax.ppermute(passed, 'tm', [(i, (i + 1) % nt) for i in range(nt)])]
    ppermute x2, waiting for transfers between devices: 1.24 us -> 2.05 us  [shifts(): lax.ppermute(x, axis, [(i, (i + d) % n) for i in range(n)])]
    pallas_call x1, Pallas kernels: 2.87 us -> 2.28 us  [partial_states(): pl.pallas_call(body, in_specs=whole(nz + 3), out_specs=tuple(whole(2)), o...]
  transfers between devices with their start and end apart: 9 -> 9, of which waited for: 4 -> 7; matrix products, arithmetic and copies ran while one was open for 0% -> 0% of each run, Pallas kernels for 7% -> 11%
where the time goes in v3:
time: 39.9 us; the launch traced here: 39.7 us
  starting transfers between devices  18.2 us (46%)
  waiting for transfers between devices  11.1 us (28%)
  Pallas kernels  9.67 us (24%)
  between operations  0.67 us (2%)
    ppermute x6, starting transfers between devices, along(): lax.ppermute(parts[d], 'taps', [(i, (i + d) % n) for i in range(n)])  15.9 us
    ppermute x6, waiting for transfers between devices, along(): lax.ppermute(parts[d], 'taps', [(i, (i + d) % n) for i in range(n)])  7.83 us
    pallas_call x1, Pallas kernels, tap_sums(): pl.pallas_call(body, in_specs=[pl.BlockSpec(memory_space=pltpu.HBM)] * (n...  3.29 us
    pallas_call x1, Pallas kernels, partial_states(): pl.pallas_call(body, in_specs=whole(nz + 3), out_specs=tuple(whole(2)), o...  2.28 us
    ppermute x2, waiting for transfers between devices, shifts(): lax.ppermute(x, axis, [(i, (i + d) % n) for i in range(n)])  2.05 us
    ppermute x1, starting transfers between devices, on_device(): enter = lax.ppermute(passed, 'tm', [(i, (i + 1) % nt) for i in range(nt)])  1.68 us
    pallas_call x1, Pallas kernels, own_response(): pl.pallas_call(body, in_specs=whole(n + m + 2), out_specs=tuple(whole(3))...  1.63 us
    pallas_call x1, Pallas kernels, mode_tables(): pl.pallas_call(body, in_specs=whole(5), out_specs=tuple(whole(5)), out_sh...  1.57 us
  transfers between devices with their start and end apart: 9, of which 7 were waited for; matrix products, arithmetic and copies ran while one was open for 0% of the time, Pallas kernels for 11%

profile of v3, /device:TPU:0, one launch (start us, length us, event | category | flops | bytes accessed | tf_op | source)
XLA Modules:
  0.0 39.7 jit_solution(10220674827831713820)
XLA Ops:
  0.6 3.3 %tap_sums.1 = (f32[272,1024]{1,0:T(8,128)S(1)}, s32[1,512]{1,0:T(1,128)S(1)}, f32[1,512]{1,0:T(1,128)S(1)}, f32[1,512]{1,0:T(1,128)S(1)}, bf16[256,512]{1,0:T(8,128)(2,1)S(1)}, /*index=5*/bf16[16,512]{1,0:T(8,128)(2,1)S(1)}) custom-call(bf16[1024,2048]{1,0:T(8,128)(2,1)} %press_hbm.1, s32[1,2048]{1,0:T(1,128)} %bitcast.5, s32[1,2048]{1,0:T(1,128)} %bitcast.6, ...), custom_call_target="tpu_custom_call" | custom-call | flops 1500000000 | bytes 6000000 | tf_op jit(solution)/shard_map/tap_sums/pallas_call | solution.py:88
  3.9 0.5 %collective-permute-start = (f32[272,1024]{1,0:T(8,128)S(1)}, f32[272,1024]{1,0:T(8,128)S(1)}, u32[]{:S(2)}, u32[]{:S(2)}) collective-permute-start(f32[272,1024]{1,0:T(8,128)S(1)} %get-tuple-element.27.refs_0_), channel_id=1, source_target_pairs={{0,1},{1,0},{2,3},{3,2},{4,5},{5,4},{6,7},{7,6},{8,9},{9,8},{10,11... | collective-permute-start | bytes 3342344 | tf_op jit(solution)/shard_map/ppermute | solution.py:402
  4.4 1.6 %mode_tables.1 = (bf16[256,256]{1,0:T(8,128)(2,1)S(1)}, f32[16,256]{1,0:T(8,128)S(1)}, f32[4,256,256]{2,1,0:T(8,128)S(1)}, f32[256,2]{1,0:T(8,128)S(1)}, f32[4,64,256]{2,1,0:T(8,128)S(1)}) custom-call(s32[1,512]{1,0:T(1,128)S(1)} %get-tuple-element.28.refs_0_, f32[1,512]{1,0:T(1,128)S(1)} %get-tuple-element.29.refs_1_, ...), custom_call_target="tpu_custom_call" | custom-call | flops 1000000000 | bytes 4000000 | tf_op jit(solution)/shard_map/mode_tables/pallas_call | solution.py:169
  6.0 0.8 %collective-permute-done.refs_1_ = f32[272,1024]{1,0:T(8,128)S(1)} collective-permute-done((f32[272,1024]{1,0:T(8,128)S(1)}, f32[272,1024]{1,0:T(8,128)S(1)}, u32[]{:S(2)}, u32[]{:S(2)}) %collective-permute-start) | collective-permute-done | bytes 1114144 | tf_op jit(solution)/shard_map/ppermute | solution.py:402
  6.8 0.5 %slot_forces.1 = (f32[64,1024]{1,0:T(8,128)S(1)}, f32[64,1024]{1,0:T(8,128)S(1)}, f32[64,1024]{1,0:T(8,128)S(1)}, f32[64,1024]{1,0:T(8,128)S(1)}, f32[16,1024]{1,0:T(8,128)S(1)}) custom-call(f32[272,1024]{1,0:T(8,128)S(1)} %get-tuple-element.27.refs_0_, f32[272,1024]{1,0:T(8,128)S(1)} %collective-permute-done.refs_1_, ...), custom_call_target="tpu_custom_call" | custom-call | flops 500000000 | bytes 2000000 | tf_op jit(solution)/shard_map/slot_forces/pallas_call | solution.py:209
  7.3 3.0 %collective-permute-start.2 = (f32[64,1024]{1,0:T(8,128)S(1)}, f32[64,1024]{1,0:T(8,128)S(1)}, u32[]{:S(2)}, u32[]{:S(2)}) collective-permute-start(f32[64,1024]{1,0:T(8,128)S(1)} %get-tuple-element.35.refs_1_), channel_id=1, source_target_pairs={{0,4},{4,8},{8,12},{12,0},{1,5},{5,9},{9,13},{13,1},{2,6},{6,10},{... | collective-permute-start | bytes 786440 | tf_op jit(solution)/shard_map/ppermute | solution.py:407
  10.3 2.1 %collective-permute-start.3 = (f32[64,1024]{1,0:T(8,128)S(1)}, f32[64,1024]{1,0:T(8,128)S(1)}, u32[]{:S(2)}, u32[]{:S(2)}) collective-permute-start(f32[64,1024]{1,0:T(8,128)S(1)} %get-tuple-element.37.refs_3_), channel_id=1, source_target_pairs={{0,12},{4,0},{8,4},{12,8},{1,13},{5,1},{9,5},{13,9},{2,14},{6,2},{... | collective-permute-start | bytes 786440 | tf_op jit(solution)/shard_map/ppermute | solution.py:407
  12.4 2.3 %partial_states.1 = (f32[16,1024]{1,0:T(8,128)S(1)}, f32[8,256]{1,0:T(8,128)S(1)}) custom-call(f32[64,1024]{1,0:T(8,128)S(1)} %get-tuple-element.34.refs_0_, f32[64,1024]{1,0:T(8,128)S(1)} %get-tuple-element.35.refs_1_, f32[64,1024]{1,0:T(8,128)S(1)} %get-tuple-element.36.refs_2_, f32[64,1024]{1,0:T(8,128)S(1)} %get-tuple-element.37.refs_3_, ...), custom_call_target="tpu_custom_call" | custom-call | flops 1500000000 | bytes 6000000 | tf_op jit(solution)/shard_map/partial_states/pallas_call | solution.py:263
  14.7 1.7 %collective-permute-start.1 = (f32[8,256]{1,0:T(8,128)S(1)}, f32[8,256]{1,0:T(8,128)S(1)}, u32[]{:S(2)}, u32[]{:S(2)}) collective-permute-start(f32[8,256]{1,0:T(8,128)S(1)} %get-tuple-element.42.ends_ref), channel_id=1, source_target_pairs={{0,2},{2,0},{1,3},{3,1},{4,6},{6,4},{5,7},{7,5},{8,10},{10,8},{9,1... | collective-permute-start | bytes 24584 | tf_op jit(solution)/shard_map/ppermute | solution.py:460
  16.4 0.8 %collective-permute-start.4 = (f32[64,1024]{1,0:T(8,128)S(1)}, f32[64,1024]{1,0:T(8,128)S(1)}, u32[]{:S(2)}, u32[]{:S(2)}) collective-permute-start(f32[64,1024]{1,0:T(8,128)S(1)} %get-tuple-element.36.refs_2_), channel_id=1, source_target_pairs={{0,8},{4,12},{8,0},{12,4},{1,9},{5,13},{9,1},{13,5},{2,10},{6,14},... | collective-permute-start | bytes 786440 | tf_op jit(solution)/shard_map/ppermute | solution.py:407
  17.2 1.2 %collective-permute-done.1 = f32[8,256]{1,0:T(8,128)S(1)} collective-permute-done((f32[8,256]{1,0:T(8,128)S(1)}, f32[8,256]{1,0:T(8,128)S(1)}, u32[]{:S(2)}, u32[]{:S(2)}) %collective-permute-start.1) | collective-permute-done | bytes 8224 | tf_op jit(solution)/shard_map/ppermute | solution.py:460
  18.4 1.1 %collective-permute-done.2.refs_1_ = f32[64,1024]{1,0:T(8,128)S(1)} collective-permute-done((f32[64,1024]{1,0:T(8,128)S(1)}, f32[64,1024]{1,0:T(8,128)S(1)}, u32[]{:S(2)}, u32[]{:S(2)}) %collective-permute-start.2) | collective-permute-done | bytes 262176 | tf_op jit(solution)/shard_map/ppermute | solution.py:407
  19.5 4.5 %collective-permute-done.3.refs_2_ = f32[64,1024]{1,0:T(8,128)S(1)} collective-permute-done((f32[64,1024]{1,0:T(8,128)S(1)}, f32[64,1024]{1,0:T(8,128)S(1)}, u32[]{:S(2)}, u32[]{:S(2)}) %collective-permute-start.3) | collective-permute-done | bytes 262176 | tf_op jit(solution)/shard_map/ppermute | solution.py:407
  24.0 0.3 floor_shares.1
  24.3 0.1 collective-permute-start.5
  24.4 1.2 %collective-permute-done.5.refs_1_ = f32[16,1024]{1,0:T(8,128)S(1)} collective-permute-done((f32[16,1024]{1,0:T(8,128)S(1)}, f32[16,1024]{1,0:T(8,128)S(1)}, u32[]{:S(2)}, u32[]{:S(2)}) %collective-permute-start.5) | collective-permute-done | bytes 65568 | tf_op jit(solution)/shard_map/ppermute | solution.py:402
  25.7 0.1 owner_shares.1
  25.7 1.7 %collective-permute-start.6 = (f32[8,1024]{1,0:T(8,128)S(1)}, f32[8,1024]{1,0:T(8,128)S(1)}, u32[]{:S(2)}, u32[]{:S(2)}) collective-permute-start(f32[8,1024]{1,0:T(8,128)S(1)} %get-tuple-element.47), channel_id=1, source_target_pairs={{0,4},{4,8},{8,12},{12,0},{1,5},{5,9},{9,13},{13,1},{2,6},{6,10},{... | collective-permute-start | bytes 98312 | tf_op jit(solution)/shard_map/ppermute | solution.py:407
  27.5 5.5 %collective-permute-start.7 = (f32[8,1024]{1,0:T(8,128)S(1)}, f32[8,1024]{1,0:T(8,128)S(1)}, u32[]{:S(2)}, u32[]{:S(2)}) collective-permute-start(f32[8,1024]{1,0:T(8,128)S(1)} %get-tuple-element.48), channel_id=1, source_target_pairs={{0,8},{4,12},{8,0},{12,4},{1,9},{5,13},{9,1},{13,5},{2,10},{6,14},... | collective-permute-start | bytes 98312 | tf_op jit(solution)/shard_map/ppermute | solution.py:407
  33.0 2.8 %collective-permute-start.8 = (f32[8,1024]{1,0:T(8,128)S(1)}, f32[8,1024]{1,0:T(8,128)S(1)}, u32[]{:S(2)}, u32[]{:S(2)}) collective-permute-start(f32[8,1024]{1,0:T(8,128)S(1)} %get-tuple-element.49), channel_id=1, source_target_pairs={{0,12},{4,0},{8,4},{12,8},{1,13},{5,1},{9,5},{13,9},{2,14},{6,2},{... | collective-permute-start | bytes 98312 | tf_op jit(solution)/shard_map/ppermute | solution.py:407
  35.8 1.2 %collective-permute-done.4.refs_1_ = f32[64,1024]{1,0:T(8,128)S(1)} collective-permute-done((f32[64,1024]{1,0:T(8,128)S(1)}, f32[64,1024]{1,0:T(8,128)S(1)}, u32[]{:S(2)}, u32[]{:S(2)}) %collective-permute-start.4) | collective-permute-done | bytes 262176 | tf_op jit(solution)/shard_map/ppermute | solution.py:407
  37.0 0.0 collective-permute-done.6.refs_3_
  37.0 1.0 %collective-permute-done.7.refs_4_ = f32[8,1024]{1,0:T(8,128)S(1)} collective-permute-done((f32[8,1024]{1,0:T(8,128)S(1)}, f32[8,1024]{1,0:T(8,128)S(1)}, u32[]{:S(2)}, u32[]{:S(2)}) %collective-permute-start.7) | collective-permute-done | bytes 32800 | tf_op jit(solution)/shard_map/ppermute | solution.py:407
  38.0 0.0 collective-permute-done.8.refs_5_
  38.0 1.6 %own_response.1 = (f32[64,1024]{1,0:T(8,128)}, f32[2,1024]{1,0:T(2,128)}, f32[2,1024]{1,0:T(2,128)}) custom-call(f32[64,1024]{1,0:T(8,128)S(1)} %get-tuple-element.43.refs_0_, f32[64,1024]{1,0:T(8,128)S(1)} %collective-permute-done.4.refs_1_, f32[8,1024]{1,0:T(8,128)S(1)} %get-tuple-element.46.refs_2_, f32[8,1024]{1,0:T(8,128)S(1)} %collective-permute-done.6.refs_3_, ...), custom_call_target="tpu_custom_call" | custom-call | flops 1000000000 | bytes 4000000 | tf_op jit(solution)/shard_map/own_response/pallas_call | solution.py:386
  (1 shorter events, 0.0 us)
Async XLA Ops:
  3.9 2.9 %collective-permute-start = (f32[272,1024]{1,0:T(8,128)S(1)}, f32[272,1024]{1,0:T(8,128)S(1)}, u32[]{:S(2)}, u32[]{:S(2)}) collective-permute-start(f32[272,1024]{1,0:T(8,128)S(1)} %get-tuple-element.27.refs_0_), channel_id=1, source_target_pairs={{0,1},{1,0},{2,3},{3,2},{4,5},{5,4},{6,7},{7,6},{8,9},{9,8},{10,11... | collective-permute-start | bytes 3342344 | tf_op jit(solution)/shard_map/ppermute | solution.py:402
  7.3 12.2 %collective-permute-start.2 = (f32[64,1024]{1,0:T(8,128)S(1)}, f32[64,1024]{1,0:T(8,128)S(1)}, u32[]{:S(2)}, u32[]{:S(2)}) collective-permute-start(f32[64,1024]{1,0:T(8,128)S(1)} %get-tuple-element.35.refs_1_), channel_id=1, source_target_pairs={{0,4},{4,8},{8,12},{12,0},{1,5},{5,9},{9,13},{13,1},{2,6},{6,10},{... | collective-permute-start | bytes 786440 | tf_op jit(solution)/shard_map/ppermute | solution.py:407
  10.3 13.7 %collective-permute-start.3 = (f32[64,1024]{1,0:T(8,128)S(1)}, f32[64,1024]{1,0:T(8,128)S(1)}, u32[]{:S(2)}, u32[]{:S(2)}) collective-permute-start(f32[64,1024]{1,0:T(8,128)S(1)} %get-tuple-element.37.refs_3_), channel_id=1, source_target_pairs={{0,12},{4,0},{8,4},{12,8},{1,13},{5,1},{9,5},{13,9},{2,14},{6,2},{... | collective-permute-start | bytes 786440 | tf_op jit(solution)/shard_map/ppermute | solution.py:407
  14.7 3.7 %collective-permute-start.1 = (f32[8,256]{1,0:T(8,128)S(1)}, f32[8,256]{1,0:T(8,128)S(1)}, u32[]{:S(2)}, u32[]{:S(2)}) collective-permute-start(f32[8,256]{1,0:T(8,128)S(1)} %get-tuple-element.42.ends_ref), channel_id=1, source_target_pairs={{0,2},{2,0},{1,3},{3,1},{4,6},{6,4},{5,7},{7,5},{8,10},{10,8},{9,1... | collective-permute-start | bytes 24584 | tf_op jit(solution)/shard_map/ppermute | solution.py:460
  16.4 20.6 %collective-permute-start.4 = (f32[64,1024]{1,0:T(8,128)S(1)}, f32[64,1024]{1,0:T(8,128)S(1)}, u32[]{:S(2)}, u32[]{:S(2)}) collective-permute-start(f32[64,1024]{1,0:T(8,128)S(1)} %get-tuple-element.36.refs_2_), channel_id=1, source_target_pairs={{0,8},{4,12},{8,0},{12,4},{1,9},{5,13},{9,1},{13,5},{2,10},{6,14},... | collective-permute-start | bytes 786440 | tf_op jit(solution)/shard_map/ppermute | solution.py:407
  24.3 1.3 %collective-permute-start.5 = (f32[16,1024]{1,0:T(8,128)S(1)}, f32[16,1024]{1,0:T(8,128)S(1)}, u32[]{:S(2)}, u32[]{:S(2)}) collective-permute-start(f32[16,1024]{1,0:T(8,128)S(1)} %get-tuple-element.44.refs_0_), channel_id=1, source_target_pairs={{0,1},{1,0},{2,3},{3,2},{4,5},{5,4},{6,7},{7,6},{8,9},{9,8},{10,11... | collective-permute-start | bytes 196616 | tf_op jit(solution)/shard_map/ppermute | solution.py:402
  25.7 11.3 %collective-permute-start.6 = (f32[8,1024]{1,0:T(8,128)S(1)}, f32[8,1024]{1,0:T(8,128)S(1)}, u32[]{:S(2)}, u32[]{:S(2)}) collective-permute-start(f32[8,1024]{1,0:T(8,128)S(1)} %get-tuple-element.47), channel_id=1, source_target_pairs={{0,4},{4,8},{8,12},{12,0},{1,5},{5,9},{9,13},{13,1},{2,6},{6,10},{... | collective-permute-start | bytes 98312 | tf_op jit(solution)/shard_map/ppermute | solution.py:407
  27.5 10.5 %collective-permute-start.7 = (f32[8,1024]{1,0:T(8,128)S(1)}, f32[8,1024]{1,0:T(8,128)S(1)}, u32[]{:S(2)}, u32[]{:S(2)}) collective-permute-start(f32[8,1024]{1,0:T(8,128)S(1)} %get-tuple-element.48), channel_id=1, source_target_pairs={{0,8},{4,12},{8,0},{12,4},{1,9},{5,13},{9,1},{13,5},{2,10},{6,14},... | collective-permute-start | bytes 98312 | tf_op jit(solution)/shard_map/ppermute | solution.py:407
  33.0 5.1 %collective-permute-start.8 = (f32[8,1024]{1,0:T(8,128)S(1)}, f32[8,1024]{1,0:T(8,128)S(1)}, u32[]{:S(2)}, u32[]{:S(2)}) collective-permute-start(f32[8,1024]{1,0:T(8,128)S(1)} %get-tuple-element.49), channel_id=1, source_target_pairs={{0,12},{4,0},{8,4},{12,8},{1,13},{5,1},{9,5},{13,9},{2,14},{6,2},{... | collective-permute-start | bytes 98312 | tf_op jit(solution)/shard_map/ppermute | solution.py:407

commit v4 on v3

--- a/solution.py
+++ b/solution.py
@@ -6,6 +6,7 @@
 from jax.sharding import PartitionSpec as P
 
 BLK = 256
+PAIRED = 4
 TILE = 128
 BF = jnp.bfloat16
 F32 = jnp.float32
@@ -58,8 +59,8 @@
     given = (tap_panel, tap_floor, tap_area)
 
     def body(press_hbm, *refs):
-        from_refs, sums_ref, kept = refs[: n + 3], refs[n + 3], refs[n + 4 : 2 * n + 4]
-        press, panel, floor, area, weights, sems = refs[2 * n + 4 :]
+        from_refs, sums_refs, kept = refs[: n + 3], refs[n + 3 : n + 3 + chunks], refs[n + 3 + chunks : -6]
+        press, panel, floor, area, weights, sems = refs[-6:]
         small = [
             pltpu.make_async_copy(a, b, sems.at[chunks + i])
             for i, (a, b) in enumerate(zip(from_refs, (panel, floor, area, *kept)))
@@ -81,15 +82,15 @@
         for i in range(chunks):
             at = slice(i * span, (i + 1) * span)
             large[i].wait()
-            sums_ref[:, at] = dot(weights[...], press[at], NT)
+            sums_refs[i][...] = dot(weights[...], press[at], NT)
         for copy in small[3:]:
             copy.wait()
 
     out = pl.pallas_call(
         body,
         in_specs=[pl.BlockSpec(memory_space=pltpu.HBM)] * (n + 4),
-        out_specs=tuple(whole(n + 1)),
-        out_shape=(jax.ShapeDtypeStruct((rows, time), F32), *(jax.ShapeDtypeStruct(x.shape, x.dtype) for x in others)),
+        out_specs=tuple(whole(n + chunks)),
+        out_shape=(*[jax.ShapeDtypeStruct((rows, span), F32)] * chunks, *(jax.ShapeDtypeStruct(x.shape, x.dtype) for x in others)),
         scratch_shapes=[
             pltpu.VMEM((time, taps), BF),
             *(pltpu.VMEM(x.shape, x.dtype) for x in given),
@@ -100,7 +101,13 @@
         cost_estimate=cost(3),
         name="tap_sums",
     )(in_hbm(pressures), *(in_hbm(x) for x in given), *(in_hbm(x) for x in others))
-    return out[0], out[1:]
+    return out[:chunks], out[chunks:]
+
+
+def placed(z, nz):
+    if nz != PAIRED:
+        return [lax.rem(z + d, nz) for d in range(nz)]
+    return [z, lax.rem(z + 2, nz), z + 1 - 2 * lax.rem(z, 2), nz - 1 - z]
 
 
 def mode_tables(order, decay, freq, panel_shape, floor_shape, nz, nc):
@@ -118,8 +125,8 @@
         column_ref[...] = jnp.broadcast_to(order_ref[...].astype(F32), (TILE, modes)).T
         z, c = lax.axis_index("taps"), lax.axis_index("floors")
         picked = []
-        for d in range(nz):
-            owner = lax.rem(z + d, nz) * nc + c
+        for at in placed(z, nz):
+            owner = at * nc + c
             picked.append(column_ref[pl.ds(pl.multiple_of(owner * mode_dev, mode_dev), mode_dev), :])
         column = jnp.concatenate(picked, axis=0)[:, :1]
         ids = lax.broadcasted_iota(jnp.int32, (slots, modes), 1).astype(F32)
@@ -184,39 +191,78 @@
     )(order, decay, freq, panel_shape, floor_shape)
 
 
-def slot_forces(sums, pt, nz):
+def slot_forces(sums, pt, tables, turns, nz, before):
     slots, panels = pt.shape
-    time = sums[0].shape[1]
+    rows, time = sums[0].shape
     nc = len(sums)
     mode_dev = slots // nz
+    plan = [(0, 1), (1, 1), (2, 2)] if nz == PAIRED else [(d, 1) for d in range(nz)]
+    n = len(before)
 
     def body(*refs):
-        sum_refs, pt_ref, out_refs, load_ref = refs[:nc], refs[nc], refs[nc + 1 : -1], refs[-1]
-        left = pt_ref[...]
+        sum_refs, (pt_ref, tab_ref, turn_ref) = refs[:nc], refs[nc : nc + 3]
+        before_refs, out_refs = refs[nc + 3 : nc + 3 + n], refs[nc + 3 + n : -3]
+        load_ref, state_refs = refs[-3], refs[-2:]
         load = sum_refs[0][panels:]
         for ref in sum_refs[1:]:
             load = load + ref[panels:]
         load_ref[...] = load
+        left = pt_ref[...]
+        turn = turn_ref[:, 0:1], turn_ref[:, 1:2]
+        state = [ref[...] for ref in before_refs]
         for b in range(time // BLK):
             cols = slice(b * BLK, (b + 1) * BLK)
             total = sum_refs[0][:panels, cols]
             for ref in sum_refs[1:]:
                 total = total + ref[:panels, cols]
             forces = dot_exact_left(left, total)
-            for d in range(nz):
-                out_refs[d][:, cols] = forces[d * mode_dev : (d + 1) * mode_dev]
+            for ref, (p, count) in zip(out_refs, plan):
+                ref[:, cols] = forces[p * mode_dev : (p + count) * mode_dev]
+            new = []
+            for part in (forces * tab_ref[0], forces * tab_ref[1]):
+                near = part[:, :TILE]
+                for k in range(TILE, BLK, TILE):
+                    near = near + part[:, k : k + TILE]
+                new.append(near)
+            if state:
+                new = [a + b for a, b in zip(new, state)]
+            state = turned(turn, new)
+        state_refs[0][...], state_refs[1][...] = state
 
     out = pl.pallas_call(
         body,
-        in_specs=whole(nc + 1),
-        out_specs=whole(nz + 1),
-        out_shape=[jax.ShapeDtypeStruct((mode_dev, time), F32)] * nz
-        + [jax.ShapeDtypeStruct((sums[0].shape[0] - panels, time), F32)],
+        in_specs=whole(nc + 3 + n),
+        out_specs=whole(len(plan) + 3),
+        out_shape=[jax.ShapeDtypeStruct((count * mode_dev, time), F32) for _, count in plan]
+        + [jax.ShapeDtypeStruct((rows - panels, time), F32)]
+        + [jax.ShapeDtypeStruct((slots, TILE), F32)] * 2,
         compiler_params=params(),
         cost_estimate=cost(1),
         name="slot_forces",
-    )(*sums, pt)
-    return out[:nz], out[nz]
+    )(*sums, pt, tables, turns, *before)
+    return out[:-3], out[-3], out[-2:]
+
+
+def end_states(spread, turns, after):
+    slots = turns.shape[0]
+
+    def body(re_ref, im_ref, turn_ref, after_ref, out_ref):
+        pad = jnp.zeros((TILE, TILE - 4), F32)
+        for k in range(0, slots, TILE):
+            at = slice(k, k + TILE)
+            state = [jnp.sum(ref[at], axis=1, keepdims=True) for ref in (re_ref, im_ref)]
+            four = [*state, turn_ref[at, 0:1], turn_ref[at, 1:2]]
+            out_ref[:, at] = jnp.concatenate([*four, pad], axis=1).T[:8]
+
+    return pl.pallas_call(
+        body,
+        in_specs=whole(4),
+        out_specs=whole(1)[0],
+        out_shape=jax.ShapeDtypeStruct((8, slots), F32),
+        compiler_params=params(),
+        cost_estimate=cost(1),
+        name="end_states",
+    )(*spread, turns, after)
 
 
 def triangle():
@@ -229,62 +275,56 @@
     return (a[0] * b[0] - a[1] * b[1], a[0] * b[1] + a[1] * b[0])
 
 
-def partial_states(forces, tables, turns, floor_slots):
-    nz = len(forces)
-    mode_dev, time = forces[0].shape
+def motion_from_rest(forces, tables, turns, floor_slots):
     slots = turns.shape[0]
     floors = floor_slots.shape[0]
+    time = max(start + x.shape[1] for x, _, start in forces)
     blocks = time // BLK
+    n = len(forces)
+    places = [(row, start, x.shape) for x, row, start in forces]
 
     def body(*refs):
-        force_refs = refs[:nz]
-        tab_ref, turn_ref, fs_ref, motion_ref, ends_ref, all_ref = refs[nz:]
-        for d in range(nz):
-            all_ref[d * mode_dev : (d + 1) * mode_dev] = force_refs[d][...]
+        tab_ref, turn_ref, fs_ref, motion_ref = refs[n:]
         tri = triangle()
-        pad = jnp.zeros((TILE, TILE - 4), F32)
-        for i in range(slots // TILE):
-            at = slice(i * TILE, (i + 1) * TILE)
-            pr, pi, qr, qi = tab_ref[0, at], tab_ref[1, at], tab_ref[2, at], tab_ref[3, at]
-            turn = turn_ref[at, 0:1], turn_ref[at, 1:2]
-            here = fs_ref[:, at].astype(BF)
-            ar = jnp.zeros((TILE, 1), F32)
-            ai = jnp.zeros((TILE, 1), F32)
-            for b in range(blocks):
-                cols = slice(b * BLK, (b + 1) * BLK)
-                force = all_ref[at, cols]
-                cr = dot_exact_right(force * pr, tri) + ar
-                ci = dot_exact_right(force * pi, tri) + ai
-                part = dot_exact_left(here, qr * cr - qi * ci)
-                motion_ref[:, cols] = part if i == 0 else motion_ref[:, cols] + part
-                ar, ai = turned(turn, (cr[:, BLK - 1 :], ci[:, BLK - 1 :]))
-            ends_ref[:, at] = jnp.concatenate([ar, ai, *turn, pad], axis=1).T[:8]
-
-    return pl.pallas_call(
-        body,
-        in_specs=whole(nz + 3),
-        out_specs=tuple(whole(2)),
-        out_shape=(
-            jax.ShapeDtypeStruct((floors, time), F32),
-            jax.ShapeDtypeStruct((8, slots), F32),
-        ),
-        scratch_shapes=[pltpu.VMEM((slots, time), F32)],
-        compiler_params=params(),
-        cost_estimate=cost(3),
-        name="partial_states",
-    )(*forces, tables, turns, floor_slots)
-
-
-def floor_shares(motion, ends, enter, tables, floor_slots, forces):
+        here = fs_ref[...].astype(BF)
+        turn = turn_ref[:, 0:1], turn_ref[:, 1:2]
+        state = None
+        for b in range(blocks):
+            found = [
+                (row, ref[:, b * BLK - start : (b + 1) * BLK - start])
+                for ref, (row, start, shape) in zip(refs, places)
+                if start <= b * BLK < start + shape[1]
+            ]
+            force = jnp.concatenate([x for _, x in sorted(found, key=lambda f: f[0])], axis=0)
+            cr = dot_exact_right(force * tab_ref[0], tri)
+            ci = dot_exact_right(force * tab_ref[1], tri)
+            if state is not None:
+                cr, ci = cr + state[0], ci + state[1]
+            part = dot_exact_left(here, tab_ref[2] * cr - tab_ref[3] * ci)
+            motion_ref[:, b * BLK : (b + 1) * BLK] = part
+            if b < blocks - 1:
+                state = turned(turn, (cr[:, BLK - 1 :], ci[:, BLK - 1 :]))
+
+    return pl.pallas_call(
+        body,
+        in_specs=whole(n + 3),
+        out_specs=whole(1)[0],
+        out_shape=jax.ShapeDtypeStruct((floors, time), F32),
+        compiler_params=params(),
+        cost_estimate=cost(2),
+        name="motion_from_rest",
+    )(*(x for x, _, _ in forces), tables, turns, floor_slots)
+
+
+def floor_shares(motion, ends, enter, tables, floor_slots, onward):
     floors, time = motion.shape
     blocks = time // BLK
+    n = len(onward)
 
     def body(motion_ref, ends_ref, enter_ref, tab_ref, fs_ref, *refs):
-        force_refs, out_ref, force_ref = refs[:-2], refs[-2], refs[-1]
-        force = force_refs[0][...]
-        for ref in force_refs[1:]:
-            force = force + ref[...]
-        force_ref[...] = force
+        out_ref = refs[n]
+        if n:
+            refs[n + 1][...] = refs[0][...] + refs[1][refs[0].shape[0] :]
         shape = fs_ref[...]
         turn = (ends_ref[2:3, :], ends_ref[3:4, :])
         later = lax.axis_index("tm") > 0
@@ -306,24 +346,30 @@
 
     return pl.pallas_call(
         body,
-        in_specs=whole(5 + len(forces)),
-        out_specs=tuple(whole(2)),
-        out_shape=(jax.ShapeDtypeStruct((floors, time), F32), jax.ShapeDtypeStruct(forces[0].shape, F32)),
+        in_specs=whole(5 + n),
+        out_specs=whole(1 + len(onward[:1])),
+        out_shape=[
+            jax.ShapeDtypeStruct(x, F32) for x in [(floors, time)] + [x.shape for x in onward[:1]]
+        ],
         compiler_params=params(),
         cost_estimate=cost(1),
         name="floor_shares",
-    )(motion, ends, enter, tables, floor_slots, *forces)
-
-
-def owner_shares(motions, load, enter, nz, floor_dev, mode_dev):
-    nc = len(motions)
+    )(motion, ends, enter, tables, floor_slots, *onward)
+
+
+def owner_shares(motions, loads, enter, nz, floor_dev):
+    nc, parts = len(motions), len(loads)
     floors, time = motions[0].shape
-    rows = -(-(2 * floor_dev + 2) // 8) * 8
+    rows = share_rows(floor_dev)
     owners = nz * nc
+    mode_dev = enter.shape[1] // nz
+    span = time // parts
+    paired = nz == PAIRED
+    shapes = [(rows, time)] * 2 + [(2 * rows, time)] if paired else [(rows, time)] * nz
 
     def body(*refs):
-        motion_refs, load_ref, enter_ref = refs[:nc], refs[nc], refs[nc + 1]
-        out_refs, motion_all, load_all = refs[nc + 2 : nc + 2 + nz], refs[-2], refs[-1]
+        motion_refs, load_refs, enter_ref = refs[:nc], refs[nc : nc + parts], refs[nc + parts]
+        out_refs, motion_all, load_all = refs[nc + parts + 1 : -2], refs[-2], refs[-1]
         z, c = lax.axis_index("taps"), lax.axis_index("floors")
         later = lax.axis_index("tm") > 0
         motion = motion_refs[0][...]
@@ -332,70 +378,152 @@
         for o in range(owners):
             at = slice(o * floor_dev, (o + 1) * floor_dev)
             motion_all[o] = motion[at]
-            load_all[o] = load_ref[at]
-        for d in range(nz):
-            owner = lax.rem(z + d, nz) * nc + c
-            out = out_refs[d]
-            out[...] = jnp.zeros_like(out)
+            for k in range(parts):
+                load_all[o, :, k * span : (k + 1) * span] = load_refs[k][at]
+        for p, place in enumerate(placed(z, nz)):
+            owner = place * nc + c
+            out = out_refs[2].at[(p - 2) * rows : (p - 1) * rows] if paired and p > 1 else out_refs[p]
+            out[...] = jnp.zeros((rows, time), F32)
             out[:floor_dev] = motion_all[owner]
             out[floor_dev : 2 * floor_dev] = load_all[owner]
-            at = slice(d * mode_dev, (d + 1) * mode_dev)
-            out[2 * floor_dev : 2 * floor_dev + 2, :mode_dev] = jnp.where(later, enter_ref[0:2, at], 0.0)
-
-    return pl.pallas_call(
-        body,
-        in_specs=whole(nc + 2),
-        out_specs=whole(nz),
-        out_shape=[jax.ShapeDtypeStruct((rows, time), F32)] * nz,
+            state = enter_ref[0:2, p * mode_dev : (p + 1) * mode_dev]
+            out[2 * floor_dev : 2 * floor_dev + 2, :mode_dev] = jnp.where(later, state, 0.0)
+
+    return pl.pallas_call(
+        body,
+        in_specs=whole(nc + parts + 1),
+        out_specs=whole(len(shapes)),
+        out_shape=[jax.ShapeDtypeStruct(x, F32) for x in shapes],
         scratch_shapes=[pltpu.VMEM((owners, floor_dev, time), F32)] * 2,
         compiler_params=params(),
         cost_estimate=cost(1),
         name="owner_shares",
-    )(*motions, load, enter)
-
-
-def own_response(forces, shares, tables, turns, floor_dev, load_scale):
-    mode_dev, time = forces[0].shape
-    n, m = len(forces), len(shares)
+    )(*motions, *loads, enter)
+
+
+def share_rows(floor_dev):
+    return -(-(2 * floor_dev + 2) // 8) * 8
+
+
+def onward_second(two, arrived, share, share_arrived):
+    mode_dev, half = two.shape
+    rows = share.shape[0]
+
+    def body(two_ref, arrived_ref, share_ref, share_arrived_ref, out_ref):
+        out_ref[:mode_dev] = two_ref[...] + arrived_ref[mode_dev:]
+        total = share_ref[...] + share_arrived_ref[rows:]
+        out_ref[mode_dev : mode_dev + rows] = total[:, :half]
+        out_ref[mode_dev + rows :] = total[:, half:]
+
+    return pl.pallas_call(
+        body,
+        in_specs=whole(4),
+        out_specs=whole(1)[0],
+        out_shape=jax.ShapeDtypeStruct((mode_dev + 2 * rows, half), F32),
+        compiler_params=params(),
+        cost_estimate=cost(1),
+        name="onward_second",
+    )(two, arrived, share, share_arrived)
+
+
+def block_sums(force, tables, tri):
+    return [dot_exact_right(force * table, tri) for table in tables]
+
+
+def sum_at(refs, forces, b, mode_dev):
+    total = None
+    for ref, (x, row, start) in zip(refs, forces):
+        if start <= b * BLK < start + x.shape[1]:
+            part = ref[row : row + mode_dev, b * BLK - start : (b + 1) * BLK - start]
+            total = part if total is None else total + part
+    return total
+
+
+def own_start(forces, tables, turns, until):
+    mode_dev = forces[0][0].shape[0]
+    n = len(forces)
+
+    def body(*refs):
+        tab_ref, turn_ref, resp_ref, state_ref = refs[n:]
+        turn = turn_ref[:mode_dev, 0:1], turn_ref[:mode_dev, 1:2]
+        tri = triangle()
+        state = None
+        for b in range(until // BLK):
+            cr, ci = block_sums(sum_at(refs, forces, b, mode_dev), (tab_ref[0], tab_ref[1]), tri)
+            if state is not None:
+                cr, ci = cr + state[0], ci + state[1]
+            resp_ref[:, b * BLK : (b + 1) * BLK] = tab_ref[2] * cr - tab_ref[3] * ci
+            state = turned(turn, (cr[:, BLK - 1 :], ci[:, BLK - 1 :]))
+        state_ref[:, 0:1], state_ref[:, 1:2] = state
+
+    return pl.pallas_call(
+        body,
+        in_specs=whole(n + 2),
+        out_specs=tuple(whole(2)),
+        out_shape=(
+            jax.ShapeDtypeStruct((mode_dev, until), F32),
+            jax.ShapeDtypeStruct((mode_dev, 2), F32),
+        ),
+        compiler_params=params(),
+        cost_estimate=cost(1),
+        name="own_start",
+    )(*(x for x, _, _ in forces), tables, turns)
+
+
+def own_response(forces, shares, tables, turns, floor_dev, load_scale, begun):
+    mode_dev = forces[0][0].shape[0]
+    rows = share_rows(floor_dev)
+    n, m, k = len(shares), len(forces), len(begun)
+    time = shares[0][0].shape[1]
     blocks = time // BLK
+    until = begun[0].shape[1] // BLK if begun else 0
 
     def body(*refs):
-        force_refs, share_refs = refs[:n], refs[n : n + m]
-        tab_ref, turn_ref, resp_ref, motion_ref, load_ref = refs[n + m :]
-        share = share_refs[0][...]
-        for ref in share_refs[1:]:
-            share = share + ref[...]
+        begun_refs = refs[m + n : m + n + k]
+        tab_ref, turn_ref, resp_ref, motion_ref, load_ref, share_ref = refs[m + n + k :]
+        for i, (x, row, start) in enumerate(shares):
+            at = slice(start, start + x.shape[1])
+            part = refs[m + i][row : row + rows]
+            share_ref[:, at] = part if i == 0 else share_ref[:, at] + part
+        share = share_ref[...]
         motion_ref[...] = share[:floor_dev]
         load_ref[...] = share[floor_dev : 2 * floor_dev] * load_scale
-        pr, pi, qr, qi = (tab_ref[i] for i in range(4))
+        qr, qi = tab_ref[2], tab_ref[3]
         turn = turn_ref[:mode_dev, 0:1], turn_ref[:mode_dev, 1:2]
         column = share[:, :TILE].T
         at = 2 * floor_dev
-        ar, ai = column[:mode_dev, at : at + 1], column[:mode_dev, at + 1 : at + 2]
+        state = column[:mode_dev, at : at + 1], column[:mode_dev, at + 1 : at + 2]
         tri = triangle()
+        sums = {
+            b: block_sums(sum_at(refs, forces, b, mode_dev), (tab_ref[0], tab_ref[1]), tri)
+            for b in range(until, blocks)
+        }
         for b in range(blocks):
             cols = slice(b * BLK, (b + 1) * BLK)
-            force = force_refs[0][:, cols]
-            for ref in force_refs[1:]:
-                force = force + ref[:, cols]
-            cr = dot_exact_right(force * pr, tri) + ar
-            ci = dot_exact_right(force * pi, tri) + ai
-            resp_ref[:, cols] = qr * cr - qi * ci
-            ar, ai = turned(turn, (cr[:, BLK - 1 :], ci[:, BLK - 1 :]))
-
-    return pl.pallas_call(
-        body,
-        in_specs=whole(n + m + 2),
+            if b < until:
+                resp_ref[:, cols] = begun_refs[0][:, cols] + (qr * state[0] - qi * state[1])
+                state = turned(turn, state)
+                if b == until - 1:
+                    state = state[0] + begun_refs[1][:, 0:1], state[1] + begun_refs[1][:, 1:2]
+            else:
+                cr, ci = (x + y for x, y in zip(sums[b], state))
+                resp_ref[:, cols] = qr * cr - qi * ci
+                state = turned(turn, (cr[:, BLK - 1 :], ci[:, BLK - 1 :]))
+
+    return pl.pallas_call(
+        body,
+        in_specs=whole(m + n + k + 2),
         out_specs=tuple(whole(3)),
         out_shape=(
             jax.ShapeDtypeStruct((mode_dev, time), F32),
             jax.ShapeDtypeStruct((floor_dev, time), F32),
             jax.ShapeDtypeStruct((floor_dev, time), F32),
         ),
-        compiler_params=params(),
-        cost_estimate=cost(2),
+        scratch_shapes=[pltpu.VMEM((rows, time), F32)],
+        compiler_params=params(),
+        cost_estimate=cost(1),
         name="own_response",
-    )(*forces, *shares, tables, turns)
+    )(*(x for x, _, _ in forces), *(x for x, _, _ in shares), *begun, tables, turns)
 
 
 def shifts(x, axis, n):
@@ -440,11 +568,24 @@
         panels,
         floors,
     )
-    sums = [mine] + shifts(mine, "floors", nc)
+    sums = [[x] + shifts(x, "floors", nc) for x in mine]
     pt, floor_slots, tables, turns, own = mode_tables(*kept, nz, nc)
-    forces, load = slot_forces(sums, pt, nz)
-    got_forces = along(forces, nz)
-    motion, ends = partial_states(forces, tables, turns, floor_slots)
+    forces, loads, spread = [], [], []
+    for part in sums:
+        force, load, spread = slot_forces(part, pt, tables, turns, nz, spread)
+        forces.append(force)
+        loads.append(load)
+    half = time // 2
+    span = time // len(forces)
+    pair, two = ([(i, i ^ d) for i in range(nz)] for d in (1, 2))
+    laid = [(x, p * mode_dev, k * span) for k, part in enumerate(forces) for p, x in enumerate(part)]
+    if nz == PAIRED:
+        crossed = [lax.ppermute(part[2], "taps", pair) for part in forces]
+        onward = [forces[0][1], crossed[0]]
+    else:
+        crossed, onward = [(x, 0, k * span) for k, part in enumerate(forces) for x in along(part, nz)], []
+    motion = motion_from_rest(laid, tables, turns, floor_slots)
+    ends = end_states(spread, turns, motion)
     enter = jnp.zeros_like(ends)
     for hop in range(nt - 1):
         passed = ends
@@ -459,14 +600,21 @@
             )
         enter = lax.ppermute(passed, "tm", [(i, (i + 1) % nt) for i in range(nt)])
         enter = jnp.where(lax.axis_index("tm") > 0, enter, 0.0)
-    early = [x for d, x in enumerate(got_forces) if d != nz // 2]
-    motion, force = floor_shares(motion, ends, enter, tables, floor_slots, early)
-    got_forces = [force, got_forces[nz // 2]]
+    motion, *onward = floor_shares(motion, ends, enter, tables, floor_slots, onward)
     motions = [motion] + shifts(motion, "floors", nc)
-    shares = owner_shares(motions, load, enter, nz, floor_dev, mode_dev)
-    return own_response(
-        got_forces, along(shares, nz), own, turns, floor_dev, load_scale
-    )
+    shares = owner_shares(motions, loads, enter, nz, floor_dev)
+    if nz == PAIRED:
+        rows = share_rows(floor_dev)
+        other = lax.ppermute(shares[2], "taps", pair)
+        first = lax.ppermute(onward[0], "taps", two)
+        second = lax.ppermute(onward_second(forces[1][1], crossed[1], shares[1], other), "taps", two)
+        begun = own_start([(forces[0][0], 0, 0), (crossed[0], 0, 0), (first, 0, 0)], own, turns, half)
+        crossed = [(forces[1][0], 0, half), (crossed[1], 0, half), (second, 0, half)]
+        shares = [(shares[0], 0, 0), (other, 0, 0), (second, mode_dev, 0), (second, mode_dev + rows, half)]
+    else:
+        begun = []
+        shares = [(x, 0, 0) for x in along(shares, nz)]
+    return own_response(crossed, shares, own, turns, floor_dev, load_scale, begun)
 
 
 def solution(mesh):

time: 39.9 us -> 38.1 us (0.955)
  starting transfers between devices: 18.2 us -> 13.5 us
  waiting for transfers between devices: 11.1 us -> 13.7 us
    ppermute x6 -> x5, starting transfers between devices: 15.9 us -> 11.3 us  [the longest x2 3.52 us: on_device(): crossed = [lax.ppermute(part[2], 'taps', pair) for part in forces]]
    ppermute x6 -> x5, waiting for transfers between devices: 7.83 us -> 10.7 us  [the longest x1 7.75 us: on_device(): first = lax.ppermute(onward[0], 'taps', two)]
    ppermute x2 -> x3, waiting for transfers between devices: 2.05 us -> 1.25 us  [shifts(): lax.ppermute(x, axis, [(i, (i + d) % n) for i in range(n)])]
    ppermute x1, waiting for transfers between devices: 1.22 us -> 1.71 us  [on_device(): enter = lax.ppermute(passed, 'tm', [(i, (i + 1) % nt) for i in range(nt)])]
    pallas_call x5 -> x9, Pallas kernels: 4.82 us -> 5.15 us  [the longest x1 1.45 us: motion_from_rest(): pl.pallas_call(body, in_specs=whole(n + 3), out_specs=whole(1)[0], out_sh...]
  transfers between devices with their start and end apart: 9 -> 9, of which waited for: 7 -> 6; matrix products, arithmetic and copies ran while one was open for 0% -> 0% of each run, Pallas kernels for 11% -> 14%
where the time goes in v4:
time: 38.1 us; the launch traced here: 37.9 us
  waiting for transfers between devices  13.7 us (36%)
  starting transfers between devices  13.5 us (35%)
  Pallas kernels  10 us (26%)
  between operations  0.68 us (2%)
    ppermute x1, waiting for transfers between devices, on_device(): first = lax.ppermute(onward[0], 'taps', two)  7.75 us
    ppermute x2, starting transfers between devices, on_device(): crossed = [lax.ppermute(part[2], 'taps', pair) for part in forces]  3.52 us
    pallas_call x1, Pallas kernels, tap_sums(): pl.pallas_call(body, in_specs=[pl.BlockSpec(memory_space=pltpu.HBM)] * (n...  3.29 us
    ppermute x1, starting transfers between devices, on_device(): lax.ppermute(onward_second(forces[1][1], crossed[1], shares[1], other), '...  3.15 us
    ppermute x1, starting transfers between devices, on_device(): first = lax.ppermute(onward[0], 'taps', two)  2.59 us
    ppermute x1, starting transfers between devices, on_device(): other = lax.ppermute(shares[2], 'taps', pair)  2.09 us
    ppermute x1, waiting for transfers between devices, on_device(): lax.ppermute(onward_second(forces[1][1], crossed[1], shares[1], other), '...  1.78 us
    ppermute x1, waiting for transfers between devices, on_device(): enter = lax.ppermute(passed, 'tm', [(i, (i + 1) % nt) for i in range(nt)])  1.71 us
  transfers between devices with their start and end apart: 9, of which 6 were waited for; matrix products, arithmetic and copies ran while one was open for 0% of the time, Pallas kernels for 14%

profile of v4, /device:TPU:0, one launch (start us, length us, event | category | flops | bytes accessed | tf_op | source)
XLA Modules:
  0.0 37.9 jit_solution(14295297095755345002)
XLA Ops:
  0.6 3.3 %tap_sums.1 = (f32[272,512]{1,0:T(8,128)S(1)}, f32[272,512]{1,0:T(8,128)S(1)}, s32[1,512]{1,0:T(1,128)S(1)}, f32[1,512]{1,0:T(1,128)S(1)}, f32[1,512]{1,0:T(1,12...) custom-call(bf16[1024,2048]{1,0:T(8,128)(2,1)} %press_hbm.1, s32[1,2048]{1,0:T(1,128)} %bitcast.5, ...), custom_call_target="tpu_custom_call" | custom-call | flops 1500000000 | bytes 6000000 | tf_op jit(solution)/shard_map/tap_sums/pallas_call | solution.py:89
  3.9 0.5 %collective-permute-start.1 = (f32[272,512]{1,0:T(8,128)S(1)}, f32[272,512]{1,0:T(8,128)S(1)}, u32[]{:S(2)}, u32[]{:S(2)}) collective-permute-start(f32[272,512]{1,0:T(8,128)S(1)} %get-tuple-element.43.refs_0_), channel_id=1, source_target_pairs={{0,1},{1,0},{2,3},{3,2},{4,5},{5,4},{6,7},{7,6},{8,9},{9,8},{10,11... | collective-permute-start | bytes 1671176 | tf_op jit(solution)/shard_map/ppermute | solution.py:530
  4.4 0.1 collective-permute-start
  4.5 1.6 %mode_tables.1 = (bf16[256,256]{1,0:T(8,128)(2,1)S(1)}, f32[16,256]{1,0:T(8,128)S(1)}, f32[4,256,256]{2,1,0:T(8,128)S(1)}, f32[256,2]{1,0:T(8,128)S(1)}, f32[4,64,256]{2,1,0:T(8,128)S(1)}) custom-call(s32[1,512]{1,0:T(1,128)S(1)} %get-tuple-element.35.refs_0_, f32[1,512]{1,0:T(1,128)S(1)} %get-tuple-element.36.refs_1_, ...), custom_call_target="tpu_custom_call" | custom-call | flops 1000000000 | bytes 4000000 | tf_op jit(solution)/shard_map/mode_tables/pallas_call | solution.py:176
  6.1 0.0 collective-permute-done.1.refs_1_
  6.1 0.4 %slot_forces.2 = (f32[64,512]{1,0:T(8,128)S(1)}, f32[64,512]{1,0:T(8,128)S(1)}, f32[128,512]{1,0:T(8,128)S(1)}, f32[16,512]{1,0:T(8,128)S(1)}, f32[256,128]{1,0:T(8,128)S(1)}, /*index=5*/f32[256,128]{1,0:T(8,128)S(1)}) custom-call(f32[272,512]{1,0:T(8,128)S(1)} %get-tuple-element.43.refs_0_, f32[272,512]{1,0:T(8,128)S(1)} %collective-permute-done.1.refs_1_, ...), custom_call_target="tpu_custom_call" | custom-call | flops 500000000 | bytes 2000000 | tf_op jit(solution)/shard_map/slot_forces/pallas_call | solution.py:232
  6.5 3.1 %collective-permute-start.4 = (f32[128,512]{1,0:T(8,128)S(1)}, f32[128,512]{1,0:T(8,128)S(1)}, u32[]{:S(2)}, u32[]{:S(2)}) collective-permute-start(f32[128,512]{1,0:T(8,128)S(1)} %get-tuple-element.51.refs_2_), channel_id=1, source_target_pairs={{0,4},{4,0},{8,12},{12,8},{1,5},{5,1},{9,13},{13,9},{2,6},{6,2},{1... | collective-permute-start | bytes 786440 | tf_op jit(solution)/shard_map/ppermute | solution.py:583
  9.6 0.0 collective-permute-done.refs_1_
  9.6 0.4 %slot_forces.3 = (f32[64,512]{1,0:T(8,128)S(1)}, f32[64,512]{1,0:T(8,128)S(1)}, f32[128,512]{1,0:T(8,128)S(1)}, f32[16,512]{1,0:T(8,128)S(1)}, f32[256,128]{1,0:T(8,128)S(1)}, /*index=5*/f32[256,128]{1,0:T(8,128)S(1)}) custom-call(f32[272,512]{1,0:T(8,128)S(1)} %get-tuple-element.34.refs_0_, f32[272,512]{1,0:T(8,128)S(1)} %collective-permute-done.refs_1_, ...), custom_call_target="tpu_custom_call" | custom-call | flops 500000000 | bytes 2000000 | tf_op jit(solution)/shard_map/slot_forces/pallas_call | solution.py:232
  10.0 1.5 %motion_from_rest.1.after_ref.motion_ref = f32[16,1024]{1,0:T(8,128)S(1)} custom-call(f32[64,512]{1,0:T(8,128)S(1)} %get-tuple-element.49.refs_0_, f32[64,512]{1,0:T(8,128)S(1)} %get-tuple-element.50.refs_1_.refs_0_, f32[128,512]{1,0:T(8,128)S(1)} %get-tuple-element.51.refs_2_, f32[64,512]{1,0:T(8,128)S(1)} %get-tuple-element.46.refs_3_.refs_0_, ...), custom_call_target="tpu_custom_call" | custom-call | flops 1000000000 | bytes 4000000 | tf_op jit(solution)/shard_map/motion_from_rest/pallas_call | solution.py:308
  11.5 0.4 %end_states.1.ends_ref = f32[8,256]{1,0:T(8,128)S(1)} custom-call(f32[256,128]{1,0:T(8,128)S(1)} %get-tuple-element.53.re_ref, f32[256,128]{1,0:T(8,128)S(1)} %get-tuple-element.54.im_ref, f32[256,2]{1,0:T(8,128)S(1)} %get-tuple-element.42.refs_4_.refs_7_.turn_ref.refs_10_, f32[16,1024]{1,0:T(8,128)S(1)} %motion_from_rest.1.after_ref.motion_ref), custom_call_target="tpu_custom_call" | custom-call | flops 500000000 | bytes 2000000 | tf_op jit(solution)/shard_map/end_states/pallas_call | solution.py:257
  11.9 1.5 %collective-permute-start.3 = (f32[8,256]{1,0:T(8,128)S(1)}, f32[8,256]{1,0:T(8,128)S(1)}, u32[]{:S(2)}, u32[]{:S(2)}) collective-permute-start(f32[8,256]{1,0:T(8,128)S(1)} %end_states.1.ends_ref), channel_id=1, source_target_pairs={{0,2},{2,0},{1,3},{3,1},{4,6},{6,4},{5,7},{7,5},{8,10},{10,8},{9,1... | collective-permute-start | bytes 24584 | tf_op jit(solution)/shard_map/ppermute | solution.py:601
  13.4 0.5 %collective-permute-start.2 = (f32[128,512]{1,0:T(8,128)S(1)}, f32[128,512]{1,0:T(8,128)S(1)}, u32[]{:S(2)}, u32[]{:S(2)}) collective-permute-start(f32[128,512]{1,0:T(8,128)S(1)} %get-tuple-element.47.refs_5_), channel_id=1, source_target_pairs={{0,4},{4,0},{8,12},{12,8},{1,5},{5,1},{9,13},{13,9},{2,6},{6,2},{1... | collective-permute-start | bytes 786440 | tf_op jit(solution)/shard_map/ppermute | solution.py:583
  13.9 1.7 %collective-permute-done.3 = f32[8,256]{1,0:T(8,128)S(1)} collective-permute-done((f32[8,256]{1,0:T(8,128)S(1)}, f32[8,256]{1,0:T(8,128)S(1)}, u32[]{:S(2)}, u32[]{:S(2)}) %collective-permute-start.3) | collective-permute-done | bytes 8224 | tf_op jit(solution)/shard_map/ppermute | solution.py:601
  15.6 1.1 %collective-permute-done.4.refs_1_ = f32[128,512]{1,0:T(8,128)S(1)} collective-permute-done((f32[128,512]{1,0:T(8,128)S(1)}, f32[128,512]{1,0:T(8,128)S(1)}, u32[]{:S(2)}, u32[]{:S(2)}) %collective-permute-start.4) | collective-permute-done | bytes 262176 | tf_op jit(solution)/shard_map/ppermute | solution.py:583
  16.7 0.3 floor_shares.1
  17.0 0.1 collective-permute-start.5
  17.1 1.2 %collective-permute-done.5.refs_1_ = f32[16,1024]{1,0:T(8,128)S(1)} collective-permute-done((f32[16,1024]{1,0:T(8,128)S(1)}, f32[16,1024]{1,0:T(8,128)S(1)}, u32[]{:S(2)}, u32[]{:S(2)}) %collective-permute-start.5) | collective-permute-done | bytes 65568 | tf_op jit(solution)/shard_map/ppermute | solution.py:530
  18.3 0.1 owner_shares.1
  18.4 2.1 %collective-permute-start.6 = (f32[16,1024]{1,0:T(8,128)S(1)}, f32[16,1024]{1,0:T(8,128)S(1)}, u32[]{:S(2)}, u32[]{:S(2)}) collective-permute-start(f32[16,1024]{1,0:T(8,128)S(1)} %get-tuple-element.59), channel_id=1, source_target_pairs={{0,4},{4,0},{8,12},{12,8},{1,5},{5,1},{9,13},{13,9},{2,6},{6,2},{1... | collective-permute-start | bytes 196616 | tf_op jit(solution)/shard_map/ppermute | solution.py:608
  20.5 2.6 %collective-permute-start.8 = (f32[64,512]{1,0:T(8,128)S(1)}, f32[64,512]{1,0:T(8,128)S(1)}, u32[]{:S(2)}, u32[]{:S(2)}) collective-permute-start(f32[64,512]{1,0:T(8,128)S(1)} %get-tuple-element.61), channel_id=1, source_target_pairs={{0,8},{4,12},{8,0},{12,4},{1,9},{5,13},{9,1},{13,5},{2,10},{6,14},... | collective-permute-start | bytes 393224 | tf_op jit(solution)/shard_map/ppermute | solution.py:609
  23.1 0.0 collective-permute-done.2.arrived_ref.refs_1_
  23.1 0.1 collective-permute-done.6.share_arrived_ref.refs_4_
  23.2 3.1 %collective-permute-start.7 = (f32[80,512]{1,0:T(8,128)S(1)}, f32[80,512]{1,0:T(8,128)S(1)}, u32[]{:S(2)}, u32[]{:S(2)}) collective-permute-start(f32[80,512]{1,0:T(8,128)S(1)} %onward_second.1), channel_id=1, source_target_pairs={{0,8},{4,12},{8,0},{12,4},{1,9},{5,13},{9,1},{13,5},{2,10},{6,14},... | collective-permute-start | bytes 491528 | tf_op jit(solution)/shard_map/ppermute | solution.py:610
  26.3 7.8 %collective-permute-done.8.refs_2_ = f32[64,512]{1,0:T(8,128)S(1)} collective-permute-done((f32[64,512]{1,0:T(8,128)S(1)}, f32[64,512]{1,0:T(8,128)S(1)}, u32[]{:S(2)}, u32[]{:S(2)}) %collective-permute-start.8) | collective-permute-done | bytes 131104 | tf_op jit(solution)/shard_map/ppermute | solution.py:609
  34.1 0.6 %own_start.1 = (f32[64,512]{1,0:T(8,128)S(1)}, f32[64,2]{1,0:T(8,128)S(1)}) custom-call(f32[64,512]{1,0:T(8,128)S(1)} %get-tuple-element.49.refs_0_, f32[128,512]{1,0:T(8,128)S(1)} %collective-permute-done.4.refs_1_, f32[64,512]{1,0:T(8,128)S(1)} %collective-permute-done.8.refs_2_, f32[4,64,256]{2,1,0:T(8,128)S(1)} %get-tuple-element.62.refs_3_.refs_9_, ...), custom_call_target="tpu_custom_call" | custom-call | flops 500000000 | bytes 2000000 | tf_op jit(solution)/shard_map/own_start/pallas_call | solution.py:459
  34.7 1.8 %collective-permute-done.7.refs_2_.refs_5_.refs_6_ = f32[80,512]{1,0:T(8,128)S(1)} collective-permute-done((f32[80,512]{1,0:T(8,128)S(1)}, f32[80,512]{1,0:T(8,128)S(1)}, u32[]{:S(2)}, u32[]{:S(2)}) %collective-permute-start.7) | collective-permute-done | bytes 163872 | tf_op jit(solution)/shard_map/ppermute | solution.py:610
  36.5 1.4 %own_response.1 = (f32[64,1024]{1,0:T(8,128)}, f32[2,1024]{1,0:T(2,128)}, f32[2,1024]{1,0:T(2,128)}) custom-call(f32[64,512]{1,0:T(8,128)S(1)} %get-tuple-element.46.refs_3_.refs_0_, f32[128,512]{1,0:T(8,128)S(1)} %collective-permute-done.2.arrived_ref.refs_1_, f32[80,512]{1,0:T(8,128)S(1)} %collective-permute-done.7.refs_2_.refs_5_.refs_6_, ...), custom_call_target="tpu_custom_call" | custom-call | flops 500000000 | bytes 2000000 | tf_op jit(solution)/shard_map/own_response/pallas_call | solution.py:513
  (2 shorter events, 0.0 us)
Async XLA Ops:
  3.9 2.2 %collective-permute-start.1 = (f32[272,512]{1,0:T(8,128)S(1)}, f32[272,512]{1,0:T(8,128)S(1)}, u32[]{:S(2)}, u32[]{:S(2)}) collective-permute-start(f32[272,512]{1,0:T(8,128)S(1)} %get-tuple-element.43.refs_0_), channel_id=1, source_target_pairs={{0,1},{1,0},{2,3},{3,2},{4,5},{5,4},{6,7},{7,6},{8,9},{9,8},{10,11... | collective-permute-start | bytes 1671176 | tf_op jit(solution)/shard_map/ppermute | solution.py:530
  4.4 5.1 %collective-permute-start = (f32[272,512]{1,0:T(8,128)S(1)}, f32[272,512]{1,0:T(8,128)S(1)}, u32[]{:S(2)}, u32[]{:S(2)}) collective-permute-start(f32[272,512]{1,0:T(8,128)S(1)} %get-tuple-element.34.refs_0_), channel_id=1, source_target_pairs={{0,1},{1,0},{2,3},{3,2},{4,5},{5,4},{6,7},{7,6},{8,9},{9,8},{10,11... | collective-permute-start | bytes 1671176 | tf_op jit(solution)/shard_map/ppermute | solution.py:530
  6.5 10.2 %collective-permute-start.4 = (f32[128,512]{1,0:T(8,128)S(1)}, f32[128,512]{1,0:T(8,128)S(1)}, u32[]{:S(2)}, u32[]{:S(2)}) collective-permute-start(f32[128,512]{1,0:T(8,128)S(1)} %get-tuple-element.51.refs_2_), channel_id=1, source_target_pairs={{0,4},{4,0},{8,12},{12,8},{1,5},{5,1},{9,13},{13,9},{2,6},{6,2},{1... | collective-permute-start | bytes 786440 | tf_op jit(solution)/shard_map/ppermute | solution.py:583
  11.9 3.7 %collective-permute-start.3 = (f32[8,256]{1,0:T(8,128)S(1)}, f32[8,256]{1,0:T(8,128)S(1)}, u32[]{:S(2)}, u32[]{:S(2)}) collective-permute-start(f32[8,256]{1,0:T(8,128)S(1)} %end_states.1.ends_ref), channel_id=1, source_target_pairs={{0,2},{2,0},{1,3},{3,1},{4,6},{6,4},{5,7},{7,5},{8,10},{10,8},{9,1... | collective-permute-start | bytes 24584 | tf_op jit(solution)/shard_map/ppermute | solution.py:601
  13.4 9.6 %collective-permute-start.2 = (f32[128,512]{1,0:T(8,128)S(1)}, f32[128,512]{1,0:T(8,128)S(1)}, u32[]{:S(2)}, u32[]{:S(2)}) collective-permute-start(f32[128,512]{1,0:T(8,128)S(1)} %get-tuple-element.47.refs_5_), channel_id=1, source_target_pairs={{0,4},{4,0},{8,12},{12,8},{1,5},{5,1},{9,13},{13,9},{2,6},{6,2},{1... | collective-permute-start | bytes 786440 | tf_op jit(solution)/shard_map/ppermute | solution.py:583
  17.0 1.3 %collective-permute-start.5 = (f32[16,1024]{1,0:T(8,128)S(1)}, f32[16,1024]{1,0:T(8,128)S(1)}, u32[]{:S(2)}, u32[]{:S(2)}) collective-permute-start(f32[16,1024]{1,0:T(8,128)S(1)} %get-tuple-element.55.refs_0_), channel_id=1, source_target_pairs={{0,1},{1,0},{2,3},{3,2},{4,5},{5,4},{6,7},{7,6},{8,9},{9,8},{10,11... | collective-permute-start | bytes 196616 | tf_op jit(solution)/shard_map/ppermute | solution.py:530
  18.4 4.8 %collective-permute-start.6 = (f32[16,1024]{1,0:T(8,128)S(1)}, f32[16,1024]{1,0:T(8,128)S(1)}, u32[]{:S(2)}, u32[]{:S(2)}) collective-permute-start(f32[16,1024]{1,0:T(8,128)S(1)} %get-tuple-element.59), channel_id=1, source_target_pairs={{0,4},{4,0},{8,12},{12,8},{1,5},{5,1},{9,13},{13,9},{2,6},{6,2},{1... | collective-permute-start | bytes 196616 | tf_op jit(solution)/shard_map/ppermute | solution.py:608
  20.5 13.6 %collective-permute-start.8 = (f32[64,512]{1,0:T(8,128)S(1)}, f32[64,512]{1,0:T(8,128)S(1)}, u32[]{:S(2)}, u32[]{:S(2)}) collective-permute-start(f32[64,512]{1,0:T(8,128)S(1)} %get-tuple-element.61), channel_id=1, source_target_pairs={{0,8},{4,12},{8,0},{12,4},{1,9},{5,13},{9,1},{13,5},{2,10},{6,14},... | collective-permute-start | bytes 393224 | tf_op jit(solution)/shard_map/ppermute | solution.py:609
  23.2 13.3 %collective-permute-start.7 = (f32[80,512]{1,0:T(8,128)S(1)}, f32[80,512]{1,0:T(8,128)S(1)}, u32[]{:S(2)}, u32[]{:S(2)}) collective-permute-start(f32[80,512]{1,0:T(8,128)S(1)} %onward_second.1), channel_id=1, source_target_pairs={{0,8},{4,12},{8,0},{12,4},{1,9},{5,13},{9,1},{13,5},{2,10},{6,14},... | collective-permute-start | bytes 491528 | tf_op jit(solution)/shard_map/ppermute | solution.py:610

commit v5 on v4

--- a/solution.py
+++ b/solution.py
@@ -59,8 +59,8 @@
     given = (tap_panel, tap_floor, tap_area)
 
     def body(press_hbm, *refs):
-        from_refs, sums_refs, kept = refs[: n + 3], refs[n + 3 : n + 3 + chunks], refs[n + 3 + chunks : -6]
-        press, panel, floor, area, weights, sems = refs[-6:]
+        from_refs, sums_ref, kept = refs[: n + 3], refs[n + 3], refs[n + 4 : 2 * n + 4]
+        press, panel, floor, area, weights, sems = refs[2 * n + 4 :]
         small = [
             pltpu.make_async_copy(a, b, sems.at[chunks + i])
             for i, (a, b) in enumerate(zip(from_refs, (panel, floor, area, *kept)))
@@ -82,15 +82,15 @@
         for i in range(chunks):
             at = slice(i * span, (i + 1) * span)
             large[i].wait()
-            sums_refs[i][...] = dot(weights[...], press[at], NT)
+            sums_ref[:, at] = dot(weights[...], press[at], NT)
         for copy in small[3:]:
             copy.wait()
 
     out = pl.pallas_call(
         body,
         in_specs=[pl.BlockSpec(memory_space=pltpu.HBM)] * (n + 4),
-        out_specs=tuple(whole(n + chunks)),
-        out_shape=(*[jax.ShapeDtypeStruct((rows, span), F32)] * chunks, *(jax.ShapeDtypeStruct(x.shape, x.dtype) for x in others)),
+        out_specs=tuple(whole(n + 1)),
+        out_shape=(jax.ShapeDtypeStruct((rows, time), F32), *(jax.ShapeDtypeStruct(x.shape, x.dtype) for x in others)),
         scratch_shapes=[
             pltpu.VMEM((time, taps), BF),
             *(pltpu.VMEM(x.shape, x.dtype) for x in given),
@@ -101,7 +101,7 @@
         cost_estimate=cost(3),
         name="tap_sums",
     )(in_hbm(pressures), *(in_hbm(x) for x in given), *(in_hbm(x) for x in others))
-    return out[:chunks], out[chunks:]
+    return out[0], out[1:]
 
 
 def placed(z, nz):
@@ -196,7 +196,6 @@
     rows, time = sums[0].shape
     nc = len(sums)
     mode_dev = slots // nz
-    plan = [(0, 1), (1, 1), (2, 2)] if nz == PAIRED else [(d, 1) for d in range(nz)]
     n = len(before)
 
     def body(*refs):
@@ -216,8 +215,8 @@
             for ref in sum_refs[1:]:
                 total = total + ref[:panels, cols]
             forces = dot_exact_left(left, total)
-            for ref, (p, count) in zip(out_refs, plan):
-                ref[:, cols] = forces[p * mode_dev : (p + count) * mode_dev]
+            for p, ref in enumerate(out_refs):
+                ref[:, cols] = forces[p * mode_dev : (p + 1) * mode_dev]
             new = []
             for part in (forces * tab_ref[0], forces * tab_ref[1]):
                 near = part[:, :TILE]
@@ -232,8 +231,8 @@
     out = pl.pallas_call(
         body,
         in_specs=whole(nc + 3 + n),
-        out_specs=whole(len(plan) + 3),
-        out_shape=[jax.ShapeDtypeStruct((count * mode_dev, time), F32) for _, count in plan]
+        out_specs=whole(nz + 3),
+        out_shape=[jax.ShapeDtypeStruct((mode_dev, time), F32)] * nz
         + [jax.ShapeDtypeStruct((rows - panels, time), F32)]
         + [jax.ShapeDtypeStruct((slots, TILE), F32)] * 2,
         compiler_params=params(),
@@ -324,7 +323,7 @@
     def body(motion_ref, ends_ref, enter_ref, tab_ref, fs_ref, *refs):
         out_ref = refs[n]
         if n:
-            refs[n + 1][...] = refs[0][...] + refs[1][refs[0].shape[0] :]
+            refs[n + 1][...] = refs[0][...] + refs[1][...]
         shape = fs_ref[...]
         turn = (ends_ref[2:3, :], ends_ref[3:4, :])
         later = lax.axis_index("tm") > 0
@@ -405,25 +404,21 @@
     return -(-(2 * floor_dev + 2) // 8) * 8
 
 
-def onward_second(two, arrived, share, share_arrived):
-    mode_dev, half = two.shape
+def share_onward(share, arrived):
     rows = share.shape[0]
 
-    def body(two_ref, arrived_ref, share_ref, share_arrived_ref, out_ref):
-        out_ref[:mode_dev] = two_ref[...] + arrived_ref[mode_dev:]
-        total = share_ref[...] + share_arrived_ref[rows:]
-        out_ref[mode_dev : mode_dev + rows] = total[:, :half]
-        out_ref[mode_dev + rows :] = total[:, half:]
-
-    return pl.pallas_call(
-        body,
-        in_specs=whole(4),
+    def body(share_ref, arrived_ref, out_ref):
+        out_ref[...] = share_ref[...] + arrived_ref[rows:]
+
+    return pl.pallas_call(
+        body,
+        in_specs=whole(2),
         out_specs=whole(1)[0],
-        out_shape=jax.ShapeDtypeStruct((mode_dev + 2 * rows, half), F32),
+        out_shape=jax.ShapeDtypeStruct(share.shape, F32),
         compiler_params=params(),
         cost_estimate=cost(1),
-        name="onward_second",
-    )(two, arrived, share, share_arrived)
+        name="share_onward",
+    )(share, arrived)
 
 
 def block_sums(force, tables, tri):
@@ -439,48 +434,15 @@
     return total
 
 
-def own_start(forces, tables, turns, until):
-    mode_dev = forces[0][0].shape[0]
-    n = len(forces)
-
-    def body(*refs):
-        tab_ref, turn_ref, resp_ref, state_ref = refs[n:]
-        turn = turn_ref[:mode_dev, 0:1], turn_ref[:mode_dev, 1:2]
-        tri = triangle()
-        state = None
-        for b in range(until // BLK):
-            cr, ci = block_sums(sum_at(refs, forces, b, mode_dev), (tab_ref[0], tab_ref[1]), tri)
-            if state is not None:
-                cr, ci = cr + state[0], ci + state[1]
-            resp_ref[:, b * BLK : (b + 1) * BLK] = tab_ref[2] * cr - tab_ref[3] * ci
-            state = turned(turn, (cr[:, BLK - 1 :], ci[:, BLK - 1 :]))
-        state_ref[:, 0:1], state_ref[:, 1:2] = state
-
-    return pl.pallas_call(
-        body,
-        in_specs=whole(n + 2),
-        out_specs=tuple(whole(2)),
-        out_shape=(
-            jax.ShapeDtypeStruct((mode_dev, until), F32),
-            jax.ShapeDtypeStruct((mode_dev, 2), F32),
-        ),
-        compiler_params=params(),
-        cost_estimate=cost(1),
-        name="own_start",
-    )(*(x for x, _, _ in forces), tables, turns)
-
-
-def own_response(forces, shares, tables, turns, floor_dev, load_scale, begun):
+def own_response(forces, shares, tables, turns, floor_dev, load_scale):
     mode_dev = forces[0][0].shape[0]
     rows = share_rows(floor_dev)
-    n, m, k = len(shares), len(forces), len(begun)
+    n, m = len(shares), len(forces)
     time = shares[0][0].shape[1]
     blocks = time // BLK
-    until = begun[0].shape[1] // BLK if begun else 0
 
     def body(*refs):
-        begun_refs = refs[m + n : m + n + k]
-        tab_ref, turn_ref, resp_ref, motion_ref, load_ref, share_ref = refs[m + n + k :]
+        tab_ref, turn_ref, resp_ref, motion_ref, load_ref, share_ref = refs[m + n :]
         for i, (x, row, start) in enumerate(shares):
             at = slice(start, start + x.shape[1])
             part = refs[m + i][row : row + rows]
@@ -494,25 +456,15 @@
         at = 2 * floor_dev
         state = column[:mode_dev, at : at + 1], column[:mode_dev, at + 1 : at + 2]
         tri = triangle()
-        sums = {
-            b: block_sums(sum_at(refs, forces, b, mode_dev), (tab_ref[0], tab_ref[1]), tri)
-            for b in range(until, blocks)
-        }
         for b in range(blocks):
-            cols = slice(b * BLK, (b + 1) * BLK)
-            if b < until:
-                resp_ref[:, cols] = begun_refs[0][:, cols] + (qr * state[0] - qi * state[1])
-                state = turned(turn, state)
-                if b == until - 1:
-                    state = state[0] + begun_refs[1][:, 0:1], state[1] + begun_refs[1][:, 1:2]
-            else:
-                cr, ci = (x + y for x, y in zip(sums[b], state))
-                resp_ref[:, cols] = qr * cr - qi * ci
-                state = turned(turn, (cr[:, BLK - 1 :], ci[:, BLK - 1 :]))
-
-    return pl.pallas_call(
-        body,
-        in_specs=whole(m + n + k + 2),
+            sums = block_sums(sum_at(refs, forces, b, mode_dev), (tab_ref[0], tab_ref[1]), tri)
+            cr, ci = (x + y for x, y in zip(sums, state))
+            resp_ref[:, b * BLK : (b + 1) * BLK] = qr * cr - qi * ci
+            state = turned(turn, (cr[:, BLK - 1 :], ci[:, BLK - 1 :]))
+
+    return pl.pallas_call(
+        body,
+        in_specs=whole(m + n + 2),
         out_specs=tuple(whole(3)),
         out_shape=(
             jax.ShapeDtypeStruct((mode_dev, time), F32),
@@ -523,7 +475,7 @@
         compiler_params=params(),
         cost_estimate=cost(1),
         name="own_response",
-    )(*(x for x, _, _ in forces), *(x for x, _, _ in shares), *begun, tables, turns)
+    )(*(x for x, _, _ in forces), *(x for x, _, _ in shares), tables, turns)
 
 
 def shifts(x, axis, n):
@@ -568,22 +520,21 @@
         panels,
         floors,
     )
-    sums = [[x] + shifts(x, "floors", nc) for x in mine]
+    sums = [[mine] + shifts(mine, "floors", nc)]
     pt, floor_slots, tables, turns, own = mode_tables(*kept, nz, nc)
     forces, loads, spread = [], [], []
     for part in sums:
         force, load, spread = slot_forces(part, pt, tables, turns, nz, spread)
         forces.append(force)
         loads.append(load)
-    half = time // 2
     span = time // len(forces)
     pair, two = ([(i, i ^ d) for i in range(nz)] for d in (1, 2))
     laid = [(x, p * mode_dev, k * span) for k, part in enumerate(forces) for p, x in enumerate(part)]
     if nz == PAIRED:
-        crossed = [lax.ppermute(part[2], "taps", pair) for part in forces]
-        onward = [forces[0][1], crossed[0]]
+        onward = [forces[0][1], lax.ppermute(forces[0][3], "taps", pair)]
+        direct = lax.ppermute(forces[0][2], "taps", pair)
     else:
-        crossed, onward = [(x, 0, k * span) for k, part in enumerate(forces) for x in along(part, nz)], []
+        crossed, onward = [(x, 0, 0) for x in along(forces[0], nz)], []
     motion = motion_from_rest(laid, tables, turns, floor_slots)
     ends = end_states(spread, turns, motion)
     enter = jnp.zeros_like(ends)
@@ -599,22 +550,17 @@
                 [*turned(over, (enter[0:1], enter[1:2])), jnp.zeros_like(ends[2:])]
             )
         enter = lax.ppermute(passed, "tm", [(i, (i + 1) % nt) for i in range(nt)])
-        enter = jnp.where(lax.axis_index("tm") > 0, enter, 0.0)
     motion, *onward = floor_shares(motion, ends, enter, tables, floor_slots, onward)
     motions = [motion] + shifts(motion, "floors", nc)
     shares = owner_shares(motions, loads, enter, nz, floor_dev)
     if nz == PAIRED:
-        rows = share_rows(floor_dev)
         other = lax.ppermute(shares[2], "taps", pair)
-        first = lax.ppermute(onward[0], "taps", two)
-        second = lax.ppermute(onward_second(forces[1][1], crossed[1], shares[1], other), "taps", two)
-        begun = own_start([(forces[0][0], 0, 0), (crossed[0], 0, 0), (first, 0, 0)], own, turns, half)
-        crossed = [(forces[1][0], 0, half), (crossed[1], 0, half), (second, 0, half)]
-        shares = [(shares[0], 0, 0), (other, 0, 0), (second, mode_dev, 0), (second, mode_dev + rows, half)]
+        last = lax.ppermute(share_onward(shares[1], other), "taps", two)
+        crossed = [(x, 0, 0) for x in (forces[0][0], direct, lax.ppermute(onward[0], "taps", two))]
+        shares = [(x, 0, 0) for x in (shares[0], other, last)]
     else:
-        begun = []
         shares = [(x, 0, 0) for x in along(shares, nz)]
-    return own_response(crossed, shares, own, turns, floor_dev, load_scale, begun)
+    return own_response(crossed, shares, own, turns, floor_dev, load_scale)
 
 
 def solution(mesh):

time: 38.1 us -> 36.2 us (0.950)
  waiting for transfers between devices: 13.7 us -> 12.3 us
  Pallas kernels: 10 us -> 9.36 us
    ppermute x4, waiting for transfers between devices: 10.6 us -> 3.44 us  [the longest x1 1.93 us: on_device(): last = lax.ppermute(share_onward(shares[1], other), 'taps', two)]
    ppermute x1, waiting for transfers between devices: 0.08 us -> 5.07 us  [on_device(): other = lax.ppermute(shares[2], 'taps', pair)]
    ppermute x4, starting transfers between devices: 9.26 us -> 10.1 us  [the longest x1 3.5 us: on_device(): last = lax.ppermute(share_onward(shares[1], other), 'taps', two)]
    ppermute x3 -> x2, waiting for transfers between devices: 1.25 us -> 2.06 us  [shifts(): lax.ppermute(x, axis, [(i, (i + d) % n) for i in range(n)])]
    pallas_call x5 -> x3, Pallas kernels: 2.88 us -> 2.22 us  [the longest x1 1.62 us: own_response(): pl.pallas_call(body, in_specs=whole(m + n + 2), out_specs=tuple(whole(3))...]
    ppermute x1, starting transfers between devices: 2.09 us -> 1.61 us  [on_device(): other = lax.ppermute(shares[2], 'taps', pair)]
  transfers between devices with their start and end apart: 9 -> 8, of which waited for: 6 -> 6; matrix products, arithmetic and copies ran while one was open for 0% -> 0% of each run, Pallas kernels for 14% -> 11%
where the time goes in v5:
time: 36.2 us; the launch traced here: 36 us
  starting transfers between devices  13.7 us (38%)
  waiting for transfers between devices  12.3 us (34%)
  Pallas kernels  9.36 us (26%)
  between operations  0.66 us (2%)
    ppermute x1, waiting for transfers between devices, on_device(): other = lax.ppermute(shares[2], 'taps', pair)  5.07 us
    ppermute x1, starting transfers between devices, on_device(): last = lax.ppermute(share_onward(shares[1], other), 'taps', two)  3.5 us
    pallas_call x1, Pallas kernels, tap_sums(): pl.pallas_call(body, in_specs=[pl.BlockSpec(memory_space=pltpu.HBM)] * (n...  3.29 us
    ppermute x1, starting transfers between devices, on_device(): lax.ppermute(onward[0], 'taps', two)  3.14 us
    ppermute x1, starting transfers between devices, on_device(): onward = [forces[0][1], lax.ppermute(forces[0][3], 'taps', pair)]  3 us
    ppermute x2, waiting for transfers between devices, shifts(): lax.ppermute(x, axis, [(i, (i + d) % n) for i in range(n)])  2.06 us
    ppermute x1, waiting for transfers between devices, on_device(): last = lax.ppermute(share_onward(shares[1], other), 'taps', two)  1.93 us
    ppermute x1, waiting for transfers between devices, on_device(): enter = lax.ppermute(passed, 'tm', [(i, (i + 1) % nt) for i in range(nt)])  1.71 us
  transfers between devices with their start and end apart: 8, of which 6 were waited for; matrix products, arithmetic and copies ran while one was open for 0% of the time, Pallas kernels for 11%

profile of v5, /device:TPU:0, one launch (start us, length us, event | category | flops | bytes accessed | tf_op | source)
XLA Modules:
  0.0 36.0 jit_solution(3989166962754563204)
XLA Ops:
  0.6 3.3 %tap_sums.1 = (f32[272,1024]{1,0:T(8,128)S(1)}, s32[1,512]{1,0:T(1,128)S(1)}, f32[1,512]{1,0:T(1,128)S(1)}, f32[1,512]{1,0:T(1,128)S(1)}, bf16[256,512]{1,0:T(8,128)(2,1)S(1)}, /*index=5*/bf16[16,512]{1,0:T(8,128)(2,1)S(1)}) custom-call(bf16[1024,2048]{1,0:T(8,128)(2,1)} %press_hbm.1, s32[1,2048]{1,0:T(1,128)} %bitcast.5, s32[1,2048]{1,0:T(1,128)} %bitcast.6, ...), custom_call_target="tpu_custom_call" | custom-call | flops 1500000000 | bytes 6000000 | tf_op jit(solution)/shard_map/tap_sums/pallas_call | solution.py:89
  3.9 0.5 %collective-permute-start = (f32[272,1024]{1,0:T(8,128)S(1)}, f32[272,1024]{1,0:T(8,128)S(1)}, u32[]{:S(2)}, u32[]{:S(2)}) collective-permute-start(f32[272,1024]{1,0:T(8,128)S(1)} %get-tuple-element.26.refs_0_), channel_id=1, source_target_pairs={{0,1},{1,0},{2,3},{3,2},{4,5},{5,4},{6,7},{7,6},{8,9},{9,8},{10,11... | collective-permute-start | bytes 3342344 | tf_op jit(solution)/shard_map/ppermute | solution.py:482
  4.4 1.6 %mode_tables.1 = (bf16[256,256]{1,0:T(8,128)(2,1)S(1)}, f32[16,256]{1,0:T(8,128)S(1)}, f32[4,256,256]{2,1,0:T(8,128)S(1)}, f32[256,2]{1,0:T(8,128)S(1)}, f32[4,64,256]{2,1,0:T(8,128)S(1)}) custom-call(s32[1,512]{1,0:T(1,128)S(1)} %get-tuple-element.27.refs_0_, f32[1,512]{1,0:T(1,128)S(1)} %get-tuple-element.28.refs_1_, ...), custom_call_target="tpu_custom_call" | custom-call | flops 1000000000 | bytes 4000000 | tf_op jit(solution)/shard_map/mode_tables/pallas_call | solution.py:176
  6.0 0.8 %collective-permute-done.refs_1_ = f32[272,1024]{1,0:T(8,128)S(1)} collective-permute-done((f32[272,1024]{1,0:T(8,128)S(1)}, f32[272,1024]{1,0:T(8,128)S(1)}, u32[]{:S(2)}, u32[]{:S(2)}) %collective-permute-start) | collective-permute-done | bytes 1114144 | tf_op jit(solution)/shard_map/ppermute | solution.py:482
  6.8 0.6 %slot_forces.1 = (f32[64,1024]{1,0:T(8,128)S(1)}, f32[64,1024]{1,0:T(8,128)S(1)}, f32[64,1024]{1,0:T(8,128)S(1)}, f32[64,1024]{1,0:T(8,128)S(1)}, f32[16,1024]{1...) custom-call(f32[272,1024]{1,0:T(8,128)S(1)} %get-tuple-element.26.refs_0_, ...), custom_call_target="tpu_custom_call" | custom-call | flops 500000000 | bytes 2000000 | tf_op jit(solution)/shard_map/slot_forces/pallas_call | solution.py:231
  7.4 3.0 %collective-permute-start.3 = (f32[64,1024]{1,0:T(8,128)S(1)}, f32[64,1024]{1,0:T(8,128)S(1)}, u32[]{:S(2)}, u32[]{:S(2)}) collective-permute-start(f32[64,1024]{1,0:T(8,128)S(1)} %get-tuple-element.38.refs_3_), channel_id=1, source_target_pairs={{0,4},{4,0},{8,12},{12,8},{1,5},{5,1},{9,13},{13,9},{2,6},{6,2},{1... | collective-permute-start | bytes 786440 | tf_op jit(solution)/shard_map/ppermute | solution.py:534
  10.4 1.5 %motion_from_rest.1.after_ref.motion_ref = f32[16,1024]{1,0:T(8,128)S(1)} custom-call(f32[64,1024]{1,0:T(8,128)S(1)} %get-tuple-element.35.refs_0_, f32[64,1024]{1,0:T(8,128)S(1)} %get-tuple-element.37.refs_1_.refs_0_, f32[64,1024]{1,0:T(8,128)S(1)} %get-tuple-element.36.refs_2_, f32[64,1024]{1,0:T(8,128)S(1)} %get-tuple-element.38.refs_3_, ...), custom_call_target="tpu_custom_call" | custom-call | flops 1000000000 | bytes 4000000 | tf_op jit(solution)/shard_map/motion_from_rest/pallas_call | solution.py:307
  11.9 0.4 %end_states.1.ends_ref = f32[8,256]{1,0:T(8,128)S(1)} custom-call(f32[256,128]{1,0:T(8,128)S(1)} %get-tuple-element.40.re_ref, f32[256,128]{1,0:T(8,128)S(1)} %get-tuple-element.41.im_ref, f32[256,2]{1,0:T(8,128)S(1)} %get-tuple-element.34.refs_4_.refs_5_.turn_ref.refs_7_, f32[16,1024]{1,0:T(8,128)S(1)} %motion_from_rest.1.after_ref.motion_ref), custom_call_target="tpu_custom_call" | custom-call | flops 500000000 | bytes 2000000 | tf_op jit(solution)/shard_map/end_states/pallas_call | solution.py:256
  12.3 1.5 %collective-permute-start.2 = (f32[8,256]{1,0:T(8,128)S(1)}, f32[8,256]{1,0:T(8,128)S(1)}, u32[]{:S(2)}, u32[]{:S(2)}) collective-permute-start(f32[8,256]{1,0:T(8,128)S(1)} %end_states.1.ends_ref), channel_id=1, source_target_pairs={{0,2},{2,0},{1,3},{3,1},{4,6},{6,4},{5,7},{7,5},{8,10},{10,8},{9,1... | collective-permute-start | bytes 24584 | tf_op jit(solution)/shard_map/ppermute | solution.py:552
  13.8 0.5 %collective-permute-start.1 = (f32[64,1024]{1,0:T(8,128)S(1)}, f32[64,1024]{1,0:T(8,128)S(1)}, u32[]{:S(2)}, u32[]{:S(2)}) collective-permute-start(f32[64,1024]{1,0:T(8,128)S(1)} %get-tuple-element.36.refs_2_), channel_id=1, source_target_pairs={{0,4},{4,0},{8,12},{12,8},{1,5},{5,1},{9,13},{13,9},{2,6},{6,2},{1... | collective-permute-start | bytes 786440 | tf_op jit(solution)/shard_map/ppermute | solution.py:535
  14.3 1.7 %collective-permute-done.2.enter_ref.refs_3_ = f32[8,256]{1,0:T(8,128)S(1)} collective-permute-done((f32[8,256]{1,0:T(8,128)S(1)}, f32[8,256]{1,0:T(8,128)S(1)}, u32[]{:S(2)}, u32[]{:S(2)}) %collective-permute-start.2) | collective-permute-done | bytes 8224 | tf_op jit(solution)/shard_map/ppermute | solution.py:552
  16.0 1.5 %collective-permute-done.3.refs_1_ = f32[64,1024]{1,0:T(8,128)S(1)} collective-permute-done((f32[64,1024]{1,0:T(8,128)S(1)}, f32[64,1024]{1,0:T(8,128)S(1)}, u32[]{:S(2)}, u32[]{:S(2)}) %collective-permute-start.3) | collective-permute-done | bytes 262176 | tf_op jit(solution)/shard_map/ppermute | solution.py:534
  17.5 0.3 floor_shares.1
  17.8 3.1 %collective-permute-start.4 = (f32[64,1024]{1,0:T(8,128)S(1)}, f32[64,1024]{1,0:T(8,128)S(1)}, u32[]{:S(2)}, u32[]{:S(2)}) collective-permute-start(f32[64,1024]{1,0:T(8,128)S(1)} %get-tuple-element.42), channel_id=1, source_target_pairs={{0,8},{4,12},{8,0},{12,4},{1,9},{5,13},{9,1},{13,5},{2,10},{6,14},... | collective-permute-start | bytes 786440 | tf_op jit(solution)/shard_map/ppermute | solution.py:559
  21.0 0.0 collective-permute-start.5
  21.0 1.3 %collective-permute-done.5.refs_1_ = f32[16,1024]{1,0:T(8,128)S(1)} collective-permute-done((f32[16,1024]{1,0:T(8,128)S(1)}, f32[16,1024]{1,0:T(8,128)S(1)}, u32[]{:S(2)}, u32[]{:S(2)}) %collective-permute-start.5) | collective-permute-done | bytes 65568 | tf_op jit(solution)/shard_map/ppermute | solution.py:482
  22.2 0.1 owner_shares.1
  22.3 1.6 %collective-permute-start.6 = (f32[16,1024]{1,0:T(8,128)S(1)}, f32[16,1024]{1,0:T(8,128)S(1)}, u32[]{:S(2)}, u32[]{:S(2)}) collective-permute-start(f32[16,1024]{1,0:T(8,128)S(1)} %get-tuple-element.46), channel_id=1, source_target_pairs={{0,4},{4,0},{8,12},{12,8},{1,5},{5,1},{9,13},{13,9},{2,6},{6,2},{1... | collective-permute-start | bytes 196616 | tf_op jit(solution)/shard_map/ppermute | solution.py:557
  23.9 5.1 %collective-permute-done.6.arrived_ref.refs_4_ = f32[16,1024]{1,0:T(8,128)S(1)} collective-permute-done((f32[16,1024]{1,0:T(8,128)S(1)}, f32[16,1024]{1,0:T(8,128)S(1)}, u32[]{:S(2)}, u32[]{:S(2)}) %collective-permute-start.6) | collective-permute-done | bytes 65568 | tf_op jit(solution)/shard_map/ppermute | solution.py:557
  29.0 3.5 %collective-permute-start.7 = (f32[8,1024]{1,0:T(8,128)S(1)}, f32[8,1024]{1,0:T(8,128)S(1)}, u32[]{:S(2)}, u32[]{:S(2)}) collective-permute-start(f32[8,1024]{1,0:T(8,128)S(1)} %share_onward.1), channel_id=1, source_target_pairs={{0,8},{4,12},{8,0},{12,4},{1,9},{5,13},{9,1},{13,5},{2,10},{6,14},... | collective-permute-start | bytes 98312 | tf_op jit(solution)/shard_map/ppermute | solution.py:558
  32.5 0.0 collective-permute-done.1.refs_1_
  32.5 1.9 %collective-permute-done.7.refs_5_ = f32[8,1024]{1,0:T(8,128)S(1)} collective-permute-done((f32[8,1024]{1,0:T(8,128)S(1)}, f32[8,1024]{1,0:T(8,128)S(1)}, u32[]{:S(2)}, u32[]{:S(2)}) %collective-permute-start.7) | collective-permute-done | bytes 32800 | tf_op jit(solution)/shard_map/ppermute | solution.py:558
  34.4 0.0 collective-permute-done.4.refs_2_
  34.4 1.6 %own_response.1 = (f32[64,1024]{1,0:T(8,128)}, f32[2,1024]{1,0:T(2,128)}, f32[2,1024]{1,0:T(2,128)}) custom-call(f32[64,1024]{1,0:T(8,128)S(1)} %get-tuple-element.35.refs_0_, f32[64,1024]{1,0:T(8,128)S(1)} %collective-permute-done.1.refs_1_, f32[64,1024]{1,0:T(8,128)S(1)} %collective-permute-done.4.refs_2_, f32[8,1024]{1,0:T(8,128)S(1)} %get-tuple-element.45.refs_3_, ...), custom_call_target="tpu_custom_call" | custom-call | flops 500000000 | bytes 2000000 | tf_op jit(solution)/shard_map/own_response/pallas_call | solution.py:465
  (1 shorter events, 0.0 us)
Async XLA Ops:
  3.9 2.9 %collective-permute-start = (f32[272,1024]{1,0:T(8,128)S(1)}, f32[272,1024]{1,0:T(8,128)S(1)}, u32[]{:S(2)}, u32[]{:S(2)}) collective-permute-start(f32[272,1024]{1,0:T(8,128)S(1)} %get-tuple-element.26.refs_0_), channel_id=1, source_target_pairs={{0,1},{1,0},{2,3},{3,2},{4,5},{5,4},{6,7},{7,6},{8,9},{9,8},{10,11... | collective-permute-start | bytes 3342344 | tf_op jit(solution)/shard_map/ppermute | solution.py:482
  7.4 10.1 %collective-permute-start.3 = (f32[64,1024]{1,0:T(8,128)S(1)}, f32[64,1024]{1,0:T(8,128)S(1)}, u32[]{:S(2)}, u32[]{:S(2)}) collective-permute-start(f32[64,1024]{1,0:T(8,128)S(1)} %get-tuple-element.38.refs_3_), channel_id=1, source_target_pairs={{0,4},{4,0},{8,12},{12,8},{1,5},{5,1},{9,13},{13,9},{2,6},{6,2},{1... | collective-permute-start | bytes 786440 | tf_op jit(solution)/shard_map/ppermute | solution.py:534
  12.3 3.7 %collective-permute-start.2 = (f32[8,256]{1,0:T(8,128)S(1)}, f32[8,256]{1,0:T(8,128)S(1)}, u32[]{:S(2)}, u32[]{:S(2)}) collective-permute-start(f32[8,256]{1,0:T(8,128)S(1)} %end_states.1.ends_ref), channel_id=1, source_target_pairs={{0,2},{2,0},{1,3},{3,1},{4,6},{6,4},{5,7},{7,5},{8,10},{10,8},{9,1... | collective-permute-start | bytes 24584 | tf_op jit(solution)/shard_map/ppermute | solution.py:552
  13.8 18.6 %collective-permute-start.1 = (f32[64,1024]{1,0:T(8,128)S(1)}, f32[64,1024]{1,0:T(8,128)S(1)}, u32[]{:S(2)}, u32[]{:S(2)}) collective-permute-start(f32[64,1024]{1,0:T(8,128)S(1)} %get-tuple-element.36.refs_2_), channel_id=1, source_target_pairs={{0,4},{4,0},{8,12},{12,8},{1,5},{5,1},{9,13},{13,9},{2,6},{6,2},{1... | collective-permute-start | bytes 786440 | tf_op jit(solution)/shard_map/ppermute | solution.py:535
  17.8 16.6 %collective-permute-start.4 = (f32[64,1024]{1,0:T(8,128)S(1)}, f32[64,1024]{1,0:T(8,128)S(1)}, u32[]{:S(2)}, u32[]{:S(2)}) collective-permute-start(f32[64,1024]{1,0:T(8,128)S(1)} %get-tuple-element.42), channel_id=1, source_target_pairs={{0,8},{4,12},{8,0},{12,4},{1,9},{5,13},{9,1},{13,5},{2,10},{6,14},... | collective-permute-start | bytes 786440 | tf_op jit(solution)/shard_map/ppermute | solution.py:559
  21.0 1.3 %collective-permute-start.5 = (f32[16,1024]{1,0:T(8,128)S(1)}, f32[16,1024]{1,0:T(8,128)S(1)}, u32[]{:S(2)}, u32[]{:S(2)}) collective-permute-start(f32[16,1024]{1,0:T(8,128)S(1)} %get-tuple-element.43.refs_0_), channel_id=1, source_target_pairs={{0,1},{1,0},{2,3},{3,2},{4,5},{5,4},{6,7},{7,6},{8,9},{9,8},{10,11... | collective-permute-start | bytes 196616 | tf_op jit(solution)/shard_map/ppermute | solution.py:482
  22.3 6.7 %collective-permute-start.6 = (f32[16,1024]{1,0:T(8,128)S(1)}, f32[16,1024]{1,0:T(8,128)S(1)}, u32[]{:S(2)}, u32[]{:S(2)}) collective-permute-start(f32[16,1024]{1,0:T(8,128)S(1)} %get-tuple-element.46), channel_id=1, source_target_pairs={{0,4},{4,0},{8,12},{12,8},{1,5},{5,1},{9,13},{13,9},{2,6},{6,2},{1... | collective-permute-start | bytes 196616 | tf_op jit(solution)/shard_map/ppermute | solution.py:557
  29.0 5.4 %collective-permute-start.7 = (f32[8,1024]{1,0:T(8,128)S(1)}, f32[8,1024]{1,0:T(8,128)S(1)}, u32[]{:S(2)}, u32[]{:S(2)}) collective-permute-start(f32[8,1024]{1,0:T(8,128)S(1)} %share_onward.1), channel_id=1, source_target_pairs={{0,8},{4,12},{8,0},{12,4},{1,9},{5,13},{9,1},{13,5},{2,10},{6,14},... | collective-permute-start | bytes 98312 | tf_op jit(solution)/shard_map/ppermute | solution.py:558

commit v6 on v5

--- a/solution.py
+++ b/solution.py
@@ -191,11 +191,23 @@
     )(order, decay, freq, panel_shape, floor_shape)
 
 
+def direct_until(time):
+    return time // 4 // BLK * BLK
+
+
+def send_plan(nz, time):
+    until = direct_until(time)
+    if nz != PAIRED or not until:
+        return [(p, 0, time) for p in range(nz)]
+    return [(0, 0, time), (1, until, time), (2, 0, time), (3, until, time), (1, 0, until), (3, 0, until)]
+
+
 def slot_forces(sums, pt, tables, turns, nz, before):
     slots, panels = pt.shape
     rows, time = sums[0].shape
     nc = len(sums)
     mode_dev = slots // nz
+    plan = send_plan(nz, time)
     n = len(before)
 
     def body(*refs):
@@ -215,8 +227,10 @@
             for ref in sum_refs[1:]:
                 total = total + ref[:panels, cols]
             forces = dot_exact_left(left, total)
-            for p, ref in enumerate(out_refs):
-                ref[:, cols] = forces[p * mode_dev : (p + 1) * mode_dev]
+            for ref, (p, start, stop) in zip(out_refs, plan):
+                if start <= b * BLK < stop:
+                    at = slice(b * BLK - start, (b + 1) * BLK - start)
+                    ref[:, at] = forces[p * mode_dev : (p + 1) * mode_dev]
             new = []
             for part in (forces * tab_ref[0], forces * tab_ref[1]):
                 near = part[:, :TILE]
@@ -231,8 +245,8 @@
     out = pl.pallas_call(
         body,
         in_specs=whole(nc + 3 + n),
-        out_specs=whole(nz + 3),
-        out_shape=[jax.ShapeDtypeStruct((mode_dev, time), F32)] * nz
+        out_specs=whole(len(plan) + 3),
+        out_shape=[jax.ShapeDtypeStruct((mode_dev, stop - start), F32) for _, start, stop in plan]
         + [jax.ShapeDtypeStruct((rows - panels, time), F32)]
         + [jax.ShapeDtypeStruct((slots, TILE), F32)] * 2,
         compiler_params=params(),
@@ -356,19 +370,28 @@
     )(motion, ends, enter, tables, floor_slots, *onward)
 
 
-def owner_shares(motions, loads, enter, nz, floor_dev):
+def owner_shares(motions, loads, enter, direct, begin, nz, floor_dev):
     nc, parts = len(motions), len(loads)
     floors, time = motions[0].shape
-    rows = share_rows(floor_dev)
+    rows, cols = share_shape(floor_dev, time)
     owners = nz * nc
     mode_dev = enter.shape[1] // nz
     span = time // parts
-    paired = nz == PAIRED
-    shapes = [(rows, time)] * 2 + [(2 * rows, time)] if paired else [(rows, time)] * nz
+    n, m = len(direct), len(begin)
+    half = time // 2
+    shapes = [(rows, cols)] * nz
+    if n:
+        shapes[2] = (mode_dev + 2 * rows, half)
+        shapes += [(mode_dev, half), begin[0].shape]
 
     def body(*refs):
         motion_refs, load_refs, enter_ref = refs[:nc], refs[nc : nc + parts], refs[nc + parts]
-        out_refs, motion_all, load_all = refs[nc + parts + 1 : -2], refs[-2], refs[-1]
+        more, out_refs = refs[nc + parts + 1 : nc + parts + 1 + n + m], refs[nc + parts + 1 + n + m : -3]
+        motion_all, load_all, share_ref = refs[-3:]
+        if n:
+            out_refs[2][:mode_dev] = more[0][:, :half]
+            out_refs[nz][...] = more[0][:, half:]
+            out_refs[nz + 1][...] = more[1][...] + more[2][...]
         z, c = lax.axis_index("taps"), lax.axis_index("floors")
         later = lax.axis_index("tm") > 0
         motion = motion_refs[0][...]
@@ -381,44 +404,33 @@
                 load_all[o, :, k * span : (k + 1) * span] = load_refs[k][at]
         for p, place in enumerate(placed(z, nz)):
             owner = place * nc + c
-            out = out_refs[2].at[(p - 2) * rows : (p - 1) * rows] if paired and p > 1 else out_refs[p]
-            out[...] = jnp.zeros((rows, time), F32)
-            out[:floor_dev] = motion_all[owner]
-            out[floor_dev : 2 * floor_dev] = load_all[owner]
+            out = share_ref if n and p == 2 else out_refs[p]
+            out[...] = jnp.zeros((rows, cols), F32)
+            for k, ref in enumerate((motion_all, load_all)):
+                for h in (0, 1):
+                    at = slice((2 * k + h) * floor_dev, (2 * k + h + 1) * floor_dev)
+                    out[at, :half] = ref[owner, :, h * half : (h + 1) * half]
             state = enter_ref[0:2, p * mode_dev : (p + 1) * mode_dev]
-            out[2 * floor_dev : 2 * floor_dev + 2, :mode_dev] = jnp.where(later, state, 0.0)
+            out[:2, half : half + mode_dev] = jnp.where(later, state, 0.0)
+        if n:
+            out_refs[2][mode_dev : mode_dev + rows] = share_ref[:, :half]
+            out_refs[2][mode_dev + rows :, :TILE] = share_ref[:, half:]
+            out_refs[2][mode_dev + rows :, TILE:] = jnp.zeros((rows, half - TILE), F32)
 
     return pl.pallas_call(
         body,
-        in_specs=whole(nc + parts + 1),
+        in_specs=whole(nc + parts + 1 + n + m),
         out_specs=whole(len(shapes)),
         out_shape=[jax.ShapeDtypeStruct(x, F32) for x in shapes],
-        scratch_shapes=[pltpu.VMEM((owners, floor_dev, time), F32)] * 2,
+        scratch_shapes=[pltpu.VMEM((owners, floor_dev, time), F32)] * 2 + [pltpu.VMEM((rows, cols), F32)],
         compiler_params=params(),
         cost_estimate=cost(1),
         name="owner_shares",
-    )(*motions, *loads, enter)
-
-
-def share_rows(floor_dev):
-    return -(-(2 * floor_dev + 2) // 8) * 8
-
-
-def share_onward(share, arrived):
-    rows = share.shape[0]
-
-    def body(share_ref, arrived_ref, out_ref):
-        out_ref[...] = share_ref[...] + arrived_ref[rows:]
-
-    return pl.pallas_call(
-        body,
-        in_specs=whole(2),
-        out_specs=whole(1)[0],
-        out_shape=jax.ShapeDtypeStruct(share.shape, F32),
-        compiler_params=params(),
-        cost_estimate=cost(1),
-        name="share_onward",
-    )(share, arrived)
+    )(*motions, *loads, enter, *direct, *begin)
+
+
+def share_shape(floor_dev, time):
+    return -(-4 * floor_dev // 8) * 8, time // 2 + TILE
 
 
 def block_sums(force, tables, tri):
@@ -436,25 +448,27 @@
 
 def own_response(forces, shares, tables, turns, floor_dev, load_scale):
     mode_dev = forces[0][0].shape[0]
-    rows = share_rows(floor_dev)
     n, m = len(shares), len(forces)
-    time = shares[0][0].shape[1]
+    half = shares[0][0].shape[1] - TILE
+    time = 2 * half
+    rows, width = share_shape(floor_dev, time)
     blocks = time // BLK
 
     def body(*refs):
         tab_ref, turn_ref, resp_ref, motion_ref, load_ref, share_ref = refs[m + n :]
-        for i, (x, row, start) in enumerate(shares):
-            at = slice(start, start + x.shape[1])
-            part = refs[m + i][row : row + rows]
+        for i, (_, row, start, stop) in enumerate(shares):
+            at = slice(start, stop)
+            part = refs[m + i][row : row + rows, : stop - start]
             share_ref[:, at] = part if i == 0 else share_ref[:, at] + part
         share = share_ref[...]
-        motion_ref[...] = share[:floor_dev]
-        load_ref[...] = share[floor_dev : 2 * floor_dev] * load_scale
+        for h in (0, 1):
+            at = slice(h * half, (h + 1) * half)
+            motion_ref[:, at] = share[h * floor_dev : (h + 1) * floor_dev, :half]
+            load_ref[:, at] = share[(2 + h) * floor_dev : (3 + h) * floor_dev, :half] * load_scale
         qr, qi = tab_ref[2], tab_ref[3]
         turn = turn_ref[:mode_dev, 0:1], turn_ref[:mode_dev, 1:2]
-        column = share[:, :TILE].T
-        at = 2 * floor_dev
-        state = column[:mode_dev, at : at + 1], column[:mode_dev, at + 1 : at + 2]
+        column = share[:, half:].T
+        state = column[:mode_dev, 0:1], column[:mode_dev, 1:2]
         tri = triangle()
         for b in range(blocks):
             sums = block_sums(sum_at(refs, forces, b, mode_dev), (tab_ref[0], tab_ref[1]), tri)
@@ -471,11 +485,11 @@
             jax.ShapeDtypeStruct((floor_dev, time), F32),
             jax.ShapeDtypeStruct((floor_dev, time), F32),
         ),
-        scratch_shapes=[pltpu.VMEM((rows, time), F32)],
+        scratch_shapes=[pltpu.VMEM((rows, width), F32)],
         compiler_params=params(),
         cost_estimate=cost(1),
         name="own_response",
-    )(*(x for x, _, _ in forces), *(x for x, _, _ in shares), tables, turns)
+    )(*(x for x, _, _ in forces), *(x[0] for x in shares), tables, turns)
 
 
 def shifts(x, axis, n):
@@ -527,16 +541,18 @@
         force, load, spread = slot_forces(part, pt, tables, turns, nz, spread)
         forces.append(force)
         loads.append(load)
-    span = time // len(forces)
-    pair, two = ([(i, i ^ d) for i in range(nz)] for d in (1, 2))
-    laid = [(x, p * mode_dev, k * span) for k, part in enumerate(forces) for p, x in enumerate(part)]
+    pair, two, mirror = ([(i, i ^ d) for i in range(nz)] for d in (1, 2, 3))
+    until = direct_until(time)
+    laid = [(x, p * mode_dev, start) for x, (p, start, _) in zip(forces[0], send_plan(nz, time))]
     if nz == PAIRED:
         onward = [forces[0][1], lax.ppermute(forces[0][3], "taps", pair)]
-        direct = lax.ppermute(forces[0][2], "taps", pair)
+        direct = [forces[0][2]]
+        begin = [lax.ppermute(x, "taps", way) for x, way in zip(forces[0][4:], (two, mirror))]
     else:
         crossed, onward = [(x, 0, 0) for x in along(forces[0], nz)], []
+        direct, begin = [], []
     motion = motion_from_rest(laid, tables, turns, floor_slots)
-    ends = end_states(spread, turns, motion)
+    ends = end_states(spread, turns, turns)
     enter = jnp.zeros_like(ends)
     for hop in range(nt - 1):
         passed = ends
@@ -552,14 +568,18 @@
         enter = lax.ppermute(passed, "tm", [(i, (i + 1) % nt) for i in range(nt)])
     motion, *onward = floor_shares(motion, ends, enter, tables, floor_slots, onward)
     motions = [motion] + shifts(motion, "floors", nc)
-    shares = owner_shares(motions, loads, enter, nz, floor_dev)
+    shares = owner_shares(motions, loads, enter, direct, begin, nz, floor_dev)
     if nz == PAIRED:
-        other = lax.ppermute(shares[2], "taps", pair)
-        last = lax.ppermute(share_onward(shares[1], other), "taps", two)
-        crossed = [(x, 0, 0) for x in (forces[0][0], direct, lax.ppermute(onward[0], "taps", two))]
-        shares = [(x, 0, 0) for x in (shares[0], other, last)]
+        ways = (two, pair, mirror, pair)
+        away, near, far, rest = (lax.ppermute(x, "taps", way) for x, way in zip(shares[1:5], ways))
+        onward = lax.ppermute(onward[0], "taps", two)
+        half, (rows, cols) = time // 2, share_shape(floor_dev, time)
+        crossed = [(forces[0][0], 0, 0), (near, 0, 0), (rest, 0, half)]
+        crossed += [(shares[5], 0, 0), (onward, 0, until)]
+        shares = [(x, 0, 0, cols) for x in (shares[0], away, far)]
+        shares += [(near, mode_dev, 0, half), (near, mode_dev + rows, half, cols)]
     else:
-        shares = [(x, 0, 0) for x in along(shares, nz)]
+        shares = [(x, 0, 0, x.shape[1]) for x in along(shares, nz)]
     return own_response(crossed, shares, own, turns, floor_dev, load_scale)
 
 

time: 36.2 us -> 35.8 us (0.989)
  waiting for transfers between devices: 12.3 us -> 9.03 us
  starting transfers between devices: 13.7 us -> 16.5 us
    ppermute x4 -> x7, starting transfers between devices: 8.7 us -> 11.4 us  [the longest x6 8.92 us: on_device(): lax.ppermute(x, 'taps', way)]
    ppermute x1, waiting for transfers between devices: 1.71 us -> 0.01 us  [on_device(): enter = lax.ppermute(passed, 'tm', [(i, (i + 1) % nt) for i in range(nt)])]
    ppermute x1, waiting for transfers between devices: 1.51 us -> 0.01 us  [on_device(): onward = [forces[0][1], lax.ppermute(forces[0][3], 'taps', pair)]]
    ppermute x2, waiting for transfers between devices: 2.06 us -> 0.81 us  [shifts(): lax.ppermute(x, axis, [(i, (i + d) % n) for i in range(n)])]
    ppermute x4 -> x7, waiting for transfers between devices: 7 us -> 8.22 us  [the longest x6 8.22 us: on_device(): lax.ppermute(x, 'taps', way)]
  transfers between devices with their start and end apart: 8 -> 11, of which waited for: 6 -> 5; matrix products, arithmetic and copies ran while one was open for 0% -> 0% of each run, Pallas kernels for 11% -> 11%
where the time goes in v6:
time: 35.8 us; the launch traced here: 35.6 us
  starting transfers between devices  16.5 us (46%)
  Pallas kernels  9.35 us (26%)
  waiting for transfers between devices  9.03 us (25%)
  between operations  0.67 us (2%)
    ppermute x6, starting transfers between devices, on_device(): lax.ppermute(x, 'taps', way)  8.92 us
    ppermute x6, waiting for transfers between devices, on_device(): lax.ppermute(x, 'taps', way)  8.22 us
    pallas_call x1, Pallas kernels, tap_sums(): pl.pallas_call(body, in_specs=[pl.BlockSpec(memory_space=pltpu.HBM)] * (n...  3.29 us
    ppermute x1, starting transfers between devices, on_device(): onward = [forces[0][1], lax.ppermute(forces[0][3], 'taps', pair)]  3 us
    ppermute x1, starting transfers between devices, on_device(): onward = lax.ppermute(onward[0], 'taps', two)  2.49 us
    pallas_call x1, Pallas kernels, own_response(): pl.pallas_call(body, in_specs=whole(m + n + 2), out_specs=tuple(whole(3))...  1.62 us
    pallas_call x1, Pallas kernels, mode_tables(): pl.pallas_call(body, in_specs=whole(5), out_specs=tuple(whole(5)), out_sh...  1.58 us
    ppermute x1, starting transfers between devices, on_device(): enter = lax.ppermute(passed, 'tm', [(i, (i + 1) % nt) for i in range(nt)])  1.53 us
  transfers between devices with their start and end apart: 11, of which 5 were waited for; matrix products, arithmetic and copies ran while one was open for 0% of the time, Pallas kernels for 11%

profile of v6, /device:TPU:0, one launch (start us, length us, event | category | flops | bytes accessed | tf_op | source)
XLA Modules:
  0.0 35.6 jit_solution(5878901102299523601)
XLA Ops:
  0.6 3.3 %tap_sums.1 = (f32[272,1024]{1,0:T(8,128)S(1)}, s32[1,512]{1,0:T(1,128)S(1)}, f32[1,512]{1,0:T(1,128)S(1)}, f32[1,512]{1,0:T(1,128)S(1)}, bf16[256,512]{1,0:T(8,128)(2,1)S(1)}, /*index=5*/bf16[16,512]{1,0:T(8,128)(2,1)S(1)}) custom-call(bf16[1024,2048]{1,0:T(8,128)(2,1)} %press_hbm.1, s32[1,2048]{1,0:T(1,128)} %bitcast.5, s32[1,2048]{1,0:T(1,128)} %bitcast.6, ...), custom_call_target="tpu_custom_call" | custom-call | flops 1500000000 | bytes 6000000 | tf_op jit(solution)/shard_map/tap_sums/pallas_call | solution.py:89
  3.9 0.5 %collective-permute-start = (f32[272,1024]{1,0:T(8,128)S(1)}, f32[272,1024]{1,0:T(8,128)S(1)}, u32[]{:S(2)}, u32[]{:S(2)}) collective-permute-start(f32[272,1024]{1,0:T(8,128)S(1)} %get-tuple-element.31.refs_0_), channel_id=1, source_target_pairs={{0,1},{1,0},{2,3},{3,2},{4,5},{5,4},{6,7},{7,6},{8,9},{9,8},{10,11... | collective-permute-start | bytes 3342344 | tf_op jit(solution)/shard_map/ppermute | solution.py:496
  4.4 1.6 %mode_tables.1 = (bf16[256,256]{1,0:T(8,128)(2,1)S(1)}, f32[16,256]{1,0:T(8,128)S(1)}, f32[4,256,256]{2,1,0:T(8,128)S(1)}, f32[256,2]{1,0:T(8,128)S(1)}, f32[4,64,256]{2,1,0:T(8,128)S(1)}) custom-call(s32[1,512]{1,0:T(1,128)S(1)} %get-tuple-element.32.refs_0_, f32[1,512]{1,0:T(1,128)S(1)} %get-tuple-element.33.refs_1_, ...), custom_call_target="tpu_custom_call" | custom-call | flops 1000000000 | bytes 4000000 | tf_op jit(solution)/shard_map/mode_tables/pallas_call | solution.py:176
  6.0 0.8 %collective-permute-done.refs_1_ = f32[272,1024]{1,0:T(8,128)S(1)} collective-permute-done((f32[272,1024]{1,0:T(8,128)S(1)}, f32[272,1024]{1,0:T(8,128)S(1)}, u32[]{:S(2)}, u32[]{:S(2)}) %collective-permute-start) | collective-permute-done | bytes 1114144 | tf_op jit(solution)/shard_map/ppermute | solution.py:496
  6.8 0.6 %slot_forces.1 = (f32[64,1024]{1,0:T(8,128)S(1)}, f32[64,768]{1,0:T(8,128)S(1)}, f32[64,1024]{1,0:T(8,128)S(1)}, f32[64,768]{1,0:T(8,128)S(1)}, f32[64,256]{1,0:...) custom-call(f32[272,1024]{1,0:T(8,128)S(1)} %get-tuple-element.31.re, ...), custom_call_target="tpu_custom_call" | custom-call | flops 500000000 | bytes 2000000 | tf_op jit(solution)/shard_map/slot_forces/pallas_call | solution.py:245
  7.4 3.0 %collective-permute-start.2 = (f32[64,768]{1,0:T(8,128)S(1)}, f32[64,768]{1,0:T(8,128)S(1)}, u32[]{:S(2)}, u32[]{:S(2)}) collective-permute-start(f32[64,768]{1,0:T(8,128)S(1)} %get-tuple-element.43.refs_3_), channel_id=1, source_target_pairs={{0,4},{4,0},{8,12},{12,8},{1,5},{5,1},{9,13},{13,9},{2,6},{6,2},{1... | collective-permute-start | bytes 589832 | tf_op jit(solution)/shard_map/ppermute | solution.py:548
  10.4 0.4 %end_states.1.ends_ref = f32[8,256]{1,0:T(8,128)S(1)} custom-call(f32[256,128]{1,0:T(8,128)S(1)} %get-tuple-element.47.re_ref, f32[256,128]{1,0:T(8,128)S(1)} %get-tuple-element.48.im_ref, f32[256,2]{1,0:T(8,128)S(1)} %get-tuple-element.39.refs_4_.refs_7_.turn_ref.after_ref.refs_11_, f32[256,2]{1,0:T(8,128)S(1)} %get-tuple-element.39.refs_4_.refs_7_.turn_ref.after_ref.refs_11_), custom_call_target="tpu_custom_call" | custom-call | flops 500000000 | bytes 2000000 | tf_op jit(solution)/shard_map/end_states/pallas_call | solution.py:270
  10.8 1.5 %collective-permute-start.1 = (f32[8,256]{1,0:T(8,128)S(1)}, f32[8,256]{1,0:T(8,128)S(1)}, u32[]{:S(2)}, u32[]{:S(2)}) collective-permute-start(f32[8,256]{1,0:T(8,128)S(1)} %end_states.1.ends_ref), channel_id=1, source_target_pairs={{0,2},{2,0},{1,3},{3,1},{4,6},{6,4},{5,7},{7,5},{8,10},{10,8},{9,1... | collective-permute-start | bytes 24584 | tf_op jit(solution)/shard_map/ppermute | solution.py:568
  12.4 2.6 %collective-permute-start.4 = (f32[64,256]{1,0:T(8,128)S(1)}, f32[64,256]{1,0:T(8,128)S(1)}, u32[]{:S(2)}, u32[]{:S(2)}) collective-permute-start(f32[64,256]{1,0:T(8,128)S(1)} %get-tuple-element.44.refs_4_), channel_id=1, source_target_pairs={{0,8},{4,12},{8,0},{12,4},{1,9},{5,13},{9,1},{13,5},{2,10},{6,14},... | collective-permute-start | bytes 196616 | tf_op jit(solution)/shard_map/ppermute | solution.py:550
  15.0 0.2 collective-permute-start.5
  15.2 1.5 %motion_from_rest.1.motion_ref = f32[16,1024]{1,0:T(8,128)S(1)} custom-call(f32[64,1024]{1,0:T(8,128)S(1)} %get-tuple-element.40.refs_0_, f32[64,768]{1,0:T(8,128)S(1)} %get-tuple-element.41.refs_1_.refs_0_, f32[64,1024]{1,0:T(8,128)S(1)} %get-tuple-element.42.refs_2_.refs_4_, f32[64,768]{1,0:T(8,128)S(1)} %get-tuple-element.43.refs_3_, ...), custom_call_target="tpu_custom_call" | custom-call | flops 1000000000 | bytes 4000000 | tf_op jit(solution)/shard_map/motion_from_rest/pallas_call | solution.py:321
  16.6 0.0 collective-permute-done.1.enter_ref.refs_3_
  16.7 0.0 collective-permute-done.2.refs_1_
  16.7 0.3 floor_shares.1
  17.0 0.1 collective-permute-start.3
  17.1 2.5 %collective-permute-start.8 = (f32[64,768]{1,0:T(8,128)S(1)}, f32[64,768]{1,0:T(8,128)S(1)}, u32[]{:S(2)}, u32[]{:S(2)}) collective-permute-start(f32[64,768]{1,0:T(8,128)S(1)} %get-tuple-element.54), channel_id=1, source_target_pairs={{0,8},{4,12},{8,0},{12,4},{1,9},{5,13},{9,1},{13,5},{2,10},{6,14},... | collective-permute-start | bytes 589832 | tf_op jit(solution)/shard_map/ppermute | solution.py:575
  19.5 0.7 %collective-permute-done.4.refs_5_ = f32[64,256]{1,0:T(8,128)S(1)} collective-permute-done((f32[64,256]{1,0:T(8,128)S(1)}, f32[64,256]{1,0:T(8,128)S(1)}, u32[]{:S(2)}, u32[]{:S(2)}) %collective-permute-start.4) | collective-permute-done | bytes 65568 | tf_op jit(solution)/shard_map/ppermute | solution.py:550
  20.3 0.8 %collective-permute-done.5.refs_6_ = f32[64,256]{1,0:T(8,128)S(1)} collective-permute-done((f32[64,256]{1,0:T(8,128)S(1)}, f32[64,256]{1,0:T(8,128)S(1)}, u32[]{:S(2)}, u32[]{:S(2)}) %collective-permute-start.5) | collective-permute-done | bytes 65568 | tf_op jit(solution)/shard_map/ppermute | solution.py:550
  21.1 0.0 collective-permute-done.3.refs_1_
  21.1 0.1 owner_shares.1
  21.2 1.7 %collective-permute-start.6 = (f32[80,512]{1,0:T(8,128)S(1)}, f32[80,512]{1,0:T(8,128)S(1)}, u32[]{:S(2)}, u32[]{:S(2)}) collective-permute-start(f32[80,512]{1,0:T(8,128)S(1)} %get-tuple-element.51), channel_id=1, source_target_pairs={{0,4},{4,0},{8,12},{12,8},{1,5},{5,1},{9,13},{13,9},{2,6},{6,2},{1... | collective-permute-start | bytes 491528 | tf_op jit(solution)/shard_map/ppermute | solution.py:574
  22.9 0.4 %collective-permute-start.7 = (f32[64,512]{1,0:T(8,128)S(1)}, f32[64,512]{1,0:T(8,128)S(1)}, u32[]{:S(2)}, u32[]{:S(2)}) collective-permute-start(f32[64,512]{1,0:T(8,128)S(1)} %get-tuple-element.52), channel_id=1, source_target_pairs={{0,4},{4,0},{8,12},{12,8},{1,5},{5,1},{9,13},{13,9},{2,6},{6,2},{1... | collective-permute-start | bytes 393224 | tf_op jit(solution)/shard_map/ppermute | solution.py:574
  23.3 1.6 %collective-permute-start.9 = (f32[8,640]{1,0:T(8,128)S(1)}, f32[8,640]{1,0:T(8,128)S(1)}, u32[]{:S(2)}, u32[]{:S(2)}) collective-permute-start(f32[8,640]{1,0:T(8,128)S(1)} %get-tuple-element.56), channel_id=1, source_target_pairs={{0,8},{4,12},{8,0},{12,4},{1,9},{5,13},{9,1},{13,5},{2,10},{6,14},... | collective-permute-start | bytes 61448 | tf_op jit(solution)/shard_map/ppermute | solution.py:574
  24.8 2.5 %collective-permute-start.10 = (f32[8,640]{1,0:T(8,128)S(1)}, f32[8,640]{1,0:T(8,128)S(1)}, u32[]{:S(2)}, u32[]{:S(2)}) collective-permute-start(f32[8,640]{1,0:T(8,128)S(1)} %get-tuple-element.57), channel_id=1, source_target_pairs={{0,12},{4,8},{8,4},{12,0},{1,13},{5,9},{9,5},{13,1},{2,14},{6,10},... | collective-permute-start | bytes 61448 | tf_op jit(solution)/shard_map/ppermute | solution.py:574
  27.3 4.1 %collective-permute-done.9.refs_6_ = f32[8,640]{1,0:T(8,128)S(1)} collective-permute-done((f32[8,640]{1,0:T(8,128)S(1)}, f32[8,640]{1,0:T(8,128)S(1)}, u32[]{:S(2)}, u32[]{:S(2)}) %collective-permute-start.9) | collective-permute-done | bytes 20512 | tf_op jit(solution)/shard_map/ppermute | solution.py:574
  31.3 2.6 %collective-permute-done.10.refs_7_ = f32[8,640]{1,0:T(8,128)S(1)} collective-permute-done((f32[8,640]{1,0:T(8,128)S(1)}, f32[8,640]{1,0:T(8,128)S(1)}, u32[]{:S(2)}, u32[]{:S(2)}) %collective-permute-start.10) | collective-permute-done | bytes 20512 | tf_op jit(solution)/shard_map/ppermute | solution.py:574
  33.9 0.0 collective-permute-done.7.refs_2_
  34.0 0.0 collective-permute-done.8.refs_4_
  34.0 0.0 collective-permute-done.6.refs_1_.refs_8_.refs_9_
  34.0 1.6 %own_response.1 = (f32[64,1024]{1,0:T(8,128)}, f32[2,1024]{1,0:T(2,128)}, f32[2,1024]{1,0:T(2,128)}) custom-call(f32[64,1024]{1,0:T(8,128)S(1)} %get-tuple-element.40.refs_0_, f32[80,512]{1,0:T(8,128)S(1)} %collective-permute-done.6.refs_1_.refs_8_.refs_9_, f32[64,512]{1,0:T(8,128)S(1)} %collective-permute-done.7.refs_2_, ...), custom_call_target="tpu_custom_call" | custom-call | flops 500000000 | bytes 2000000 | tf_op jit(solution)/shard_map/own_response/pallas_call | solution.py:479
Async XLA Ops:
  3.9 2.9 %collective-permute-start = (f32[272,1024]{1,0:T(8,128)S(1)}, f32[272,1024]{1,0:T(8,128)S(1)}, u32[]{:S(2)}, u32[]{:S(2)}) collective-permute-start(f32[272,1024]{1,0:T(8,128)S(1)} %get-tuple-element.31.refs_0_), channel_id=1, source_target_pairs={{0,1},{1,0},{2,3},{3,2},{4,5},{5,4},{6,7},{7,6},{8,9},{9,8},{10,11... | collective-permute-start | bytes 3342344 | tf_op jit(solution)/shard_map/ppermute | solution.py:496
  7.4 9.2 %collective-permute-start.2 = (f32[64,768]{1,0:T(8,128)S(1)}, f32[64,768]{1,0:T(8,128)S(1)}, u32[]{:S(2)}, u32[]{:S(2)}) collective-permute-start(f32[64,768]{1,0:T(8,128)S(1)} %get-tuple-element.43.refs_3_), channel_id=1, source_target_pairs={{0,4},{4,0},{8,12},{12,8},{1,5},{5,1},{9,13},{13,9},{2,6},{6,2},{1... | collective-permute-start | bytes 589832 | tf_op jit(solution)/shard_map/ppermute | solution.py:548
  10.8 5.8 %collective-permute-start.1 = (f32[8,256]{1,0:T(8,128)S(1)}, f32[8,256]{1,0:T(8,128)S(1)}, u32[]{:S(2)}, u32[]{:S(2)}) collective-permute-start(f32[8,256]{1,0:T(8,128)S(1)} %end_states.1.ends_ref), channel_id=1, source_target_pairs={{0,2},{2,0},{1,3},{3,1},{4,6},{6,4},{5,7},{7,5},{8,10},{10,8},{9,1... | collective-permute-start | bytes 24584 | tf_op jit(solution)/shard_map/ppermute | solution.py:568
  12.4 7.9 %collective-permute-start.4 = (f32[64,256]{1,0:T(8,128)S(1)}, f32[64,256]{1,0:T(8,128)S(1)}, u32[]{:S(2)}, u32[]{:S(2)}) collective-permute-start(f32[64,256]{1,0:T(8,128)S(1)} %get-tuple-element.44.refs_4_), channel_id=1, source_target_pairs={{0,8},{4,12},{8,0},{12,4},{1,9},{5,13},{9,1},{13,5},{2,10},{6,14},... | collective-permute-start | bytes 196616 | tf_op jit(solution)/shard_map/ppermute | solution.py:550
  15.0 6.1 %collective-permute-start.5 = (f32[64,256]{1,0:T(8,128)S(1)}, f32[64,256]{1,0:T(8,128)S(1)}, u32[]{:S(2)}, u32[]{:S(2)}) collective-permute-start(f32[64,256]{1,0:T(8,128)S(1)} %get-tuple-element.45.refs_5_), channel_id=1, source_target_pairs={{0,12},{4,8},{8,4},{12,0},{1,13},{5,9},{9,5},{13,1},{2,14},{6,10},... | collective-permute-start | bytes 196616 | tf_op jit(solution)/shard_map/ppermute | solution.py:550
  17.0 4.1 %collective-permute-start.3 = (f32[16,1024]{1,0:T(8,128)S(1)}, f32[16,1024]{1,0:T(8,128)S(1)}, u32[]{:S(2)}, u32[]{:S(2)}) collective-permute-start(f32[16,1024]{1,0:T(8,128)S(1)} %get-tuple-element.49.refs_0_), channel_id=1, source_target_pairs={{0,1},{1,0},{2,3},{3,2},{4,5},{5,4},{6,7},{7,6},{8,9},{9,8},{10,11... | collective-permute-start | bytes 196616 | tf_op jit(solution)/shard_map/ppermute | solution.py:496
  17.1 16.9 %collective-permute-start.8 = (f32[64,768]{1,0:T(8,128)S(1)}, f32[64,768]{1,0:T(8,128)S(1)}, u32[]{:S(2)}, u32[]{:S(2)}) collective-permute-start(f32[64,768]{1,0:T(8,128)S(1)} %get-tuple-element.54), channel_id=1, source_target_pairs={{0,8},{4,12},{8,0},{12,4},{1,9},{5,13},{9,1},{13,5},{2,10},{6,14},... | collective-permute-start | bytes 589832 | tf_op jit(solution)/shard_map/ppermute | solution.py:575
  21.2 12.8 %collective-permute-start.6 = (f32[80,512]{1,0:T(8,128)S(1)}, f32[80,512]{1,0:T(8,128)S(1)}, u32[]{:S(2)}, u32[]{:S(2)}) collective-permute-start(f32[80,512]{1,0:T(8,128)S(1)} %get-tuple-element.51), channel_id=1, source_target_pairs={{0,4},{4,0},{8,12},{12,8},{1,5},{5,1},{9,13},{13,9},{2,6},{6,2},{1... | collective-permute-start | bytes 491528 | tf_op jit(solution)/shard_map/ppermute | solution.py:574
  22.9 11.1 %collective-permute-start.7 = (f32[64,512]{1,0:T(8,128)S(1)}, f32[64,512]{1,0:T(8,128)S(1)}, u32[]{:S(2)}, u32[]{:S(2)}) collective-permute-start(f32[64,512]{1,0:T(8,128)S(1)} %get-tuple-element.52), channel_id=1, source_target_pairs={{0,4},{4,0},{8,12},{12,8},{1,5},{5,1},{9,13},{13,9},{2,6},{6,2},{1... | collective-permute-start | bytes 393224 | tf_op jit(solution)/shard_map/ppermute | solution.py:574
  23.3 8.1 %collective-permute-start.9 = (f32[8,640]{1,0:T(8,128)S(1)}, f32[8,640]{1,0:T(8,128)S(1)}, u32[]{:S(2)}, u32[]{:S(2)}) collective-permute-start(f32[8,640]{1,0:T(8,128)S(1)} %get-tuple-element.56), channel_id=1, source_target_pairs={{0,8},{4,12},{8,0},{12,4},{1,9},{5,13},{9,1},{13,5},{2,10},{6,14},... | collective-permute-start | bytes 61448 | tf_op jit(solution)/shard_map/ppermute | solution.py:574
  24.8 9.1 %collective-permute-start.10 = (f32[8,640]{1,0:T(8,128)S(1)}, f32[8,640]{1,0:T(8,128)S(1)}, u32[]{:S(2)}, u32[]{:S(2)}) collective-permute-start(f32[8,640]{1,0:T(8,128)S(1)} %get-tuple-element.57), channel_id=1, source_target_pairs={{0,12},{4,8},{8,4},{12,0},{1,13},{5,9},{9,5},{13,1},{2,14},{6,10},... | collective-permute-start | bytes 61448 | tf_op jit(solution)/shard_map/ppermute | solution.py:574

commit v7 on v6

--- a/solution.py
+++ b/solution.py
@@ -300,7 +300,7 @@
         tab_ref, turn_ref, fs_ref, motion_ref = refs[n:]
         tri = triangle()
         here = fs_ref[...].astype(BF)
-        turn = turn_ref[:, 0:1], turn_ref[:, 1:2]
+        turn = [spread(turn_ref[:, i : i + 1]) for i in (0, 1)]
         state = None
         for b in range(blocks):
             found = [
@@ -309,14 +309,14 @@
                 if start <= b * BLK < start + shape[1]
             ]
             force = jnp.concatenate([x for _, x in sorted(found, key=lambda f: f[0])], axis=0)
-            cr = dot_exact_right(force * tab_ref[0], tri)
-            ci = dot_exact_right(force * tab_ref[1], tri)
+            cr, ci = block_sums(force, (tab_ref[0], tab_ref[1]), tri)
+            last = [spread(x[:, BLK - 1 :]) for x in (cr, ci)]
             if state is not None:
-                cr, ci = cr + state[0], ci + state[1]
+                cr, ci = cr + widened(state[0]), ci + widened(state[1])
+                last = [x + y for x, y in zip(last, state)]
             part = dot_exact_left(here, tab_ref[2] * cr - tab_ref[3] * ci)
             motion_ref[:, b * BLK : (b + 1) * BLK] = part
-            if b < blocks - 1:
-                state = turned(turn, (cr[:, BLK - 1 :], ci[:, BLK - 1 :]))
+            state = turned(turn, last)
 
     return pl.pallas_call(
         body,
@@ -433,6 +433,14 @@
     return -(-4 * floor_dev // 8) * 8, time // 2 + TILE
 
 
+def spread(column):
+    return jnp.broadcast_to(column, (column.shape[0], TILE))
+
+
+def widened(tile):
+    return jnp.concatenate([tile] * (BLK // TILE), axis=1)
+
+
 def block_sums(force, tables, tri):
     return [dot_exact_right(force * table, tri) for table in tables]
 
@@ -466,15 +474,18 @@
             motion_ref[:, at] = share[h * floor_dev : (h + 1) * floor_dev, :half]
             load_ref[:, at] = share[(2 + h) * floor_dev : (3 + h) * floor_dev, :half] * load_scale
         qr, qi = tab_ref[2], tab_ref[3]
-        turn = turn_ref[:mode_dev, 0:1], turn_ref[:mode_dev, 1:2]
+        turn = [spread(turn_ref[:mode_dev, i : i + 1]) for i in (0, 1)]
         column = share[:, half:].T
-        state = column[:mode_dev, 0:1], column[:mode_dev, 1:2]
+        state = [spread(column[:mode_dev, i : i + 1]) for i in (0, 1)]
         tri = triangle()
+        sums = [
+            block_sums(sum_at(refs, forces, b, mode_dev), (tab_ref[0], tab_ref[1]), tri)
+            for b in range(blocks)
+        ]
         for b in range(blocks):
-            sums = block_sums(sum_at(refs, forces, b, mode_dev), (tab_ref[0], tab_ref[1]), tri)
-            cr, ci = (x + y for x, y in zip(sums, state))
+            cr, ci = (x + widened(y) for x, y in zip(sums[b], state))
             resp_ref[:, b * BLK : (b + 1) * BLK] = qr * cr - qi * ci
-            state = turned(turn, (cr[:, BLK - 1 :], ci[:, BLK - 1 :]))
+            state = turned(turn, [spread(x[:, BLK - 1 :]) + y for x, y in zip(sums[b], state)])
 
     return pl.pallas_call(
         body,

time: 35.8 us -> 35.4 us (0.989)
  Pallas kernels: 9.35 us -> 8.95 us
    pallas_call x1, Pallas kernels: 1.62 us -> 1.22 us  [own_response(): pl.pallas_call(body, in_specs=whole(m + n + 2), out_specs=tuple(whole(3))...]
where the time goes in v7:
time: 35.4 us; the launch traced here: 35.2 us
  starting transfers between devices  16.5 us (47%)
  waiting for transfers between devices  9.03 us (26%)
  Pallas kernels  8.95 us (25%)
  between operations  0.67 us (2%)
    ppermute x6, starting transfers between devices, on_device(): lax.ppermute(x, 'taps', way)  8.92 us
    ppermute x6, waiting for transfers between devices, on_device(): lax.ppermute(x, 'taps', way)  8.22 us
    pallas_call x1, Pallas kernels, tap_sums(): pl.pallas_call(body, in_specs=[pl.BlockSpec(memory_space=pltpu.HBM)] * (n...  3.29 us
    ppermute x1, starting transfers between devices, on_device(): onward = [forces[0][1], lax.ppermute(forces[0][3], 'taps', pair)]  3 us
    ppermute x1, starting transfers between devices, on_device(): onward = lax.ppermute(onward[0], 'taps', two)  2.49 us
    pallas_call x1, Pallas kernels, mode_tables(): pl.pallas_call(body, in_specs=whole(5), out_specs=tuple(whole(5)), out_sh...  1.58 us
    ppermute x1, starting transfers between devices, on_device(): enter = lax.ppermute(passed, 'tm', [(i, (i + 1) % nt) for i in range(nt)])  1.53 us
    pallas_call x1, Pallas kernels, motion_from_rest(): pl.pallas_call(body, in_specs=whole(n + 3), out_specs=whole(1)[0], out_sh...  1.46 us
  transfers between devices with their start and end apart: 11, of which 5 were waited for; matrix products, arithmetic and copies ran while one was open for 0% of the time, Pallas kernels for 11%

profile of v7, /device:TPU:0, one launch (start us, length us, event | category | flops | bytes accessed | tf_op | source)
XLA Modules:
  0.0 35.2 jit_solution(13472363092609011550)
XLA Ops:
  0.6 3.3 %tap_sums.1 = (f32[272,1024]{1,0:T(8,128)S(1)}, s32[1,512]{1,0:T(1,128)S(1)}, f32[1,512]{1,0:T(1,128)S(1)}, f32[1,512]{1,0:T(1,128)S(1)}, bf16[256,512]{1,0:T(8,128)(2,1)S(1)}, /*index=5*/bf16[16,512]{1,0:T(8,128)(2,1)S(1)}) custom-call(bf16[1024,2048]{1,0:T(8,128)(2,1)} %press_hbm.1, s32[1,2048]{1,0:T(1,128)} %bitcast.5, s32[1,2048]{1,0:T(1,128)} %bitcast.6, ...), custom_call_target="tpu_custom_call" | custom-call | flops 1500000000 | bytes 6000000 | tf_op jit(solution)/shard_map/tap_sums/pallas_call | solution.py:89
  3.9 0.5 %collective-permute-start = (f32[272,1024]{1,0:T(8,128)S(1)}, f32[272,1024]{1,0:T(8,128)S(1)}, u32[]{:S(2)}, u32[]{:S(2)}) collective-permute-start(f32[272,1024]{1,0:T(8,128)S(1)} %get-tuple-element.31.refs_0_), channel_id=1, source_target_pairs={{0,1},{1,0},{2,3},{3,2},{4,5},{5,4},{6,7},{7,6},{8,9},{9,8},{10,11... | collective-permute-start | bytes 3342344 | tf_op jit(solution)/shard_map/ppermute | solution.py:507
  4.4 1.6 %mode_tables.1 = (bf16[256,256]{1,0:T(8,128)(2,1)S(1)}, f32[16,256]{1,0:T(8,128)S(1)}, f32[4,256,256]{2,1,0:T(8,128)S(1)}, f32[256,2]{1,0:T(8,128)S(1)}, f32[4,64,256]{2,1,0:T(8,128)S(1)}) custom-call(s32[1,512]{1,0:T(1,128)S(1)} %get-tuple-element.32.refs_0_, f32[1,512]{1,0:T(1,128)S(1)} %get-tuple-element.33.refs_1_, ...), custom_call_target="tpu_custom_call" | custom-call | flops 1000000000 | bytes 4000000 | tf_op jit(solution)/shard_map/mode_tables/pallas_call | solution.py:176
  6.0 0.8 %collective-permute-done.refs_1_ = f32[272,1024]{1,0:T(8,128)S(1)} collective-permute-done((f32[272,1024]{1,0:T(8,128)S(1)}, f32[272,1024]{1,0:T(8,128)S(1)}, u32[]{:S(2)}, u32[]{:S(2)}) %collective-permute-start) | collective-permute-done | bytes 1114144 | tf_op jit(solution)/shard_map/ppermute | solution.py:507
  6.8 0.6 %slot_forces.1 = (f32[64,1024]{1,0:T(8,128)S(1)}, f32[64,768]{1,0:T(8,128)S(1)}, f32[64,1024]{1,0:T(8,128)S(1)}, f32[64,768]{1,0:T(8,128)S(1)}, f32[64,256]{1,0:...) custom-call(f32[272,1024]{1,0:T(8,128)S(1)} %get-tuple-element.31.re, ...), custom_call_target="tpu_custom_call" | custom-call | flops 500000000 | bytes 2000000 | tf_op jit(solution)/shard_map/slot_forces/pallas_call | solution.py:245
  7.4 3.0 %collective-permute-start.2 = (f32[64,768]{1,0:T(8,128)S(1)}, f32[64,768]{1,0:T(8,128)S(1)}, u32[]{:S(2)}, u32[]{:S(2)}) collective-permute-start(f32[64,768]{1,0:T(8,128)S(1)} %get-tuple-element.43.refs_3_), channel_id=1, source_target_pairs={{0,4},{4,0},{8,12},{12,8},{1,5},{5,1},{9,13},{13,9},{2,6},{6,2},{1... | collective-permute-start | bytes 589832 | tf_op jit(solution)/shard_map/ppermute | solution.py:559
  10.4 0.4 %end_states.1.ends_ref = f32[8,256]{1,0:T(8,128)S(1)} custom-call(f32[256,128]{1,0:T(8,128)S(1)} %get-tuple-element.47.re_ref, f32[256,128]{1,0:T(8,128)S(1)} %get-tuple-element.48.im_ref, f32[256,2]{1,0:T(8,128)S(1)} %get-tuple-element.39.refs_4_.refs_7_.turn_ref.after_ref.refs_11_, f32[256,2]{1,0:T(8,128)S(1)} %get-tuple-element.39.refs_4_.refs_7_.turn_ref.after_ref.refs_11_), custom_call_target="tpu_custom_call" | custom-call | flops 500000000 | bytes 2000000 | tf_op jit(solution)/shard_map/end_states/pallas_call | solution.py:270
  10.8 1.5 %collective-permute-start.1 = (f32[8,256]{1,0:T(8,128)S(1)}, f32[8,256]{1,0:T(8,128)S(1)}, u32[]{:S(2)}, u32[]{:S(2)}) collective-permute-start(f32[8,256]{1,0:T(8,128)S(1)} %end_states.1.ends_ref), channel_id=1, source_target_pairs={{0,2},{2,0},{1,3},{3,1},{4,6},{6,4},{5,7},{7,5},{8,10},{10,8},{9,1... | collective-permute-start | bytes 24584 | tf_op jit(solution)/shard_map/ppermute | solution.py:579
  12.4 2.6 %collective-permute-start.4 = (f32[64,256]{1,0:T(8,128)S(1)}, f32[64,256]{1,0:T(8,128)S(1)}, u32[]{:S(2)}, u32[]{:S(2)}) collective-permute-start(f32[64,256]{1,0:T(8,128)S(1)} %get-tuple-element.44.refs_4_), channel_id=1, source_target_pairs={{0,8},{4,12},{8,0},{12,4},{1,9},{5,13},{9,1},{13,5},{2,10},{6,14},... | collective-permute-start | bytes 196616 | tf_op jit(solution)/shard_map/ppermute | solution.py:561
  15.0 0.2 collective-permute-start.5
  15.2 1.5 %motion_from_rest.1.motion_ref = f32[16,1024]{1,0:T(8,128)S(1)} custom-call(f32[64,1024]{1,0:T(8,128)S(1)} %get-tuple-element.40.refs_0_, f32[64,768]{1,0:T(8,128)S(1)} %get-tuple-element.41.refs_1_.refs_0_, f32[64,1024]{1,0:T(8,128)S(1)} %get-tuple-element.42.refs_2_.refs_4_, f32[64,768]{1,0:T(8,128)S(1)} %get-tuple-element.43.refs_3_, ...), custom_call_target="tpu_custom_call" | custom-call | flops 1000000000 | bytes 4000000 | tf_op jit(solution)/shard_map/motion_from_rest/pallas_call | solution.py:321
  16.6 0.0 collective-permute-done.1.enter_ref.refs_3_
  16.7 0.0 collective-permute-done.2.refs_1_
  16.7 0.3 floor_shares.1
  17.0 0.1 collective-permute-start.3
  17.1 2.5 %collective-permute-start.8 = (f32[64,768]{1,0:T(8,128)S(1)}, f32[64,768]{1,0:T(8,128)S(1)}, u32[]{:S(2)}, u32[]{:S(2)}) collective-permute-start(f32[64,768]{1,0:T(8,128)S(1)} %get-tuple-element.54), channel_id=1, source_target_pairs={{0,8},{4,12},{8,0},{12,4},{1,9},{5,13},{9,1},{13,5},{2,10},{6,14},... | collective-permute-start | bytes 589832 | tf_op jit(solution)/shard_map/ppermute | solution.py:586
  19.5 0.7 %collective-permute-done.4.refs_5_ = f32[64,256]{1,0:T(8,128)S(1)} collective-permute-done((f32[64,256]{1,0:T(8,128)S(1)}, f32[64,256]{1,0:T(8,128)S(1)}, u32[]{:S(2)}, u32[]{:S(2)}) %collective-permute-start.4) | collective-permute-done | bytes 65568 | tf_op jit(solution)/shard_map/ppermute | solution.py:561
  20.3 0.8 %collective-permute-done.5.refs_6_ = f32[64,256]{1,0:T(8,128)S(1)} collective-permute-done((f32[64,256]{1,0:T(8,128)S(1)}, f32[64,256]{1,0:T(8,128)S(1)}, u32[]{:S(2)}, u32[]{:S(2)}) %collective-permute-start.5) | collective-permute-done | bytes 65568 | tf_op jit(solution)/shard_map/ppermute | solution.py:561
  21.1 0.0 collective-permute-done.3.refs_1_
  21.1 0.1 owner_shares.1
  21.2 1.7 %collective-permute-start.6 = (f32[80,512]{1,0:T(8,128)S(1)}, f32[80,512]{1,0:T(8,128)S(1)}, u32[]{:S(2)}, u32[]{:S(2)}) collective-permute-start(f32[80,512]{1,0:T(8,128)S(1)} %get-tuple-element.51), channel_id=1, source_target_pairs={{0,4},{4,0},{8,12},{12,8},{1,5},{5,1},{9,13},{13,9},{2,6},{6,2},{1... | collective-permute-start | bytes 491528 | tf_op jit(solution)/shard_map/ppermute | solution.py:585
  22.9 0.4 %collective-permute-start.7 = (f32[64,512]{1,0:T(8,128)S(1)}, f32[64,512]{1,0:T(8,128)S(1)}, u32[]{:S(2)}, u32[]{:S(2)}) collective-permute-start(f32[64,512]{1,0:T(8,128)S(1)} %get-tuple-element.52), channel_id=1, source_target_pairs={{0,4},{4,0},{8,12},{12,8},{1,5},{5,1},{9,13},{13,9},{2,6},{6,2},{1... | collective-permute-start | bytes 393224 | tf_op jit(solution)/shard_map/ppermute | solution.py:585
  23.3 1.6 %collective-permute-start.9 = (f32[8,640]{1,0:T(8,128)S(1)}, f32[8,640]{1,0:T(8,128)S(1)}, u32[]{:S(2)}, u32[]{:S(2)}) collective-permute-start(f32[8,640]{1,0:T(8,128)S(1)} %get-tuple-element.56), channel_id=1, source_target_pairs={{0,8},{4,12},{8,0},{12,4},{1,9},{5,13},{9,1},{13,5},{2,10},{6,14},... | collective-permute-start | bytes 61448 | tf_op jit(solution)/shard_map/ppermute | solution.py:585
  24.8 2.5 %collective-permute-start.10 = (f32[8,640]{1,0:T(8,128)S(1)}, f32[8,640]{1,0:T(8,128)S(1)}, u32[]{:S(2)}, u32[]{:S(2)}) collective-permute-start(f32[8,640]{1,0:T(8,128)S(1)} %get-tuple-element.57), channel_id=1, source_target_pairs={{0,12},{4,8},{8,4},{12,0},{1,13},{5,9},{9,5},{13,1},{2,14},{6,10},... | collective-permute-start | bytes 61448 | tf_op jit(solution)/shard_map/ppermute | solution.py:585
  27.3 4.1 %collective-permute-done.9.refs_6_ = f32[8,640]{1,0:T(8,128)S(1)} collective-permute-done((f32[8,640]{1,0:T(8,128)S(1)}, f32[8,640]{1,0:T(8,128)S(1)}, u32[]{:S(2)}, u32[]{:S(2)}) %collective-permute-start.9) | collective-permute-done | bytes 20512 | tf_op jit(solution)/shard_map/ppermute | solution.py:585
  31.3 2.6 %collective-permute-done.10.refs_7_ = f32[8,640]{1,0:T(8,128)S(1)} collective-permute-done((f32[8,640]{1,0:T(8,128)S(1)}, f32[8,640]{1,0:T(8,128)S(1)}, u32[]{:S(2)}, u32[]{:S(2)}) %collective-permute-start.10) | collective-permute-done | bytes 20512 | tf_op jit(solution)/shard_map/ppermute | solution.py:585
  33.9 0.0 collective-permute-done.7.refs_2_
  34.0 0.0 collective-permute-done.8.refs_4_
  34.0 0.0 collective-permute-done.6.refs_1_.refs_8_.refs_9_
  34.0 1.2 %own_response.1 = (f32[64,1024]{1,0:T(8,128)}, f32[2,1024]{1,0:T(2,128)}, f32[2,1024]{1,0:T(2,128)}) custom-call(f32[64,1024]{1,0:T(8,128)S(1)} %get-tuple-element.40.refs_0_, f32[80,512]{1,0:T(8,128)S(1)} %collective-permute-done.6.refs_1_.refs_8_.refs_9_, f32[64,512]{1,0:T(8,128)S(1)} %collective-permute-done.7.refs_2_, ...), custom_call_target="tpu_custom_call" | custom-call | flops 500000000 | bytes 2000000 | tf_op jit(solution)/shard_map/own_response/pallas_call | solution.py:490
Async XLA Ops:
  3.9 2.9 %collective-permute-start = (f32[272,1024]{1,0:T(8,128)S(1)}, f32[272,1024]{1,0:T(8,128)S(1)}, u32[]{:S(2)}, u32[]{:S(2)}) collective-permute-start(f32[272,1024]{1,0:T(8,128)S(1)} %get-tuple-element.31.refs_0_), channel_id=1, source_target_pairs={{0,1},{1,0},{2,3},{3,2},{4,5},{5,4},{6,7},{7,6},{8,9},{9,8},{10,11... | collective-permute-start | bytes 3342344 | tf_op jit(solution)/shard_map/ppermute | solution.py:507
  7.4 9.2 %collective-permute-start.2 = (f32[64,768]{1,0:T(8,128)S(1)}, f32[64,768]{1,0:T(8,128)S(1)}, u32[]{:S(2)}, u32[]{:S(2)}) collective-permute-start(f32[64,768]{1,0:T(8,128)S(1)} %get-tuple-element.43.refs_3_), channel_id=1, source_target_pairs={{0,4},{4,0},{8,12},{12,8},{1,5},{5,1},{9,13},{13,9},{2,6},{6,2},{1... | collective-permute-start | bytes 589832 | tf_op jit(solution)/shard_map/ppermute | solution.py:559
  10.8 5.8 %collective-permute-start.1 = (f32[8,256]{1,0:T(8,128)S(1)}, f32[8,256]{1,0:T(8,128)S(1)}, u32[]{:S(2)}, u32[]{:S(2)}) collective-permute-start(f32[8,256]{1,0:T(8,128)S(1)} %end_states.1.ends_ref), channel_id=1, source_target_pairs={{0,2},{2,0},{1,3},{3,1},{4,6},{6,4},{5,7},{7,5},{8,10},{10,8},{9,1... | collective-permute-start | bytes 24584 | tf_op jit(solution)/shard_map/ppermute | solution.py:579
  12.4 7.9 %collective-permute-start.4 = (f32[64,256]{1,0:T(8,128)S(1)}, f32[64,256]{1,0:T(8,128)S(1)}, u32[]{:S(2)}, u32[]{:S(2)}) collective-permute-start(f32[64,256]{1,0:T(8,128)S(1)} %get-tuple-element.44.refs_4_), channel_id=1, source_target_pairs={{0,8},{4,12},{8,0},{12,4},{1,9},{5,13},{9,1},{13,5},{2,10},{6,14},... | collective-permute-start | bytes 196616 | tf_op jit(solution)/shard_map/ppermute | solution.py:561
  15.0 6.1 %collective-permute-start.5 = (f32[64,256]{1,0:T(8,128)S(1)}, f32[64,256]{1,0:T(8,128)S(1)}, u32[]{:S(2)}, u32[]{:S(2)}) collective-permute-start(f32[64,256]{1,0:T(8,128)S(1)} %get-tuple-element.45.refs_5_), channel_id=1, source_target_pairs={{0,12},{4,8},{8,4},{12,0},{1,13},{5,9},{9,5},{13,1},{2,14},{6,10},... | collective-permute-start | bytes 196616 | tf_op jit(solution)/shard_map/ppermute | solution.py:561
  17.0 4.1 %collective-permute-start.3 = (f32[16,1024]{1,0:T(8,128)S(1)}, f32[16,1024]{1,0:T(8,128)S(1)}, u32[]{:S(2)}, u32[]{:S(2)}) collective-permute-start(f32[16,1024]{1,0:T(8,128)S(1)} %get-tuple-element.49.refs_0_), channel_id=1, source_target_pairs={{0,1},{1,0},{2,3},{3,2},{4,5},{5,4},{6,7},{7,6},{8,9},{9,8},{10,11... | collective-permute-start | bytes 196616 | tf_op jit(solution)/shard_map/ppermute | solution.py:507
  17.1 16.9 %collective-permute-start.8 = (f32[64,768]{1,0:T(8,128)S(1)}, f32[64,768]{1,0:T(8,128)S(1)}, u32[]{:S(2)}, u32[]{:S(2)}) collective-permute-start(f32[64,768]{1,0:T(8,128)S(1)} %get-tuple-element.54), channel_id=1, source_target_pairs={{0,8},{4,12},{8,0},{12,4},{1,9},{5,13},{9,1},{13,5},{2,10},{6,14},... | collective-permute-start | bytes 589832 | tf_op jit(solution)/shard_map/ppermute | solution.py:586
  21.2 12.8 %collective-permute-start.6 = (f32[80,512]{1,0:T(8,128)S(1)}, f32[80,512]{1,0:T(8,128)S(1)}, u32[]{:S(2)}, u32[]{:S(2)}) collective-permute-start(f32[80,512]{1,0:T(8,128)S(1)} %get-tuple-element.51), channel_id=1, source_target_pairs={{0,4},{4,0},{8,12},{12,8},{1,5},{5,1},{9,13},{13,9},{2,6},{6,2},{1... | collective-permute-start | bytes 491528 | tf_op jit(solution)/shard_map/ppermute | solution.py:585
  22.9 11.1 %collective-permute-start.7 = (f32[64,512]{1,0:T(8,128)S(1)}, f32[64,512]{1,0:T(8,128)S(1)}, u32[]{:S(2)}, u32[]{:S(2)}) collective-permute-start(f32[64,512]{1,0:T(8,128)S(1)} %get-tuple-element.52), channel_id=1, source_target_pairs={{0,4},{4,0},{8,12},{12,8},{1,5},{5,1},{9,13},{13,9},{2,6},{6,2},{1... | collective-permute-start | bytes 393224 | tf_op jit(solution)/shard_map/ppermute | solution.py:585
  23.3 8.1 %collective-permute-start.9 = (f32[8,640]{1,0:T(8,128)S(1)}, f32[8,640]{1,0:T(8,128)S(1)}, u32[]{:S(2)}, u32[]{:S(2)}) collective-permute-start(f32[8,640]{1,0:T(8,128)S(1)} %get-tuple-element.56), channel_id=1, source_target_pairs={{0,8},{4,12},{8,0},{12,4},{1,9},{5,13},{9,1},{13,5},{2,10},{6,14},... | collective-permute-start | bytes 61448 | tf_op jit(solution)/shard_map/ppermute | solution.py:585
  24.8 9.1 %collective-permute-start.10 = (f32[8,640]{1,0:T(8,128)S(1)}, f32[8,640]{1,0:T(8,128)S(1)}, u32[]{:S(2)}, u32[]{:S(2)}) collective-permute-start(f32[8,640]{1,0:T(8,128)S(1)} %get-tuple-element.57), channel_id=1, source_target_pairs={{0,12},{4,8},{8,4},{12,0},{1,13},{5,9},{9,5},{13,1},{2,14},{6,10},... | collective-permute-start | bytes 61448 | tf_op jit(solution)/shard_map/ppermute | solution.py:585

commit v8 on v7

--- a/solution.py
+++ b/solution.py
@@ -199,7 +199,8 @@
     until = direct_until(time)
     if nz != PAIRED or not until:
         return [(p, 0, time) for p in range(nz)]
-    return [(0, 0, time), (1, until, time), (2, 0, time), (3, until, time), (1, 0, until), (3, 0, until)]
+    late = [(p, until, time) for p in (1, 2, 3)]
+    return [(0, 0, time), *late, *((p, 0, until) for p in (1, 3, 2))]
 
 
 def slot_forces(sums, pt, tables, turns, nz, before):
@@ -381,17 +382,19 @@
     half = time // 2
     shapes = [(rows, cols)] * nz
     if n:
-        shapes[2] = (mode_dev + 2 * rows, half)
-        shapes += [(mode_dev, half), begin[0].shape]
+        width = direct[0].shape[1]
+        pieces = [(start, min(start + width, cols)) for start in range(0, cols, width)]
+        shapes[2] = (mode_dev + len(pieces) * rows, width)
+        shapes += [begin[0].shape]
 
     def body(*refs):
         motion_refs, load_refs, enter_ref = refs[:nc], refs[nc : nc + parts], refs[nc + parts]
         more, out_refs = refs[nc + parts + 1 : nc + parts + 1 + n + m], refs[nc + parts + 1 + n + m : -3]
         motion_all, load_all, share_ref = refs[-3:]
         if n:
-            out_refs[2][:mode_dev] = more[0][:, :half]
-            out_refs[nz][...] = more[0][:, half:]
-            out_refs[nz + 1][...] = more[1][...] + more[2][...]
+            out_refs[2][...] = jnp.zeros(shapes[2], F32)
+            out_refs[2][:mode_dev] = more[0][...]
+            out_refs[nz][...] = more[1][...] + more[2][...]
         z, c = lax.axis_index("taps"), lax.axis_index("floors")
         later = lax.axis_index("tm") > 0
         motion = motion_refs[0][...]
@@ -413,9 +416,9 @@
             state = enter_ref[0:2, p * mode_dev : (p + 1) * mode_dev]
             out[:2, half : half + mode_dev] = jnp.where(later, state, 0.0)
         if n:
-            out_refs[2][mode_dev : mode_dev + rows] = share_ref[:, :half]
-            out_refs[2][mode_dev + rows :, :TILE] = share_ref[:, half:]
-            out_refs[2][mode_dev + rows :, TILE:] = jnp.zeros((rows, half - TILE), F32)
+            for k, (start, stop) in enumerate(pieces):
+                at = mode_dev + k * rows
+                out_refs[2][at : at + rows, : stop - start] = share_ref[:, start:stop]
 
     return pl.pallas_call(
         body,
@@ -557,8 +560,8 @@
     laid = [(x, p * mode_dev, start) for x, (p, start, _) in zip(forces[0], send_plan(nz, time))]
     if nz == PAIRED:
         onward = [forces[0][1], lax.ppermute(forces[0][3], "taps", pair)]
-        direct = [forces[0][2]]
-        begin = [lax.ppermute(x, "taps", way) for x, way in zip(forces[0][4:], (two, mirror))]
+        direct, tail = [forces[0][6]], lax.ppermute(forces[0][2], "taps", pair)
+        begin = [lax.ppermute(x, "taps", way) for x, way in zip(forces[0][4:6], (two, mirror))]
     else:
         crossed, onward = [(x, 0, 0) for x in along(forces[0], nz)], []
         direct, begin = [], []
@@ -581,14 +584,15 @@
     motions = [motion] + shifts(motion, "floors", nc)
     shares = owner_shares(motions, loads, enter, direct, begin, nz, floor_dev)
     if nz == PAIRED:
-        ways = (two, pair, mirror, pair)
-        away, near, far, rest = (lax.ppermute(x, "taps", way) for x, way in zip(shares[1:5], ways))
+        ways = (two, pair, mirror)
+        away, near, far = (lax.ppermute(x, "taps", way) for x, way in zip(shares[1:4], ways))
         onward = lax.ppermute(onward[0], "taps", two)
-        half, (rows, cols) = time // 2, share_shape(floor_dev, time)
-        crossed = [(forces[0][0], 0, 0), (near, 0, 0), (rest, 0, half)]
-        crossed += [(shares[5], 0, 0), (onward, 0, until)]
+        rows, cols = share_shape(floor_dev, time)
+        crossed = [(forces[0][0], 0, 0), (near, 0, 0), (tail, 0, until)]
+        crossed += [(shares[4], 0, 0), (onward, 0, until)]
         shares = [(x, 0, 0, cols) for x in (shares[0], away, far)]
-        shares += [(near, mode_dev, 0, half), (near, mode_dev + rows, half, cols)]
+        for k, start in enumerate(range(0, cols, until)):
+            shares.append((near, mode_dev + k * rows, start, min(start + until, cols)))
     else:
         shares = [(x, 0, 0, x.shape[1]) for x in along(shares, nz)]
     return own_response(crossed, shares, own, turns, floor_dev, load_scale)

time: 35.4 us -> 35.2 us (level)
  waiting for transfers between devices: 9.03 us -> 8.28 us
  starting transfers between devices: 16.5 us -> 17.1 us
    ppermute x6 -> x5, waiting for transfers between devices: 8.22 us -> 4.51 us  [on_device(): lax.ppermute(x, 'taps', way)]
    ppermute x0 -> x1, waiting for transfers between devices: none -> 2.96 us  [on_device(): direct, tail = ([forces[0][6]], lax.ppermute(forces[0][2], 'taps', pair))]
    ppermute x6 -> x5, starting transfers between devices: 8.92 us -> 7.25 us  [on_device(): lax.ppermute(x, 'taps', way)]
    ppermute x1, starting transfers between devices: 2.49 us -> 3.78 us  [on_device(): onward = lax.ppermute(onward[0], 'taps', two)]
    ppermute x0 -> x1, starting transfers between devices: none -> 0.95 us  [on_device(): direct, tail = ([forces[0][6]], lax.ppermute(forces[0][2], 'taps', pair))]
  transfers between devices with their start and end apart: 11 -> 11, of which waited for: 5 -> 4; matrix products, arithmetic and copies ran while one was open for 0% -> 0% of each run, Pallas kernels for 11% -> 11%
where the time goes in v8:
time: 35.2 us; the launch traced here: 35 us
  starting transfers between devices  17.1 us (49%)
  Pallas kernels  8.95 us (25%)
  waiting for transfers between devices  8.28 us (24%)
  between operations  0.67 us (2%)
    ppermute x5, starting transfers between devices, on_device(): lax.ppermute(x, 'taps', way)  7.25 us
    ppermute x5, waiting for transfers between devices, on_device(): lax.ppermute(x, 'taps', way)  4.51 us
    ppermute x1, starting transfers between devices, on_device(): onward = lax.ppermute(onward[0], 'taps', two)  3.78 us
    pallas_call x1, Pallas kernels, tap_sums(): pl.pallas_call(body, in_specs=[pl.BlockSpec(memory_space=pltpu.HBM)] * (n...  3.29 us
    ppermute x1, starting transfers between devices, on_device(): onward = [forces[0][1], lax.ppermute(forces[0][3], 'taps', pair)]  3 us
    ppermute x1, waiting for transfers between devices, on_device(): direct, tail = ([forces[0][6]], lax.ppermute(forces[0][2], 'taps', pair))  2.96 us
    pallas_call x1, Pallas kernels, mode_tables(): pl.pallas_call(body, in_specs=whole(5), out_specs=tuple(whole(5)), out_sh...  1.58 us
    ppermute x1, starting transfers between devices, on_device(): enter = lax.ppermute(passed, 'tm', [(i, (i + 1) % nt) for i in range(nt)])  1.53 us
  transfers between devices with their start and end apart: 11, of which 4 were waited for; matrix products, arithmetic and copies ran while one was open for 0% of the time, Pallas kernels for 11%

profile of v8, /device:TPU:0, one launch (start us, length us, event | category | flops | bytes accessed | tf_op | source)
XLA Modules:
  0.0 35.0 jit_solution(2938554960382417983)
XLA Ops:
  0.6 3.3 %tap_sums.1 = (f32[272,1024]{1,0:T(8,128)S(1)}, s32[1,512]{1,0:T(1,128)S(1)}, f32[1,512]{1,0:T(1,128)S(1)}, f32[1,512]{1,0:T(1,128)S(1)}, bf16[256,512]{1,0:T(8,128)(2,1)S(1)}, /*index=5*/bf16[16,512]{1,0:T(8,128)(2,1)S(1)}) custom-call(bf16[1024,2048]{1,0:T(8,128)(2,1)} %press_hbm.1, s32[1,2048]{1,0:T(1,128)} %bitcast.5, s32[1,2048]{1,0:T(1,128)} %bitcast.6, ...), custom_call_target="tpu_custom_call" | custom-call | flops 1500000000 | bytes 6000000 | tf_op jit(solution)/shard_map/tap_sums/pallas_call | solution.py:89
  3.9 0.5 %collective-permute-start = (f32[272,1024]{1,0:T(8,128)S(1)}, f32[272,1024]{1,0:T(8,128)S(1)}, u32[]{:S(2)}, u32[]{:S(2)}) collective-permute-start(f32[272,1024]{1,0:T(8,128)S(1)} %get-tuple-element.31.refs_0_), channel_id=1, source_target_pairs={{0,1},{1,0},{2,3},{3,2},{4,5},{5,4},{6,7},{7,6},{8,9},{9,8},{10,11... | collective-permute-start | bytes 3342344 | tf_op jit(solution)/shard_map/ppermute | solution.py:510
  4.4 1.6 %mode_tables.1 = (bf16[256,256]{1,0:T(8,128)(2,1)S(1)}, f32[16,256]{1,0:T(8,128)S(1)}, f32[4,256,256]{2,1,0:T(8,128)S(1)}, f32[256,2]{1,0:T(8,128)S(1)}, f32[4,64,256]{2,1,0:T(8,128)S(1)}) custom-call(s32[1,512]{1,0:T(1,128)S(1)} %get-tuple-element.32.refs_0_, f32[1,512]{1,0:T(1,128)S(1)} %get-tuple-element.33.refs_1_, ...), custom_call_target="tpu_custom_call" | custom-call | flops 1000000000 | bytes 4000000 | tf_op jit(solution)/shard_map/mode_tables/pallas_call | solution.py:176
  6.0 0.8 %collective-permute-done.refs_1_ = f32[272,1024]{1,0:T(8,128)S(1)} collective-permute-done((f32[272,1024]{1,0:T(8,128)S(1)}, f32[272,1024]{1,0:T(8,128)S(1)}, u32[]{:S(2)}, u32[]{:S(2)}) %collective-permute-start) | collective-permute-done | bytes 1114144 | tf_op jit(solution)/shard_map/ppermute | solution.py:510
  6.8 0.6 %slot_forces.1 = (f32[64,1024]{1,0:T(8,128)S(1)}, f32[64,768]{1,0:T(8,128)S(1)}, f32[64,768]{1,0:T(8,128)S(1)}, f32[64,768]{1,0:T(8,128)S(1)}, f32[64,256]{1,0:T...) custom-call(f32[272,1024]{1,0:T(8,128)S(1)} %get-tuple-element.31.re, ...), custom_call_target="tpu_custom_call" | custom-call | flops 500000000 | bytes 2000000 | tf_op jit(solution)/shard_map/slot_forces/pallas_call | solution.py:246
  7.4 3.0 %collective-permute-start.2 = (f32[64,768]{1,0:T(8,128)S(1)}, f32[64,768]{1,0:T(8,128)S(1)}, u32[]{:S(2)}, u32[]{:S(2)}) collective-permute-start(f32[64,768]{1,0:T(8,128)S(1)} %get-tuple-element.43.refs_3_), channel_id=1, source_target_pairs={{0,4},{4,0},{8,12},{12,8},{1,5},{5,1},{9,13},{13,9},{2,6},{6,2},{1... | collective-permute-start | bytes 589832 | tf_op jit(solution)/shard_map/ppermute | solution.py:562
  10.4 0.4 %end_states.1.ends_ref = f32[8,256]{1,0:T(8,128)S(1)} custom-call(f32[256,128]{1,0:T(8,128)S(1)} %get-tuple-element.48.re_ref, f32[256,128]{1,0:T(8,128)S(1)} %get-tuple-element.49.im_ref, f32[256,2]{1,0:T(8,128)S(1)} %get-tuple-element.39.refs_4_.refs_8_.turn_ref.after_ref.refs_12_, f32[256,2]{1,0:T(8,128)S(1)} %get-tuple-element.39.refs_4_.refs_8_.turn_ref.after_ref.refs_12_), custom_call_target="tpu_custom_call" | custom-call | flops 500000000 | bytes 2000000 | tf_op jit(solution)/shard_map/end_states/pallas_call | solution.py:271
  10.8 1.5 %collective-permute-start.1 = (f32[8,256]{1,0:T(8,128)S(1)}, f32[8,256]{1,0:T(8,128)S(1)}, u32[]{:S(2)}, u32[]{:S(2)}) collective-permute-start(f32[8,256]{1,0:T(8,128)S(1)} %end_states.1.ends_ref), channel_id=1, source_target_pairs={{0,2},{2,0},{1,3},{3,1},{4,6},{6,4},{5,7},{7,5},{8,10},{10,8},{9,1... | collective-permute-start | bytes 24584 | tf_op jit(solution)/shard_map/ppermute | solution.py:582
  12.4 2.6 %collective-permute-start.4 = (f32[64,256]{1,0:T(8,128)S(1)}, f32[64,256]{1,0:T(8,128)S(1)}, u32[]{:S(2)}, u32[]{:S(2)}) collective-permute-start(f32[64,256]{1,0:T(8,128)S(1)} %get-tuple-element.44.refs_4_), channel_id=1, source_target_pairs={{0,8},{4,12},{8,0},{12,4},{1,9},{5,13},{9,1},{13,5},{2,10},{6,14},... | collective-permute-start | bytes 196616 | tf_op jit(solution)/shard_map/ppermute | solution.py:564
  15.0 0.2 collective-permute-start.5
  15.2 1.5 %motion_from_rest.1.motion_ref = f32[16,1024]{1,0:T(8,128)S(1)} custom-call(f32[64,1024]{1,0:T(8,128)S(1)} %get-tuple-element.40.refs_0_, f32[64,768]{1,0:T(8,128)S(1)} %get-tuple-element.41.refs_1_.refs_0_, f32[64,768]{1,0:T(8,128)S(1)} %get-tuple-element.42.refs_2_, f32[64,768]{1,0:T(8,128)S(1)} %get-tuple-element.43.refs_3_, ...), custom_call_target="tpu_custom_call" | custom-call | flops 1000000000 | bytes 4000000 | tf_op jit(solution)/shard_map/motion_from_rest/pallas_call | solution.py:322
  16.6 0.0 collective-permute-done.1.enter_ref.refs_3_
  16.6 0.0 collective-permute-done.2.refs_1_
  16.7 0.3 floor_shares.1
  17.0 0.1 collective-permute-start.3
  17.0 0.9 %collective-permute-start.7 = (f32[64,768]{1,0:T(8,128)S(1)}, f32[64,768]{1,0:T(8,128)S(1)}, u32[]{:S(2)}, u32[]{:S(2)}) collective-permute-start(f32[64,768]{1,0:T(8,128)S(1)} %get-tuple-element.42.refs_2_), channel_id=1, source_target_pairs={{0,4},{4,0},{8,12},{12,8},{1,5},{5,1},{9,13},{13,9},{2,6},{6,2},{1... | collective-permute-start | bytes 589832 | tf_op jit(solution)/shard_map/ppermute | solution.py:563
  18.0 3.8 %collective-permute-start.8 = (f32[64,768]{1,0:T(8,128)S(1)}, f32[64,768]{1,0:T(8,128)S(1)}, u32[]{:S(2)}, u32[]{:S(2)}) collective-permute-start(f32[64,768]{1,0:T(8,128)S(1)} %get-tuple-element.54), channel_id=1, source_target_pairs={{0,8},{4,12},{8,0},{12,4},{1,9},{5,13},{9,1},{13,5},{2,10},{6,14},... | collective-permute-start | bytes 589832 | tf_op jit(solution)/shard_map/ppermute | solution.py:589
  21.8 0.0 collective-permute-done.4.refs_5_
  21.8 0.0 collective-permute-done.5.refs_6_
  21.8 0.0 collective-permute-done.3.refs_1_
  21.8 0.1 owner_shares.1
  21.9 0.5 %collective-permute-start.6 = (f32[88,256]{1,0:T(8,128)S(1)}, f32[88,256]{1,0:T(8,128)S(1)}, u32[]{:S(2)}, u32[]{:S(2)}) collective-permute-start(f32[88,256]{1,0:T(8,128)S(1)} %get-tuple-element.52), channel_id=1, source_target_pairs={{0,4},{4,0},{8,12},{12,8},{1,5},{5,1},{9,13},{13,9},{2,6},{6,2},{1... | collective-permute-start | bytes 270344 | tf_op jit(solution)/shard_map/ppermute | solution.py:588
  22.4 1.2 %collective-permute-start.9 = (f32[8,640]{1,0:T(8,128)S(1)}, f32[8,640]{1,0:T(8,128)S(1)}, u32[]{:S(2)}, u32[]{:S(2)}) collective-permute-start(f32[8,640]{1,0:T(8,128)S(1)} %get-tuple-element.56), channel_id=1, source_target_pairs={{0,8},{4,12},{8,0},{12,4},{1,9},{5,13},{9,1},{13,5},{2,10},{6,14},... | collective-permute-start | bytes 61448 | tf_op jit(solution)/shard_map/ppermute | solution.py:588
  23.5 2.8 %collective-permute-start.10 = (f32[8,640]{1,0:T(8,128)S(1)}, f32[8,640]{1,0:T(8,128)S(1)}, u32[]{:S(2)}, u32[]{:S(2)}) collective-permute-start(f32[8,640]{1,0:T(8,128)S(1)} %get-tuple-element.57), channel_id=1, source_target_pairs={{0,12},{4,8},{8,4},{12,0},{1,13},{5,9},{9,5},{13,1},{2,14},{6,10},... | collective-permute-start | bytes 61448 | tf_op jit(solution)/shard_map/ppermute | solution.py:588
  26.3 3.0 %collective-permute-done.7.refs_2_ = f32[64,768]{1,0:T(8,128)S(1)} collective-permute-done((f32[64,768]{1,0:T(8,128)S(1)}, f32[64,768]{1,0:T(8,128)S(1)}, u32[]{:S(2)}, u32[]{:S(2)}) %collective-permute-start.7) | collective-permute-done | bytes 196640 | tf_op jit(solution)/shard_map/ppermute | solution.py:563
  29.3 2.7 %collective-permute-done.9.refs_6_ = f32[8,640]{1,0:T(8,128)S(1)} collective-permute-done((f32[8,640]{1,0:T(8,128)S(1)}, f32[8,640]{1,0:T(8,128)S(1)}, u32[]{:S(2)}, u32[]{:S(2)}) %collective-permute-start.9) | collective-permute-done | bytes 20512 | tf_op jit(solution)/shard_map/ppermute | solution.py:588
  31.9 1.8 %collective-permute-done.10.refs_7_ = f32[8,640]{1,0:T(8,128)S(1)} collective-permute-done((f32[8,640]{1,0:T(8,128)S(1)}, f32[8,640]{1,0:T(8,128)S(1)}, u32[]{:S(2)}, u32[]{:S(2)}) %collective-permute-start.10) | collective-permute-done | bytes 20512 | tf_op jit(solution)/shard_map/ppermute | solution.py:588
  33.8 0.0 collective-permute-done.6.refs_1_.refs_8_.refs_9_.refs_10_
  33.8 0.0 collective-permute-done.8.refs_4_
  33.8 1.2 %own_response.1 = (f32[64,1024]{1,0:T(8,128)}, f32[2,1024]{1,0:T(2,128)}, f32[2,1024]{1,0:T(2,128)}) custom-call(f32[64,1024]{1,0:T(8,128)S(1)} %get-tuple-element.40.refs_0_, f32[88,256]{1,0:T(8,128)S(1)} %collective-permute-done.6.refs_1_.refs_8_.refs_9_.refs_10_, f32[64,768]{1,0:T(8,128)S(1)} %collective-permute-done.7.refs_2_, ...), custom_call_target="tpu_custom_call" | custom-call | flops 500000000 | bytes 2000000 | tf_op jit(solution)/shard_map/own_response/pallas_call | solution.py:493
Async XLA Ops:
  3.9 2.9 %collective-permute-start = (f32[272,1024]{1,0:T(8,128)S(1)}, f32[272,1024]{1,0:T(8,128)S(1)}, u32[]{:S(2)}, u32[]{:S(2)}) collective-permute-start(f32[272,1024]{1,0:T(8,128)S(1)} %get-tuple-element.31.refs_0_), channel_id=1, source_target_pairs={{0,1},{1,0},{2,3},{3,2},{4,5},{5,4},{6,7},{7,6},{8,9},{9,8},{10,11... | collective-permute-start | bytes 3342344 | tf_op jit(solution)/shard_map/ppermute | solution.py:510
  7.4 9.2 %collective-permute-start.2 = (f32[64,768]{1,0:T(8,128)S(1)}, f32[64,768]{1,0:T(8,128)S(1)}, u32[]{:S(2)}, u32[]{:S(2)}) collective-permute-start(f32[64,768]{1,0:T(8,128)S(1)} %get-tuple-element.43.refs_3_), channel_id=1, source_target_pairs={{0,4},{4,0},{8,12},{12,8},{1,5},{5,1},{9,13},{13,9},{2,6},{6,2},{1... | collective-permute-start | bytes 589832 | tf_op jit(solution)/shard_map/ppermute | solution.py:562
  10.8 5.8 %collective-permute-start.1 = (f32[8,256]{1,0:T(8,128)S(1)}, f32[8,256]{1,0:T(8,128)S(1)}, u32[]{:S(2)}, u32[]{:S(2)}) collective-permute-start(f32[8,256]{1,0:T(8,128)S(1)} %end_states.1.ends_ref), channel_id=1, source_target_pairs={{0,2},{2,0},{1,3},{3,1},{4,6},{6,4},{5,7},{7,5},{8,10},{10,8},{9,1... | collective-permute-start | bytes 24584 | tf_op jit(solution)/shard_map/ppermute | solution.py:582
  12.4 9.4 %collective-permute-start.4 = (f32[64,256]{1,0:T(8,128)S(1)}, f32[64,256]{1,0:T(8,128)S(1)}, u32[]{:S(2)}, u32[]{:S(2)}) collective-permute-start(f32[64,256]{1,0:T(8,128)S(1)} %get-tuple-element.44.refs_4_), channel_id=1, source_target_pairs={{0,8},{4,12},{8,0},{12,4},{1,9},{5,13},{9,1},{13,5},{2,10},{6,14},... | collective-permute-start | bytes 196616 | tf_op jit(solution)/shard_map/ppermute | solution.py:564
  15.0 6.8 %collective-permute-start.5 = (f32[64,256]{1,0:T(8,128)S(1)}, f32[64,256]{1,0:T(8,128)S(1)}, u32[]{:S(2)}, u32[]{:S(2)}) collective-permute-start(f32[64,256]{1,0:T(8,128)S(1)} %get-tuple-element.45.refs_5_), channel_id=1, source_target_pairs={{0,12},{4,8},{8,4},{12,0},{1,13},{5,9},{9,5},{13,1},{2,14},{6,10},... | collective-permute-start | bytes 196616 | tf_op jit(solution)/shard_map/ppermute | solution.py:564
  17.0 4.8 %collective-permute-start.3 = (f32[16,1024]{1,0:T(8,128)S(1)}, f32[16,1024]{1,0:T(8,128)S(1)}, u32[]{:S(2)}, u32[]{:S(2)}) collective-permute-start(f32[16,1024]{1,0:T(8,128)S(1)} %get-tuple-element.50.refs_0_), channel_id=1, source_target_pairs={{0,1},{1,0},{2,3},{3,2},{4,5},{5,4},{6,7},{7,6},{8,9},{9,8},{10,11... | collective-permute-start | bytes 196616 | tf_op jit(solution)/shard_map/ppermute | solution.py:510
  17.0 12.2 %collective-permute-start.7 = (f32[64,768]{1,0:T(8,128)S(1)}, f32[64,768]{1,0:T(8,128)S(1)}, u32[]{:S(2)}, u32[]{:S(2)}) collective-permute-start(f32[64,768]{1,0:T(8,128)S(1)} %get-tuple-element.42.refs_2_), channel_id=1, source_target_pairs={{0,4},{4,0},{8,12},{12,8},{1,5},{5,1},{9,13},{13,9},{2,6},{6,2},{1... | collective-permute-start | bytes 589832 | tf_op jit(solution)/shard_map/ppermute | solution.py:563
  18.0 15.8 %collective-permute-start.8 = (f32[64,768]{1,0:T(8,128)S(1)}, f32[64,768]{1,0:T(8,128)S(1)}, u32[]{:S(2)}, u32[]{:S(2)}) collective-permute-start(f32[64,768]{1,0:T(8,128)S(1)} %get-tuple-element.54), channel_id=1, source_target_pairs={{0,8},{4,12},{8,0},{12,4},{1,9},{5,13},{9,1},{13,5},{2,10},{6,14},... | collective-permute-start | bytes 589832 | tf_op jit(solution)/shard_map/ppermute | solution.py:589
  21.9 11.9 %collective-permute-start.6 = (f32[88,256]{1,0:T(8,128)S(1)}, f32[88,256]{1,0:T(8,128)S(1)}, u32[]{:S(2)}, u32[]{:S(2)}) collective-permute-start(f32[88,256]{1,0:T(8,128)S(1)} %get-tuple-element.52), channel_id=1, source_target_pairs={{0,4},{4,0},{8,12},{12,8},{1,5},{5,1},{9,13},{13,9},{2,6},{6,2},{1... | collective-permute-start | bytes 270344 | tf_op jit(solution)/shard_map/ppermute | solution.py:588
  22.4 9.6 %collective-permute-start.9 = (f32[8,640]{1,0:T(8,128)S(1)}, f32[8,640]{1,0:T(8,128)S(1)}, u32[]{:S(2)}, u32[]{:S(2)}) collective-permute-start(f32[8,640]{1,0:T(8,128)S(1)} %get-tuple-element.56), channel_id=1, source_target_pairs={{0,8},{4,12},{8,0},{12,4},{1,9},{5,13},{9,1},{13,5},{2,10},{6,14},... | collective-permute-start | bytes 61448 | tf_op jit(solution)/shard_map/ppermute | solution.py:588
  23.5 10.2 %collective-permute-start.10 = (f32[8,640]{1,0:T(8,128)S(1)}, f32[8,640]{1,0:T(8,128)S(1)}, u32[]{:S(2)}, u32[]{:S(2)}) collective-permute-start(f32[8,640]{1,0:T(8,128)S(1)} %get-tuple-element.57), channel_id=1, source_target_pairs={{0,12},{4,8},{8,4},{12,0},{1,13},{5,9},{9,5},{13,1},{2,14},{6,10},... | collective-permute-start | bytes 61448 | tf_op jit(solution)/shard_map/ppermute | solution.py:588

commit v9 on v8

--- a/solution.py
+++ b/solution.py
@@ -566,7 +566,7 @@
         crossed, onward = [(x, 0, 0) for x in along(forces[0], nz)], []
         direct, begin = [], []
     motion = motion_from_rest(laid, tables, turns, floor_slots)
-    ends = end_states(spread, turns, turns)
+    ends = end_states(spread, turns, motion)
     enter = jnp.zeros_like(ends)
     for hop in range(nt - 1):
         passed = ends

time: 35.2 us -> 35.2 us (level)
  waiting for transfers between devices: 8.28 us -> 8.79 us
  starting transfers between devices: 17.1 us -> 16.6 us
    ppermute x5, waiting for transfers between devices: 4.51 us -> 5.3 us  [on_device(): lax.ppermute(x, 'taps', way)]
  transfers between devices with their start and end apart: 11 -> 11, of which waited for: 4 -> 5; matrix products, arithmetic and copies ran while one was open for 0% -> 0% of each run, Pallas kernels for 11% -> 11%
where the time goes in v9:
time: 35.2 us; the launch traced here: 35 us
  starting transfers between devices  16.6 us (47%)
  Pallas kernels  8.95 us (25%)
  waiting for transfers between devices  8.79 us (25%)
  between operations  0.68 us (2%)
    ppermute x5, starting transfers between devices, on_device(): lax.ppermute(x, 'taps', way)  7.25 us
    ppermute x5, waiting for transfers between devices, on_device(): lax.ppermute(x, 'taps', way)  5.3 us
    ppermute x1, starting transfers between devices, on_device(): onward = lax.ppermute(onward[0], 'taps', two)  3.45 us
    pallas_call x1, Pallas kernels, tap_sums(): pl.pallas_call(body, in_specs=[pl.BlockSpec(memory_space=pltpu.HBM)] * (n...  3.29 us
    ppermute x1, starting transfers between devices, on_device(): onward = [forces[0][1], lax.ppermute(forces[0][3], 'taps', pair)]  3 us
    ppermute x1, waiting for transfers between devices, on_device(): direct, tail = ([forces[0][6]], lax.ppermute(forces[0][2], 'taps', pair))  2.68 us
    pallas_call x1, Pallas kernels, mode_tables(): pl.pallas_call(body, in_specs=whole(5), out_specs=tuple(whole(5)), out_sh...  1.58 us
    ppermute x1, starting transfers between devices, on_device(): enter = lax.ppermute(passed, 'tm', [(i, (i + 1) % nt) for i in range(nt)])  1.53 us
  transfers between devices with their start and end apart: 11, of which 5 were waited for; matrix products, arithmetic and copies ran while one was open for 0% of the time, Pallas kernels for 11%

profile of v9, /device:TPU:0, one launch (start us, length us, event | category | flops | bytes accessed | tf_op | source)
XLA Modules:
  0.0 35.0 jit_solution(16201969661692598788)
XLA Ops:
  0.6 3.3 %tap_sums.1 = (f32[272,1024]{1,0:T(8,128)S(1)}, s32[1,512]{1,0:T(1,128)S(1)}, f32[1,512]{1,0:T(1,128)S(1)}, f32[1,512]{1,0:T(1,128)S(1)}, bf16[256,512]{1,0:T(8,128)(2,1)S(1)}, /*index=5*/bf16[16,512]{1,0:T(8,128)(2,1)S(1)}) custom-call(bf16[1024,2048]{1,0:T(8,128)(2,1)} %press_hbm.1, s32[1,2048]{1,0:T(1,128)} %bitcast.5, s32[1,2048]{1,0:T(1,128)} %bitcast.6, ...), custom_call_target="tpu_custom_call" | custom-call | flops 1500000000 | bytes 6000000 | tf_op jit(solution)/shard_map/tap_sums/pallas_call | solution.py:89
  3.9 0.5 %collective-permute-start = (f32[272,1024]{1,0:T(8,128)S(1)}, f32[272,1024]{1,0:T(8,128)S(1)}, u32[]{:S(2)}, u32[]{:S(2)}) collective-permute-start(f32[272,1024]{1,0:T(8,128)S(1)} %get-tuple-element.31.refs_0_), channel_id=1, source_target_pairs={{0,1},{1,0},{2,3},{3,2},{4,5},{5,4},{6,7},{7,6},{8,9},{9,8},{10,11... | collective-permute-start | bytes 3342344 | tf_op jit(solution)/shard_map/ppermute | solution.py:510
  4.4 1.6 %mode_tables.1 = (bf16[256,256]{1,0:T(8,128)(2,1)S(1)}, f32[16,256]{1,0:T(8,128)S(1)}, f32[4,256,256]{2,1,0:T(8,128)S(1)}, f32[256,2]{1,0:T(8,128)S(1)}, f32[4,64,256]{2,1,0:T(8,128)S(1)}) custom-call(s32[1,512]{1,0:T(1,128)S(1)} %get-tuple-element.32.refs_0_, f32[1,512]{1,0:T(1,128)S(1)} %get-tuple-element.33.refs_1_, ...), custom_call_target="tpu_custom_call" | custom-call | flops 1000000000 | bytes 4000000 | tf_op jit(solution)/shard_map/mode_tables/pallas_call | solution.py:176
  6.0 0.8 %collective-permute-done.refs_1_ = f32[272,1024]{1,0:T(8,128)S(1)} collective-permute-done((f32[272,1024]{1,0:T(8,128)S(1)}, f32[272,1024]{1,0:T(8,128)S(1)}, u32[]{:S(2)}, u32[]{:S(2)}) %collective-permute-start) | collective-permute-done | bytes 1114144 | tf_op jit(solution)/shard_map/ppermute | solution.py:510
  6.8 0.6 %slot_forces.1 = (f32[64,1024]{1,0:T(8,128)S(1)}, f32[64,768]{1,0:T(8,128)S(1)}, f32[64,768]{1,0:T(8,128)S(1)}, f32[64,768]{1,0:T(8,128)S(1)}, f32[64,256]{1,0:T...) custom-call(f32[272,1024]{1,0:T(8,128)S(1)} %get-tuple-element.31.re, ...), custom_call_target="tpu_custom_call" | custom-call | flops 500000000 | bytes 2000000 | tf_op jit(solution)/shard_map/slot_forces/pallas_call | solution.py:246
  7.4 3.0 %collective-permute-start.2 = (f32[64,768]{1,0:T(8,128)S(1)}, f32[64,768]{1,0:T(8,128)S(1)}, u32[]{:S(2)}, u32[]{:S(2)}) collective-permute-start(f32[64,768]{1,0:T(8,128)S(1)} %get-tuple-element.43.refs_3_), channel_id=1, source_target_pairs={{0,4},{4,0},{8,12},{12,8},{1,5},{5,1},{9,13},{13,9},{2,6},{6,2},{1... | collective-permute-start | bytes 589832 | tf_op jit(solution)/shard_map/ppermute | solution.py:562
  10.4 1.5 %motion_from_rest.1.after_ref.motion_ref = f32[16,1024]{1,0:T(8,128)S(1)} custom-call(f32[64,1024]{1,0:T(8,128)S(1)} %get-tuple-element.40.refs_0_, f32[64,768]{1,0:T(8,128)S(1)} %get-tuple-element.41.refs_1_.refs_0_, f32[64,768]{1,0:T(8,128)S(1)} %get-tuple-element.42.refs_2_, f32[64,768]{1,0:T(8,128)S(1)} %get-tuple-element.43.refs_3_, ...), custom_call_target="tpu_custom_call" | custom-call | flops 1000000000 | bytes 4000000 | tf_op jit(solution)/shard_map/motion_from_rest/pallas_call | solution.py:322
  11.9 0.4 %end_states.1.ends_ref = f32[8,256]{1,0:T(8,128)S(1)} custom-call(f32[256,128]{1,0:T(8,128)S(1)} %get-tuple-element.48.re_ref, f32[256,128]{1,0:T(8,128)S(1)} %get-tuple-element.49.im_ref, f32[256,2]{1,0:T(8,128)S(1)} %get-tuple-element.39.refs_4_.refs_8_.turn_ref.refs_12_, f32[16,1024]{1,0:T(8,128)S(1)} %motion_from_rest.1.after_ref.motion_ref), custom_call_target="tpu_custom_call" | custom-call | flops 500000000 | bytes 2000000 | tf_op jit(solution)/shard_map/end_states/pallas_call | solution.py:271
  12.3 1.5 %collective-permute-start.1 = (f32[8,256]{1,0:T(8,128)S(1)}, f32[8,256]{1,0:T(8,128)S(1)}, u32[]{:S(2)}, u32[]{:S(2)}) collective-permute-start(f32[8,256]{1,0:T(8,128)S(1)} %end_states.1.ends_ref), channel_id=1, source_target_pairs={{0,2},{2,0},{1,3},{3,1},{4,6},{6,4},{5,7},{7,5},{8,10},{10,8},{9,1... | collective-permute-start | bytes 24584 | tf_op jit(solution)/shard_map/ppermute | solution.py:582
  13.8 2.6 %collective-permute-start.4 = (f32[64,256]{1,0:T(8,128)S(1)}, f32[64,256]{1,0:T(8,128)S(1)}, u32[]{:S(2)}, u32[]{:S(2)}) collective-permute-start(f32[64,256]{1,0:T(8,128)S(1)} %get-tuple-element.44.refs_4_), channel_id=1, source_target_pairs={{0,8},{4,12},{8,0},{12,4},{1,9},{5,13},{9,1},{13,5},{2,10},{6,14},... | collective-permute-start | bytes 196616 | tf_op jit(solution)/shard_map/ppermute | solution.py:564
  16.4 0.2 collective-permute-start.5
  16.7 0.0 collective-permute-done.1.enter_ref.refs_3_
  16.7 0.0 collective-permute-done.2.refs_1_
  16.7 0.3 floor_shares.1
  17.0 0.1 collective-permute-start.3
  17.1 0.8 %collective-permute-start.7 = (f32[64,768]{1,0:T(8,128)S(1)}, f32[64,768]{1,0:T(8,128)S(1)}, u32[]{:S(2)}, u32[]{:S(2)}) collective-permute-start(f32[64,768]{1,0:T(8,128)S(1)} %get-tuple-element.42.refs_2_), channel_id=1, source_target_pairs={{0,4},{4,0},{8,12},{12,8},{1,5},{5,1},{9,13},{13,9},{2,6},{6,2},{1... | collective-permute-start | bytes 589832 | tf_op jit(solution)/shard_map/ppermute | solution.py:563
  17.8 3.5 %collective-permute-start.8 = (f32[64,768]{1,0:T(8,128)S(1)}, f32[64,768]{1,0:T(8,128)S(1)}, u32[]{:S(2)}, u32[]{:S(2)}) collective-permute-start(f32[64,768]{1,0:T(8,128)S(1)} %get-tuple-element.54), channel_id=1, source_target_pairs={{0,8},{4,12},{8,0},{12,4},{1,9},{5,13},{9,1},{13,5},{2,10},{6,14},... | collective-permute-start | bytes 589832 | tf_op jit(solution)/shard_map/ppermute | solution.py:589
  21.3 0.0 collective-permute-done.4.refs_5_
  21.3 1.8 %collective-permute-done.5.refs_6_ = f32[64,256]{1,0:T(8,128)S(1)} collective-permute-done((f32[64,256]{1,0:T(8,128)S(1)}, f32[64,256]{1,0:T(8,128)S(1)}, u32[]{:S(2)}, u32[]{:S(2)}) %collective-permute-start.5) | collective-permute-done | bytes 65568 | tf_op jit(solution)/shard_map/ppermute | solution.py:564
  23.0 0.0 collective-permute-done.3.refs_1_
  23.0 0.1 owner_shares.1
  23.1 0.1 collective-permute-start.6
  23.2 1.9 %collective-permute-start.9 = (f32[8,640]{1,0:T(8,128)S(1)}, f32[8,640]{1,0:T(8,128)S(1)}, u32[]{:S(2)}, u32[]{:S(2)}) collective-permute-start(f32[8,640]{1,0:T(8,128)S(1)} %get-tuple-element.56), channel_id=1, source_target_pairs={{0,8},{4,12},{8,0},{12,4},{1,9},{5,13},{9,1},{13,5},{2,10},{6,14},... | collective-permute-start | bytes 61448 | tf_op jit(solution)/shard_map/ppermute | solution.py:588
  25.1 2.4 %collective-permute-start.10 = (f32[8,640]{1,0:T(8,128)S(1)}, f32[8,640]{1,0:T(8,128)S(1)}, u32[]{:S(2)}, u32[]{:S(2)}) collective-permute-start(f32[8,640]{1,0:T(8,128)S(1)} %get-tuple-element.57), channel_id=1, source_target_pairs={{0,12},{4,8},{8,4},{12,0},{1,13},{5,9},{9,5},{13,1},{2,14},{6,10},... | collective-permute-start | bytes 61448 | tf_op jit(solution)/shard_map/ppermute | solution.py:588
  27.6 2.7 %collective-permute-done.7.refs_2_ = f32[64,768]{1,0:T(8,128)S(1)} collective-permute-done((f32[64,768]{1,0:T(8,128)S(1)}, f32[64,768]{1,0:T(8,128)S(1)}, u32[]{:S(2)}, u32[]{:S(2)}) %collective-permute-start.7) | collective-permute-done | bytes 196640 | tf_op jit(solution)/shard_map/ppermute | solution.py:563
  30.2 1.6 %collective-permute-done.9.refs_6_ = f32[8,640]{1,0:T(8,128)S(1)} collective-permute-done((f32[8,640]{1,0:T(8,128)S(1)}, f32[8,640]{1,0:T(8,128)S(1)}, u32[]{:S(2)}, u32[]{:S(2)}) %collective-permute-start.9) | collective-permute-done | bytes 20512 | tf_op jit(solution)/shard_map/ppermute | solution.py:588
  31.8 2.0 %collective-permute-done.10.refs_7_ = f32[8,640]{1,0:T(8,128)S(1)} collective-permute-done((f32[8,640]{1,0:T(8,128)S(1)}, f32[8,640]{1,0:T(8,128)S(1)}, u32[]{:S(2)}, u32[]{:S(2)}) %collective-permute-start.10) | collective-permute-done | bytes 20512 | tf_op jit(solution)/shard_map/ppermute | solution.py:588
  33.8 0.0 collective-permute-done.6.refs_1_.refs_8_.refs_9_.refs_10_
  33.8 0.0 collective-permute-done.8.refs_4_
  33.8 1.2 %own_response.1 = (f32[64,1024]{1,0:T(8,128)}, f32[2,1024]{1,0:T(2,128)}, f32[2,1024]{1,0:T(2,128)}) custom-call(f32[64,1024]{1,0:T(8,128)S(1)} %get-tuple-element.40.refs_0_, f32[88,256]{1,0:T(8,128)S(1)} %collective-permute-done.6.refs_1_.refs_8_.refs_9_.refs_10_, f32[64,768]{1,0:T(8,128)S(1)} %collective-permute-done.7.refs_2_, ...), custom_call_target="tpu_custom_call" | custom-call | flops 500000000 | bytes 2000000 | tf_op jit(solution)/shard_map/own_response/pallas_call | solution.py:493
Async XLA Ops:
  3.9 2.9 %collective-permute-start = (f32[272,1024]{1,0:T(8,128)S(1)}, f32[272,1024]{1,0:T(8,128)S(1)}, u32[]{:S(2)}, u32[]{:S(2)}) collective-permute-start(f32[272,1024]{1,0:T(8,128)S(1)} %get-tuple-element.31.refs_0_), channel_id=1, source_target_pairs={{0,1},{1,0},{2,3},{3,2},{4,5},{5,4},{6,7},{7,6},{8,9},{9,8},{10,11... | collective-permute-start | bytes 3342344 | tf_op jit(solution)/shard_map/ppermute | solution.py:510
  7.4 9.3 %collective-permute-start.2 = (f32[64,768]{1,0:T(8,128)S(1)}, f32[64,768]{1,0:T(8,128)S(1)}, u32[]{:S(2)}, u32[]{:S(2)}) collective-permute-start(f32[64,768]{1,0:T(8,128)S(1)} %get-tuple-element.43.refs_3_), channel_id=1, source_target_pairs={{0,4},{4,0},{8,12},{12,8},{1,5},{5,1},{9,13},{13,9},{2,6},{6,2},{1... | collective-permute-start | bytes 589832 | tf_op jit(solution)/shard_map/ppermute | solution.py:562
  12.3 4.4 %collective-permute-start.1 = (f32[8,256]{1,0:T(8,128)S(1)}, f32[8,256]{1,0:T(8,128)S(1)}, u32[]{:S(2)}, u32[]{:S(2)}) collective-permute-start(f32[8,256]{1,0:T(8,128)S(1)} %end_states.1.ends_ref), channel_id=1, source_target_pairs={{0,2},{2,0},{1,3},{3,1},{4,6},{6,4},{5,7},{7,5},{8,10},{10,8},{9,1... | collective-permute-start | bytes 24584 | tf_op jit(solution)/shard_map/ppermute | solution.py:582
  13.8 7.4 %collective-permute-start.4 = (f32[64,256]{1,0:T(8,128)S(1)}, f32[64,256]{1,0:T(8,128)S(1)}, u32[]{:S(2)}, u32[]{:S(2)}) collective-permute-start(f32[64,256]{1,0:T(8,128)S(1)} %get-tuple-element.44.refs_4_), channel_id=1, source_target_pairs={{0,8},{4,12},{8,0},{12,4},{1,9},{5,13},{9,1},{13,5},{2,10},{6,14},... | collective-permute-start | bytes 196616 | tf_op jit(solution)/shard_map/ppermute | solution.py:564
  16.4 6.6 %collective-permute-start.5 = (f32[64,256]{1,0:T(8,128)S(1)}, f32[64,256]{1,0:T(8,128)S(1)}, u32[]{:S(2)}, u32[]{:S(2)}) collective-permute-start(f32[64,256]{1,0:T(8,128)S(1)} %get-tuple-element.45.refs_5_), channel_id=1, source_target_pairs={{0,12},{4,8},{8,4},{12,0},{1,13},{5,9},{9,5},{13,1},{2,14},{6,10},... | collective-permute-start | bytes 196616 | tf_op jit(solution)/shard_map/ppermute | solution.py:564
  17.0 6.1 %collective-permute-start.3 = (f32[16,1024]{1,0:T(8,128)S(1)}, f32[16,1024]{1,0:T(8,128)S(1)}, u32[]{:S(2)}, u32[]{:S(2)}) collective-permute-start(f32[16,1024]{1,0:T(8,128)S(1)} %get-tuple-element.50.refs_0_), channel_id=1, source_target_pairs={{0,1},{1,0},{2,3},{3,2},{4,5},{5,4},{6,7},{7,6},{8,9},{9,8},{10,11... | collective-permute-start | bytes 196616 | tf_op jit(solution)/shard_map/ppermute | solution.py:510
  17.1 13.2 %collective-permute-start.7 = (f32[64,768]{1,0:T(8,128)S(1)}, f32[64,768]{1,0:T(8,128)S(1)}, u32[]{:S(2)}, u32[]{:S(2)}) collective-permute-start(f32[64,768]{1,0:T(8,128)S(1)} %get-tuple-element.42.refs_2_), channel_id=1, source_target_pairs={{0,4},{4,0},{8,12},{12,8},{1,5},{5,1},{9,13},{13,9},{2,6},{6,2},{1... | collective-permute-start | bytes 589832 | tf_op jit(solution)/shard_map/ppermute | solution.py:563
  17.8 16.0 %collective-permute-start.8 = (f32[64,768]{1,0:T(8,128)S(1)}, f32[64,768]{1,0:T(8,128)S(1)}, u32[]{:S(2)}, u32[]{:S(2)}) collective-permute-start(f32[64,768]{1,0:T(8,128)S(1)} %get-tuple-element.54), channel_id=1, source_target_pairs={{0,8},{4,12},{8,0},{12,4},{1,9},{5,13},{9,1},{13,5},{2,10},{6,14},... | collective-permute-start | bytes 589832 | tf_op jit(solution)/shard_map/ppermute | solution.py:589
  23.1 10.7 %collective-permute-start.6 = (f32[88,256]{1,0:T(8,128)S(1)}, f32[88,256]{1,0:T(8,128)S(1)}, u32[]{:S(2)}, u32[]{:S(2)}) collective-permute-start(f32[88,256]{1,0:T(8,128)S(1)} %get-tuple-element.52), channel_id=1, source_target_pairs={{0,4},{4,0},{8,12},{12,8},{1,5},{5,1},{9,13},{13,9},{2,6},{6,2},{1... | collective-permute-start | bytes 270344 | tf_op jit(solution)/shard_map/ppermute | solution.py:588
  23.2 8.6 %collective-permute-start.9 = (f32[8,640]{1,0:T(8,128)S(1)}, f32[8,640]{1,0:T(8,128)S(1)}, u32[]{:S(2)}, u32[]{:S(2)}) collective-permute-start(f32[8,640]{1,0:T(8,128)S(1)} %get-tuple-element.56), channel_id=1, source_target_pairs={{0,8},{4,12},{8,0},{12,4},{1,9},{5,13},{9,1},{13,5},{2,10},{6,14},... | collective-permute-start | bytes 61448 | tf_op jit(solution)/shard_map/ppermute | solution.py:588
  25.1 8.7 %collective-permute-start.10 = (f32[8,640]{1,0:T(8,128)S(1)}, f32[8,640]{1,0:T(8,128)S(1)}, u32[]{:S(2)}, u32[]{:S(2)}) collective-permute-start(f32[8,640]{1,0:T(8,128)S(1)} %get-tuple-element.57), channel_id=1, source_target_pairs={{0,12},{4,8},{8,4},{12,0},{1,13},{5,9},{9,5},{13,1},{2,14},{6,10},... | collective-permute-start | bytes 61448 | tf_op jit(solution)/shard_map/ppermute | solution.py:588

commit v10 on v9

--- a/solution.py
+++ b/solution.py
@@ -200,7 +200,7 @@
     if nz != PAIRED or not until:
         return [(p, 0, time) for p in range(nz)]
     late = [(p, until, time) for p in (1, 2, 3)]
-    return [(0, 0, time), *late, *((p, 0, until) for p in (1, 3, 2))]
+    return [(0, 0, time), *late, *((p, 0, until) for p in (3, 1, 2))]
 
 
 def slot_forces(sums, pt, tables, turns, nz, before):
@@ -561,7 +561,7 @@
     if nz == PAIRED:
         onward = [forces[0][1], lax.ppermute(forces[0][3], "taps", pair)]
         direct, tail = [forces[0][6]], lax.ppermute(forces[0][2], "taps", pair)
-        begin = [lax.ppermute(x, "taps", way) for x, way in zip(forces[0][4:6], (two, mirror))]
+        begin = [lax.ppermute(x, "taps", way) for x, way in zip(forces[0][4:6], (mirror, two))]
     else:
         crossed, onward = [(x, 0, 0) for x in along(forces[0], nz)], []
         direct, begin = [], []

time: 35.2 us -> 34.9 us (level)
  starting transfers between devices: 16.6 us -> 15.7 us
  waiting for transfers between devices: 8.79 us -> 9.34 us
    ppermute x1, starting transfers between devices: 3.45 us -> 1.73 us  [on_device(): onward = lax.ppermute(onward[0], 'taps', two)]
    ppermute x1, starting transfers between devices: 0.77 us -> 1.86 us  [on_device(): direct, tail = ([forces[0][6]], lax.ppermute(forces[0][2], 'taps', pair))]
    ppermute x5, waiting for transfers between devices: 5.3 us -> 6.24 us  [on_device(): lax.ppermute(x, 'taps', way)]
    ppermute x1, waiting for transfers between devices: 2.68 us -> 2.28 us  [on_device(): direct, tail = ([forces[0][6]], lax.ppermute(forces[0][2], 'taps', pair))]
  transfers between devices with their start and end apart: 11 -> 11, of which waited for: 5 -> 6; matrix products, arithmetic and copies ran while one was open for 0% -> 0% of each run, Pallas kernels for 11% -> 11%
where the time goes in v10:
time: 34.9 us; the launch traced here: 34.7 us
  starting transfers between devices  15.7 us (45%)
  waiting for transfers between devices  9.34 us (27%)
  Pallas kernels  8.95 us (26%)
  between operations  0.68 us (2%)
    ppermute x5, starting transfers between devices, on_device(): lax.ppermute(x, 'taps', way)  7.02 us
    ppermute x5, waiting for transfers between devices, on_device(): lax.ppermute(x, 'taps', way)  6.24 us
    pallas_call x1, Pallas kernels, tap_sums(): pl.pallas_call(body, in_specs=[pl.BlockSpec(memory_space=pltpu.HBM)] * (n...  3.29 us
    ppermute x1, starting transfers between devices, on_device(): onward = [forces[0][1], lax.ppermute(forces[0][3], 'taps', pair)]  3 us
    ppermute x1, waiting for transfers between devices, on_device(): direct, tail = ([forces[0][6]], lax.ppermute(forces[0][2], 'taps', pair))  2.28 us
    ppermute x1, starting transfers between devices, on_device(): direct, tail = ([forces[0][6]], lax.ppermute(forces[0][2], 'taps', pair))  1.86 us
    ppermute x1, starting transfers between devices, on_device(): onward = lax.ppermute(onward[0], 'taps', two)  1.73 us
    pallas_call x1, Pallas kernels, mode_tables(): pl.pallas_call(body, in_specs=whole(5), out_specs=tuple(whole(5)), out_sh...  1.58 us
  transfers between devices with their start and end apart: 11, of which 6 were waited for; matrix products, arithmetic and copies ran while one was open for 0% of the time, Pallas kernels for 11%

profile of v10, /device:TPU:0, one launch (start us, length us, event | category | flops | bytes accessed | tf_op | source)
XLA Modules:
  0.0 34.7 jit_solution(11481218410211129159)
XLA Ops:
  0.6 3.3 %tap_sums.1 = (f32[272,1024]{1,0:T(8,128)S(1)}, s32[1,512]{1,0:T(1,128)S(1)}, f32[1,512]{1,0:T(1,128)S(1)}, f32[1,512]{1,0:T(1,128)S(1)}, bf16[256,512]{1,0:T(8,128)(2,1)S(1)}, /*index=5*/bf16[16,512]{1,0:T(8,128)(2,1)S(1)}) custom-call(bf16[1024,2048]{1,0:T(8,128)(2,1)} %press_hbm.1, s32[1,2048]{1,0:T(1,128)} %bitcast.5, s32[1,2048]{1,0:T(1,128)} %bitcast.6, ...), custom_call_target="tpu_custom_call" | custom-call | flops 1500000000 | bytes 6000000 | tf_op jit(solution)/shard_map/tap_sums/pallas_call | solution.py:89
  3.9 0.5 %collective-permute-start = (f32[272,1024]{1,0:T(8,128)S(1)}, f32[272,1024]{1,0:T(8,128)S(1)}, u32[]{:S(2)}, u32[]{:S(2)}) collective-permute-start(f32[272,1024]{1,0:T(8,128)S(1)} %get-tuple-element.31.refs_0_), channel_id=1, source_target_pairs={{0,1},{1,0},{2,3},{3,2},{4,5},{5,4},{6,7},{7,6},{8,9},{9,8},{10,11... | collective-permute-start | bytes 3342344 | tf_op jit(solution)/shard_map/ppermute | solution.py:510
  4.4 1.6 %mode_tables.1 = (bf16[256,256]{1,0:T(8,128)(2,1)S(1)}, f32[16,256]{1,0:T(8,128)S(1)}, f32[4,256,256]{2,1,0:T(8,128)S(1)}, f32[256,2]{1,0:T(8,128)S(1)}, f32[4,64,256]{2,1,0:T(8,128)S(1)}) custom-call(s32[1,512]{1,0:T(1,128)S(1)} %get-tuple-element.32.refs_0_, f32[1,512]{1,0:T(1,128)S(1)} %get-tuple-element.33.refs_1_, ...), custom_call_target="tpu_custom_call" | custom-call | flops 1000000000 | bytes 4000000 | tf_op jit(solution)/shard_map/mode_tables/pallas_call | solution.py:176
  6.0 0.8 %collective-permute-done.refs_1_ = f32[272,1024]{1,0:T(8,128)S(1)} collective-permute-done((f32[272,1024]{1,0:T(8,128)S(1)}, f32[272,1024]{1,0:T(8,128)S(1)}, u32[]{:S(2)}, u32[]{:S(2)}) %collective-permute-start) | collective-permute-done | bytes 1114144 | tf_op jit(solution)/shard_map/ppermute | solution.py:510
  6.8 0.6 %slot_forces.1 = (f32[64,1024]{1,0:T(8,128)S(1)}, f32[64,768]{1,0:T(8,128)S(1)}, f32[64,768]{1,0:T(8,128)S(1)}, f32[64,768]{1,0:T(8,128)S(1)}, f32[64,256]{1,0:T...) custom-call(f32[272,1024]{1,0:T(8,128)S(1)} %get-tuple-element.31.re, ...), custom_call_target="tpu_custom_call" | custom-call | flops 500000000 | bytes 2000000 | tf_op jit(solution)/shard_map/slot_forces/pallas_call | solution.py:246
  7.4 3.0 %collective-permute-start.2 = (f32[64,768]{1,0:T(8,128)S(1)}, f32[64,768]{1,0:T(8,128)S(1)}, u32[]{:S(2)}, u32[]{:S(2)}) collective-permute-start(f32[64,768]{1,0:T(8,128)S(1)} %get-tuple-element.43.refs_3_), channel_id=1, source_target_pairs={{0,4},{4,0},{8,12},{12,8},{1,5},{5,1},{9,13},{13,9},{2,6},{6,2},{1... | collective-permute-start | bytes 589832 | tf_op jit(solution)/shard_map/ppermute | solution.py:562
  10.4 1.5 %motion_from_rest.1.after_ref.motion_ref = f32[16,1024]{1,0:T(8,128)S(1)} custom-call(f32[64,1024]{1,0:T(8,128)S(1)} %get-tuple-element.40.refs_0_, f32[64,768]{1,0:T(8,128)S(1)} %get-tuple-element.41.refs_1_.refs_0_, f32[64,768]{1,0:T(8,128)S(1)} %get-tuple-element.42.refs_2_, f32[64,768]{1,0:T(8,128)S(1)} %get-tuple-element.43.refs_3_, ...), custom_call_target="tpu_custom_call" | custom-call | flops 1000000000 | bytes 4000000 | tf_op jit(solution)/shard_map/motion_from_rest/pallas_call | solution.py:322
  11.9 0.4 %end_states.1.ends_ref = f32[8,256]{1,0:T(8,128)S(1)} custom-call(f32[256,128]{1,0:T(8,128)S(1)} %get-tuple-element.48.re_ref, f32[256,128]{1,0:T(8,128)S(1)} %get-tuple-element.49.im_ref, f32[256,2]{1,0:T(8,128)S(1)} %get-tuple-element.39.refs_4_.refs_8_.turn_ref.refs_12_, f32[16,1024]{1,0:T(8,128)S(1)} %motion_from_rest.1.after_ref.motion_ref), custom_call_target="tpu_custom_call" | custom-call | flops 500000000 | bytes 2000000 | tf_op jit(solution)/shard_map/end_states/pallas_call | solution.py:271
  12.3 1.5 %collective-permute-start.1 = (f32[8,256]{1,0:T(8,128)S(1)}, f32[8,256]{1,0:T(8,128)S(1)}, u32[]{:S(2)}, u32[]{:S(2)}) collective-permute-start(f32[8,256]{1,0:T(8,128)S(1)} %end_states.1.ends_ref), channel_id=1, source_target_pairs={{0,2},{2,0},{1,3},{3,1},{4,6},{6,4},{5,7},{7,5},{8,10},{10,8},{9,1... | collective-permute-start | bytes 24584 | tf_op jit(solution)/shard_map/ppermute | solution.py:582
  13.8 2.5 %collective-permute-start.4 = (f32[64,256]{1,0:T(8,128)S(1)}, f32[64,256]{1,0:T(8,128)S(1)}, u32[]{:S(2)}, u32[]{:S(2)}) collective-permute-start(f32[64,256]{1,0:T(8,128)S(1)} %get-tuple-element.44.refs_4_), channel_id=1, source_target_pairs={{0,12},{4,8},{8,4},{12,0},{1,13},{5,9},{9,5},{13,1},{2,14},{6,10},... | collective-permute-start | bytes 196616 | tf_op jit(solution)/shard_map/ppermute | solution.py:564
  16.3 0.1 collective-permute-start.5
  16.4 0.0 collective-permute-done.1.enter_ref.refs_3_
  16.4 0.0 collective-permute-done.2.refs_1_
  16.4 0.3 floor_shares.1
  16.7 0.1 collective-permute-start.3
  16.8 1.9 %collective-permute-start.7 = (f32[64,768]{1,0:T(8,128)S(1)}, f32[64,768]{1,0:T(8,128)S(1)}, u32[]{:S(2)}, u32[]{:S(2)}) collective-permute-start(f32[64,768]{1,0:T(8,128)S(1)} %get-tuple-element.42.refs_2_), channel_id=1, source_target_pairs={{0,4},{4,0},{8,12},{12,8},{1,5},{5,1},{9,13},{13,9},{2,6},{6,2},{1... | collective-permute-start | bytes 589832 | tf_op jit(solution)/shard_map/ppermute | solution.py:563
  18.7 1.7 %collective-permute-start.8 = (f32[64,768]{1,0:T(8,128)S(1)}, f32[64,768]{1,0:T(8,128)S(1)}, u32[]{:S(2)}, u32[]{:S(2)}) collective-permute-start(f32[64,768]{1,0:T(8,128)S(1)} %get-tuple-element.54), channel_id=1, source_target_pairs={{0,8},{4,12},{8,0},{12,4},{1,9},{5,13},{9,1},{13,5},{2,10},{6,14},... | collective-permute-start | bytes 589832 | tf_op jit(solution)/shard_map/ppermute | solution.py:589
  20.4 0.3 collective-permute-done.4.refs_5_
  20.7 2.3 %collective-permute-done.5.refs_6_ = f32[64,256]{1,0:T(8,128)S(1)} collective-permute-done((f32[64,256]{1,0:T(8,128)S(1)}, f32[64,256]{1,0:T(8,128)S(1)}, u32[]{:S(2)}, u32[]{:S(2)}) %collective-permute-start.5) | collective-permute-done | bytes 65568 | tf_op jit(solution)/shard_map/ppermute | solution.py:564
  23.0 0.0 collective-permute-done.3.refs_1_
  23.0 0.1 owner_shares.1
  23.1 0.1 collective-permute-start.6
  23.1 3.2 %collective-permute-start.9 = (f32[8,640]{1,0:T(8,128)S(1)}, f32[8,640]{1,0:T(8,128)S(1)}, u32[]{:S(2)}, u32[]{:S(2)}) collective-permute-start(f32[8,640]{1,0:T(8,128)S(1)} %get-tuple-element.56), channel_id=1, source_target_pairs={{0,8},{4,12},{8,0},{12,4},{1,9},{5,13},{9,1},{13,5},{2,10},{6,14},... | collective-permute-start | bytes 61448 | tf_op jit(solution)/shard_map/ppermute | solution.py:588
  26.3 1.2 %collective-permute-start.10 = (f32[8,640]{1,0:T(8,128)S(1)}, f32[8,640]{1,0:T(8,128)S(1)}, u32[]{:S(2)}, u32[]{:S(2)}) collective-permute-start(f32[8,640]{1,0:T(8,128)S(1)} %get-tuple-element.57), channel_id=1, source_target_pairs={{0,12},{4,8},{8,4},{12,0},{1,13},{5,9},{9,5},{13,1},{2,14},{6,10},... | collective-permute-start | bytes 61448 | tf_op jit(solution)/shard_map/ppermute | solution.py:588
  27.5 2.3 %collective-permute-done.7.refs_2_ = f32[64,768]{1,0:T(8,128)S(1)} collective-permute-done((f32[64,768]{1,0:T(8,128)S(1)}, f32[64,768]{1,0:T(8,128)S(1)}, u32[]{:S(2)}, u32[]{:S(2)}) %collective-permute-start.7) | collective-permute-done | bytes 196640 | tf_op jit(solution)/shard_map/ppermute | solution.py:563
  29.8 2.1 %collective-permute-done.9.refs_6_ = f32[8,640]{1,0:T(8,128)S(1)} collective-permute-done((f32[8,640]{1,0:T(8,128)S(1)}, f32[8,640]{1,0:T(8,128)S(1)}, u32[]{:S(2)}, u32[]{:S(2)}) %collective-permute-start.9) | collective-permute-done | bytes 20512 | tf_op jit(solution)/shard_map/ppermute | solution.py:588
  31.9 1.6 %collective-permute-done.10.refs_7_ = f32[8,640]{1,0:T(8,128)S(1)} collective-permute-done((f32[8,640]{1,0:T(8,128)S(1)}, f32[8,640]{1,0:T(8,128)S(1)}, u32[]{:S(2)}, u32[]{:S(2)}) %collective-permute-start.10) | collective-permute-done | bytes 20512 | tf_op jit(solution)/shard_map/ppermute | solution.py:588
  33.5 0.0 collective-permute-done.6.refs_1_.refs_8_.refs_9_.refs_10_
  33.5 0.0 collective-permute-done.8.refs_4_
  33.5 1.2 %own_response.1 = (f32[64,1024]{1,0:T(8,128)}, f32[2,1024]{1,0:T(2,128)}, f32[2,1024]{1,0:T(2,128)}) custom-call(f32[64,1024]{1,0:T(8,128)S(1)} %get-tuple-element.40.refs_0_, f32[88,256]{1,0:T(8,128)S(1)} %collective-permute-done.6.refs_1_.refs_8_.refs_9_.refs_10_, f32[64,768]{1,0:T(8,128)S(1)} %collective-permute-done.7.refs_2_, ...), custom_call_target="tpu_custom_call" | custom-call | flops 500000000 | bytes 2000000 | tf_op jit(solution)/shard_map/own_response/pallas_call | solution.py:493
Async XLA Ops:
  3.9 2.9 %collective-permute-start = (f32[272,1024]{1,0:T(8,128)S(1)}, f32[272,1024]{1,0:T(8,128)S(1)}, u32[]{:S(2)}, u32[]{:S(2)}) collective-permute-start(f32[272,1024]{1,0:T(8,128)S(1)} %get-tuple-element.31.refs_0_), channel_id=1, source_target_pairs={{0,1},{1,0},{2,3},{3,2},{4,5},{5,4},{6,7},{7,6},{8,9},{9,8},{10,11... | collective-permute-start | bytes 3342344 | tf_op jit(solution)/shard_map/ppermute | solution.py:510
  7.4 9.0 %collective-permute-start.2 = (f32[64,768]{1,0:T(8,128)S(1)}, f32[64,768]{1,0:T(8,128)S(1)}, u32[]{:S(2)}, u32[]{:S(2)}) collective-permute-start(f32[64,768]{1,0:T(8,128)S(1)} %get-tuple-element.43.refs_3_), channel_id=1, source_target_pairs={{0,4},{4,0},{8,12},{12,8},{1,5},{5,1},{9,13},{13,9},{2,6},{6,2},{1... | collective-permute-start | bytes 589832 | tf_op jit(solution)/shard_map/ppermute | solution.py:562
  12.3 4.1 %collective-permute-start.1 = (f32[8,256]{1,0:T(8,128)S(1)}, f32[8,256]{1,0:T(8,128)S(1)}, u32[]{:S(2)}, u32[]{:S(2)}) collective-permute-start(f32[8,256]{1,0:T(8,128)S(1)} %end_states.1.ends_ref), channel_id=1, source_target_pairs={{0,2},{2,0},{1,3},{3,1},{4,6},{6,4},{5,7},{7,5},{8,10},{10,8},{9,1... | collective-permute-start | bytes 24584 | tf_op jit(solution)/shard_map/ppermute | solution.py:582
  13.8 6.8 %collective-permute-start.4 = (f32[64,256]{1,0:T(8,128)S(1)}, f32[64,256]{1,0:T(8,128)S(1)}, u32[]{:S(2)}, u32[]{:S(2)}) collective-permute-start(f32[64,256]{1,0:T(8,128)S(1)} %get-tuple-element.44.refs_4_), channel_id=1, source_target_pairs={{0,12},{4,8},{8,4},{12,0},{1,13},{5,9},{9,5},{13,1},{2,14},{6,10},... | collective-permute-start | bytes 196616 | tf_op jit(solution)/shard_map/ppermute | solution.py:564
  16.3 6.7 %collective-permute-start.5 = (f32[64,256]{1,0:T(8,128)S(1)}, f32[64,256]{1,0:T(8,128)S(1)}, u32[]{:S(2)}, u32[]{:S(2)}) collective-permute-start(f32[64,256]{1,0:T(8,128)S(1)} %get-tuple-element.45.refs_5_), channel_id=1, source_target_pairs={{0,8},{4,12},{8,0},{12,4},{1,9},{5,13},{9,1},{13,5},{2,10},{6,14},... | collective-permute-start | bytes 196616 | tf_op jit(solution)/shard_map/ppermute | solution.py:564
  16.7 6.2 %collective-permute-start.3 = (f32[16,1024]{1,0:T(8,128)S(1)}, f32[16,1024]{1,0:T(8,128)S(1)}, u32[]{:S(2)}, u32[]{:S(2)}) collective-permute-start(f32[16,1024]{1,0:T(8,128)S(1)} %get-tuple-element.50.refs_0_), channel_id=1, source_target_pairs={{0,1},{1,0},{2,3},{3,2},{4,5},{5,4},{6,7},{7,6},{8,9},{9,8},{10,11... | collective-permute-start | bytes 196616 | tf_op jit(solution)/shard_map/ppermute | solution.py:510
  16.8 13.0 %collective-permute-start.7 = (f32[64,768]{1,0:T(8,128)S(1)}, f32[64,768]{1,0:T(8,128)S(1)}, u32[]{:S(2)}, u32[]{:S(2)}) collective-permute-start(f32[64,768]{1,0:T(8,128)S(1)} %get-tuple-element.42.refs_2_), channel_id=1, source_target_pairs={{0,4},{4,0},{8,12},{12,8},{1,5},{5,1},{9,13},{13,9},{2,6},{6,2},{1... | collective-permute-start | bytes 589832 | tf_op jit(solution)/shard_map/ppermute | solution.py:563
  18.7 14.8 %collective-permute-start.8 = (f32[64,768]{1,0:T(8,128)S(1)}, f32[64,768]{1,0:T(8,128)S(1)}, u32[]{:S(2)}, u32[]{:S(2)}) collective-permute-start(f32[64,768]{1,0:T(8,128)S(1)} %get-tuple-element.54), channel_id=1, source_target_pairs={{0,8},{4,12},{8,0},{12,4},{1,9},{5,13},{9,1},{13,5},{2,10},{6,14},... | collective-permute-start | bytes 589832 | tf_op jit(solution)/shard_map/ppermute | solution.py:589
  23.1 10.4 %collective-permute-start.6 = (f32[88,256]{1,0:T(8,128)S(1)}, f32[88,256]{1,0:T(8,128)S(1)}, u32[]{:S(2)}, u32[]{:S(2)}) collective-permute-start(f32[88,256]{1,0:T(8,128)S(1)} %get-tuple-element.52), channel_id=1, source_target_pairs={{0,4},{4,0},{8,12},{12,8},{1,5},{5,1},{9,13},{13,9},{2,6},{6,2},{1... | collective-permute-start | bytes 270344 | tf_op jit(solution)/shard_map/ppermute | solution.py:588
  23.1 8.8 %collective-permute-start.9 = (f32[8,640]{1,0:T(8,128)S(1)}, f32[8,640]{1,0:T(8,128)S(1)}, u32[]{:S(2)}, u32[]{:S(2)}) collective-permute-start(f32[8,640]{1,0:T(8,128)S(1)} %get-tuple-element.56), channel_id=1, source_target_pairs={{0,8},{4,12},{8,0},{12,4},{1,9},{5,13},{9,1},{13,5},{2,10},{6,14},... | collective-permute-start | bytes 61448 | tf_op jit(solution)/shard_map/ppermute | solution.py:588
  26.3 7.2 %collective-permute-start.10 = (f32[8,640]{1,0:T(8,128)S(1)}, f32[8,640]{1,0:T(8,128)S(1)}, u32[]{:S(2)}, u32[]{:S(2)}) collective-permute-start(f32[8,640]{1,0:T(8,128)S(1)} %get-tuple-element.57), channel_id=1, source_target_pairs={{0,12},{4,8},{8,4},{12,0},{1,13},{5,9},{9,5},{13,1},{2,14},{6,10},... | collective-permute-start | bytes 61448 | tf_op jit(solution)/shard_map/ppermute | solution.py:588
